TPU v7x, 128 devices: a whole 4x4x4 slice. The times are simulated.
128 devices in a mesh: dp: 16 (over y, x), tensor: 8 (over z, core).
Axes of the slice: x: 4, y: 4, z: 4, core: 2. Of those that a mesh axis runs over, the one named last changes fastest.
Arguments:
- tokens: bfloat16 [4096, 7168], P('dp', 'tensor'), may hold values from -6 to 6
- cotangent: bfloat16 [4096, 7168], P('dp', 'tensor'), may hold values from -4 to 4
- up_weight: bfloat16 [112, 1792, 128], P('tensor', 'dp'), may hold values from -0.125 to 0.125
- down_weight: bfloat16 [112, 1792, 128], P('tensor', 'dp'), may hold values from -0.09375 to 0.09375
- up_kept: int32 [112, 14], P('tensor'), may hold values from 0 to 55, as said below
- down_kept: int32 [112, 14], P('tensor'), may hold values from 0 to 55, as said below
Outputs:
- output: bfloat16 [4096, 7168], P('dp', 'tensor')
- input_grad: bfloat16 [4096, 7168], P('dp', 'tensor')
- up_grad: bfloat16 [112, 1792, 128], P('tensor', 'dp')
- down_grad: bfloat16 [112, 1792, 128], P('tensor', 'dp')
Inputs may be any that keep to these rules, and one draw needn't show every extreme that they name: `up_kept`: each row names 14 different feature blocks; every feature block is named by some row. `down_kept`: each row names 14 different feature blocks; every feature block is named by some row.
All inputs are finite; a program needn't handle non-finite values.
Results may differ from a plain program's by a relative error of at most 0.018.
Values may be sent and summed in bfloat16 or wider, within the bound.
No kernel may reach another device: no remote copies, remote signals or barrier semaphores. Data moves between devices by JAX's collectives and lax.ppermute only.
A program may use at most 192 MiB of HBM per device.

v0:
```python
import jax
import jax.numpy as jnp
from jax import lax
from jax.sharding import PartitionSpec as P

D = 7168
BLK = 128
KEEP = 14


def gelu_tanh(value):
    return jax.nn.gelu(value, approximate=True)


def place_blocks(terms, kept_index):
    block_count = D // BLK
    placed = jnp.zeros((terms.shape[0], block_count, BLK), jnp.float32)
    placed = placed.at[:, kept_index.reshape(-1)].add(terms)
    return placed.reshape(terms.shape[0], D)


def body(tokens, cotangent, up_weight, down_weight, up_kept, down_kept):
    tok_full, cot_full = (
        lax.all_gather(tokens, "tensor", axis=1, tiled=True),
        lax.all_gather(cotangent, "tensor", axis=1, tiled=True),
    )
    token_count = tok_full.shape[0]
    block_count = D // BLK
    local_count = up_kept.shape[0]
    tok_gathered = jnp.take(
        tok_full.reshape(token_count, block_count, BLK), up_kept.reshape(-1), axis=1
    )
    tok_gathered = tok_gathered.reshape(token_count, local_count, KEEP * BLK)
    up_full, down_full = (
        lax.all_gather(up_weight, "dp", axis=1, tiled=True),
        lax.all_gather(down_weight, "dp", axis=1, tiled=True),
    )
    pre_act = jnp.einsum("tfr,fre->tfe", tok_gathered, up_full, preferred_element_type=jnp.float32)
    hidden = gelu_tanh(pre_act).astype(jnp.bfloat16)
    down_four = down_full.reshape(local_count, KEEP, BLK, BLK)
    out_terms = jnp.einsum("tfe,fked->tfkd", hidden, down_four, preferred_element_type=jnp.float32)
    out_part = place_blocks(out_terms.reshape(token_count, local_count * KEEP, BLK), down_kept)
    output = lax.psum_scatter(
        out_part.astype(jnp.bfloat16), "tensor", scatter_dimension=1, tiled=True
    )
    cot_gathered = jnp.take(
        cot_full.reshape(token_count, block_count, BLK), down_kept.reshape(-1), axis=1
    )
    cot_gathered = cot_gathered.reshape(token_count, local_count, KEEP, BLK)
    grad_hidden = jnp.einsum(
        "tfkd,fked->tfe", cot_gathered, down_four, preferred_element_type=jnp.float32
    )
    unused, gelu_pull = jax.vjp(gelu_tanh, pre_act)
    grad_pre = gelu_pull(grad_hidden)[0].astype(jnp.bfloat16)
    down_term = jnp.einsum(
        "tfe,tfkd->fked", hidden, cot_gathered, preferred_element_type=jnp.float32
    )
    down_term = down_term.reshape(local_count, KEEP * BLK, BLK)
    up_term = jnp.einsum("tfr,tfe->fre", tok_gathered, grad_pre, preferred_element_type=jnp.float32)
    up_four = up_full.reshape(local_count, KEEP, BLK, BLK)
    input_terms = jnp.einsum(
        "tfe,fkce->tfkc", grad_pre, up_four, preferred_element_type=jnp.float32
    )
    input_part = place_blocks(input_terms.reshape(token_count, local_count * KEEP, BLK), up_kept)
    input_grad = lax.psum_scatter(
        input_part.astype(jnp.bfloat16), "tensor", scatter_dimension=1, tiled=True
    )
    up_sum, down_sum = (
        lax.psum_scatter(
            up_term.astype(jnp.bfloat16), "dp", scatter_dimension=1, tiled=True
        ).astype(jnp.float32),
        lax.psum_scatter(
            down_term.astype(jnp.bfloat16), "dp", scatter_dimension=1, tiled=True
        ).astype(jnp.float32),
    )
    return (output, input_grad, up_sum.astype(jnp.bfloat16), down_sum.astype(jnp.bfloat16))


def solution(mesh):
    placed = (
        P("dp", "tensor"),
        P("dp", "tensor"),
        P("tensor", "dp", None),
        P("tensor", "dp", None),
        P("tensor", None),
        P("tensor", None),
    )
    return jax.shard_map(
        body,
        mesh=mesh,
        in_specs=placed,
        out_specs=(
            P("dp", "tensor"),
            P("dp", "tensor"),
            P("tensor", "dp", None),
            P("tensor", "dp", None),
        ),
        check_vma=False,
    )
```

profile of v0, /device:TPU:0, one launch (start us, length us, event | category | flops | bytes accessed | tf_op | source)
XLA Modules:
  0.0 619.1 jit_solution(1313549827464518797)
XLA Ops:
  7.2 0.0 all-gather.5.cloned.1.call-start
  7.2 2.0 copy.20
  9.2 0.0 all-gather.5.cloned.1.call-update
  9.2 0.0 all-gather.11.cloned.1.call-start
  9.3 2.0 copy.25
  11.3 0.0 all-gather.7.cloned.1.call-start
  11.3 0.7 all-gather.7.cloned.1.call-update
  12.0 0.0 all-gather.9.cloned.1.call-start
  12.1 0.5 all-gather.9.cloned.1.call-update
  12.6 0.0 reduce-scatter.7.cloned.1.call-start
  12.7 0.8 reshape.113
  13.4 0.8 reshape.117
  14.2 0.8 reshape.119
  15.1 27.8 %all-gather.5.cloned.1.call-done = bf16[256,7168]{0,1:T(8,128)(2,1)} async-done(((bf16[256,896]{0,1:T(8,128)(2,1)}), bf16[256,7168]{0,1:T(8,128)(2,1)}) %all-gather.5.cloned.1.call-update) | async-done | bytes 3670032 | tf_op jit(solution)/shard_map/all_gather | solution.py:24
  42.9 5.9 copy.21
  48.8 10.6 %gather_fusion = bf16[196,256,128]{2,1,0:T(8,128)(2,1)} fusion(bf16[256,56,128]{2,0,1:T(8,128)(2,1)} %copy.21, s32[1024]{0:T(1024)S(1)} %pad_clamp_fusion.1), kind=kCustom, calls=%fused_computation.clone | custom fusion | bytes 25690896 | tf_op jit(solution)/shard_map/jit(_take)/gather | solution.py:30
  59.5 11.1 %select_bitcast_fusion = bf16[256,196,128]{2,0,1:T(8,128)(2,1)} fusion(bf16[196,256,128]{2,1,0:T(8,128)(2,1)} %gather_fusion, pred[196]{0:T(512)(128)(4,1)S(1)} %compare_and_fusion.1), kind=kLoop, calls=%fused_computation.4 | loop fusion | flops 6422528 | bytes 25690308 | tf_op jit(solution)/shard_map/jit(_take)/select_n | solution.py:30
  70.5 17.5 %copy.22 = bf16[256,196,128]{0,2,1:T(8,128)(2,1)} copy(bf16[256,196,128]{2,0,1:T(8,128)(2,1)} %select_bitcast_fusion) | data formatting | bytes 25690112 | tf_op jit(solution)/shard_map/jit(_take)/select_n | solution.py:30
  88.0 5.9 copy.26
  93.9 10.6 %gather_fusion.1 = bf16[196,256,128]{2,1,0:T(8,128)(2,1)} fusion(bf16[256,56,128]{2,0,1:T(8,128)(2,1)} %copy.26, s32[1024]{0:T(1024)S(1)} %pad_clamp_fusion), kind=kCustom, calls=%fused_computation.1.clone | custom fusion | bytes 25690896 | tf_op jit(solution)/shard_map/jit(_take)/gather | solution.py:46
  104.5 11.0 %broadcast_select_fusion = bf16[196,256,128]{2,1,0:T(8,128)(2,1)} fusion(bf16[196,256,128]{2,1,0:T(8,128)(2,1)} %gather_fusion.1, pred[196]{0:T(512)(128)(4,1)S(1)} %compare_and_fusion), kind=kLoop, calls=%fused_computation.5 | loop fusion | flops 6422528 | bytes 25690308 | tf_op jit(solution)/shard_map/jit(_take)/select_n | solution.py:46
  115.5 23.3 %all-gather.7.cloned.1.call-done = bf16[14,1792,128]{2,1,0:T(8,128)(2,1)} async-done(((bf16[14,112,128]{2,1,0:T(8,128)(2,1)}), bf16[14,1792,128]{2,1,0:T(8,128)(2,1)}) %all-gather.7.cloned.1.call-update) | async-done | bytes 6422544 | tf_op jit(solution)/shard_map/all_gather | solution.py:35
  138.8 8.6 %fusion.18 = f32[14,256,128]{2,1,0:T(8,128)S(1)} fusion(bf16[256,14,1792]{0,2,1:T(8,128)(2,1)} %bitcast.88, bf16[14,1792,128]{2,1,0:T(8,128)(2,1)} %all-gather.7.cloned.1.call-done), kind=kOutput, calls=%fused_computation.37 | convolution fusion | flops 1644167168 | bytes 21102592 | tf_op jit(solution)/shard_map/tfr,fre->tfe/dot_general | solution.py:38
  147.4 54.8 %all-gather.9.cloned.1.call-done = bf16[14,1792,128]{2,1,0:T(8,128)(2,1)} async-done(((bf16[14,112,128]{2,1,0:T(8,128)(2,1)}), bf16[14,1792,128]{2,1,0:T(8,128)(2,1)}) %all-gather.9.cloned.1.call-update) | async-done | bytes 6422544 | tf_op jit(solution)/shard_map/all_gather | solution.py:36
  202.3 10.1 %fusion.6 = bf16[256,14,128]{2,0,1:T(8,128)(2,1)S(1)} fusion(f32[14,256,128]{2,1,0:T(8,128)S(1)} %fusion.18, bf16[256,14,14,128]{3,0,2,1:T(8,128)(2,1)} %bitcast.90, bf16[14,14,128,128]{3,2,1,0:T(8,128)(2,1)} %bitcast.94), kind=kOutput, calls=%fused_computation.16 | convolution fusion | flops 1653342208 | bytes 22020096 | tf_op jit(solution)/shard_map/tfkd,fked->tfe/dot_general | solution.py:50
  212.3 13.1 %fusion.11 = f32[14,256,14,128]{3,1,2,0:T(8,128)} fusion(bf16[14,14,128,128]{3,2,1,0:T(8,128)(2,1)} %bitcast.92, bf16[256,14,128]{2,0,1:T(8,128)(2,1)S(1)} %fusion.6), kind=kOutput, calls=%fused_computation.24 | convolution fusion | flops 1644167168 | bytes 33030144 | tf_op jit(solution)/shard_map/tfe,fkce->tfkc/dot_general | solution.py:61
  225.4 3.8 broadcast.53.clone.1
  229.2 61.9 %scatter_fusion.1 = f32[256,56,128]{2,0,1:T(8,128)} fusion(f32[256,56,128]{2,0,1:T(8,128)} %broadcast.53.clone.1, s32[196]{0:T(256)S(1)} %bitcast.100, f32[196,256,128]{2,1,0:T(8,128)} %bitcast.86), kind=kCustom, calls=%fused_computation.3 | custom fusion | flops 6422528 | bytes 77071120 | tf_op jit(solution)/shard_map/scatter-add | solution.py:18
  291.1 5.5 convert_element_type.38
  296.6 6.0 copy.27
  302.6 0.0 reduce-scatter.5.cloned.1.call-start
  302.6 0.6 copy-done
  303.2 0.1 reshape.111
  303.3 13.5 %fusion.14 = f32[14,256,14,128]{3,1,2,0:T(8,128)} fusion(bf16[14,14,128,128]{3,2,1,0:T(8,128)(2,1)} %bitcast.95, f32[14,256,128]{2,1,0:T(8,128)S(1)} %fusion.18), kind=kOutput, calls=%fused_computation.27 | convolution fusion | flops 1648295936 | bytes 33947648 | tf_op jit(solution)/shard_map/tfe,fked->tfkd/dot_general | solution.py:41
  316.8 3.8 broadcast.53.clone
  320.6 62.0 %scatter_fusion = f32[256,56,128]{2,0,1:T(8,128)} fusion(f32[256,56,128]{2,0,1:T(8,128)} %broadcast.53.clone, s32[196]{0:T(256)S(1)} %bitcast.101, f32[196,256,128]{2,1,0:T(8,128)} %bitcast.87), kind=kCustom, calls=%fused_computation.2 | custom fusion | flops 6422528 | bytes 77071120 | tf_op jit(solution)/shard_map/scatter-add | solution.py:18
  382.6 5.4 convert_element_type.35
  388.1 5.9 copy.24
  394.0 0.0 reduce-scatter.9.cloned.1.call-start
  394.0 10.8 %convolution_convert_fusion.1 = bf16[14,1792,128]{2,1,0:T(8,128)(2,1)} fusion(bf16[256,14,1792]{0,2,1:T(8,128)(2,1)} %bitcast.89, bf16[256,14,128]{2,0,1:T(8,128)(2,1)S(1)} %fusion.6), kind=kOutput, calls=%fused_computation.7 | convolution fusion | flops 1647378432 | bytes 20185088 | tf_op jit(solution)/shard_map/tfr,tfe->fre/dot_general | solution.py:59
  404.9 0.0 reduce-scatter.11.cloned.1.call-start
  404.9 7.7 %convolution_convert_fusion = bf16[14,14,128,128]{2,3,1,0:T(8,128)(2,1)} fusion(bf16[256,14,14,128]{3,0,2,1:T(8,128)(2,1)} %bitcast.91, f32[14,256,128]{2,1,0:T(8,128)S(1)} %fusion.18), kind=kOutput, calls=%fused_computation.6 | convolution fusion | flops 1651507200 | bytes 21102592 | tf_op jit(solution)/shard_map/tfe,tfkd->fked/dot_general | solution.py:55
  412.6 0.0 reduce-scatter.7.cloned.1.call-done
  412.7 2.0 copy.30
  414.7 16.5 %reduce-scatter.5.cloned.1.call-done = bf16[256,896]{0,1:T(8,128)(2,1)} async-done(((bf16[256,7168]{0,1:T(8,128)(2,1)}), bf16[256,896]{0,1:T(8,128)(2,1)}) %reduce-scatter.5.cloned.1.call-update) | async-done | bytes 458768 | tf_op jit(solution)/shard_map/reduce_scatter | solution.py:43
  431.2 2.0 copy.29
  433.2 88.2 %reduce-scatter.9.cloned.1.call-done = bf16[14,112,128]{2,1,0:T(8,128)(2,1)} async-done(((bf16[14,1792,128]{2,1,0:T(8,128)(2,1)}), bf16[14,112,128]{2,1,0:T(8,128)(2,1)}) %reduce-scatter.9.cloned.1.call-update) | async-done | bytes 401424 | tf_op jit(solution)/shard_map/reduce_scatter | solution.py:69
  521.4 90.8 %reduce-scatter.11.cloned.1.call-done = bf16[14,112,128]{2,1,0:T(8,128)(2,1)} async-done(((bf16[14,1792,128]{2,1,0:T(8,128)(2,1)}), bf16[14,112,128]{2,1,0:T(8,128)(2,1)}) %reduce-scatter.11.cloned.1.call-update) | async-done | bytes 401424 | tf_op jit(solution)/shard_map/reduce_scatter | solution.py:72
  (15 shorter events, 0.1 us)
Async XLA Ops:
  7.2 35.8 %all-gather.5.cloned.1.call-start = ((), (), s32[]{:S(2)}) async-start(), calls=%async_computation.4 | async-start | bytes 4128768 | tf_op jit(solution)/shard_map/all_gather | solution.py:24
  9.2 78.8 %all-gather.11.cloned.1.call-start = ((), (), s32[]{:S(2)}) async-start(), calls=%async_computation.8 | async-start | bytes 4128768 | tf_op jit(solution)/shard_map/all_gather | solution.py:25
  11.3 127.5 %all-gather.7.cloned.1.call-start = ((), (), s32[]{:S(2)}) async-start(), calls=%async_computation.5 | async-start | bytes 6823936 | tf_op jit(solution)/shard_map/all_gather | solution.py:35
  12.0 190.2 %all-gather.9.cloned.1.call-start = ((), (), s32[]{:S(2)}) async-start(), calls=%async_computation.6 | async-start | bytes 6823936 | tf_op jit(solution)/shard_map/all_gather | solution.py:36
  12.6 400.1 %reduce-scatter.7.cloned.1.call-start = ((), (), s32[]{:S(2)}) async-start(), calls=%async_computation.9 | async-start | bytes 4128768 | tf_op jit(solution)/shard_map/reduce_scatter | solution.py:65
  302.5 0.7 copy-start
  302.6 128.7 %reduce-scatter.5.cloned.1.call-start = ((), (), s32[]{:S(2)}) async-start(), calls=%async_computation.7 | async-start | bytes 4128768 | tf_op jit(solution)/shard_map/reduce_scatter | solution.py:43
  394.0 127.5 %reduce-scatter.9.cloned.1.call-start = ((), (), s32[]{:S(2)}) async-start(), calls=%async_computation.10 | async-start | bytes 6823936 | tf_op jit(solution)/shard_map/reduce_scatter | solution.py:69
  404.9 207.4 %reduce-scatter.11.cloned.1.call-start = ((), (), s32[]{:S(2)}) async-start(), calls=%async_computation.11 | async-start | bytes 6823936 | tf_op jit(solution)/shard_map/reduce_scatter | solution.py:72
Sparse Core Ops, SparseCore 0:
  10.3 32.6 all-gather.4
  45.2 29.8 all-gather.10
  77.3 61.4 all-gather.6
  140.8 61.3 all-gather.8
  302.7 37.0 reduce-scatter.6
  394.1 37.0 reduce-scatter.4
  435.2 86.1 reduce-scatter.8
  525.5 86.7 reduce-scatter.10
where the time goes:
time: 621 us; the launch traced here: 619 us
  waiting for transfers between devices  303 us (49%)
  other arithmetic  157 us (25%)
  local copies, waits for them, and re-layouts  81 us (13%)
  matrix products  63.8 us (10%)
  between operations  14.2 us (2%)
    scatter-add x2, other arithmetic, place_blocks(): placed = placed.at[:, kept_index.reshape(-1)].add(terms)  124 us
    reduce_scatter x1, waiting for transfers between devices, body(): lax.psum_scatter(down_term.astype(jnp.bfloat16), 'dp', scatter_dimension=...  90.8 us
    reduce_scatter x1, waiting for transfers between devices, body(): lax.psum_scatter(up_term.astype(jnp.bfloat16), 'dp', scatter_dimension=1,...  88.2 us
    all_gather x1, waiting for transfers between devices, body(): lax.all_gather(down_weight, 'dp', axis=1, tiled=True)  54.8 us
    all_gather x1, waiting for transfers between devices, body(): lax.all_gather(tokens, 'tensor', axis=1, tiled=True)  27.8 us
    all_gather x1, waiting for transfers between devices, body(): lax.all_gather(up_weight, 'dp', axis=1, tiled=True)  23.3 us
    select_n x1, local copies, waits for them, and re-layouts, body(): jnp.take(tok_full.reshape(token_count, block_count, BLK), up_kept.reshape...  17.5 us
    reduce_scatter x1, waiting for transfers between devices, body(): lax.psum_scatter(out_part.astype(jnp.bfloat16), 'tensor', scatter_dimensi...  16.5 us
  transfers between devices with their start and end apart: 8, of which 6 were waited for; matrix products, arithmetic and copies ran while one was open for 32% of the time, Pallas kernels for 0%

commit v1 on v0

v1 whole, which is shorter than its diff:
```python
import functools

import jax
import jax.numpy as jnp
from jax import lax
from jax.experimental import pallas as pl
from jax.experimental.pallas import tpu as pltpu
from jax.sharding import PartitionSpec as P

D = 7168
BLK = 128
KEEP = 14
NFB = D // BLK
ROWS = KEEP * BLK
F32 = jnp.float32
BF16 = jnp.bfloat16
SIDE = 4
STEP = (0, -1, 1, 2)


def gelu_and_slope(v):
    c = 0.7978845608028654
    v2 = v * v
    th = jnp.tanh(c * (v + 0.044715 * v * v2))
    half = 0.5 * (1.0 + th)
    slope = half + 0.5 * v * (1.0 - th * th) * (c * (1.0 + 3 * 0.044715 * v2))
    return v * half, slope


def layer_kernel(
    has_prev, local, rows_tbl, upk, dnk, tok, cot,
    u0, um, up, u2a, u2b, d0, dm, dp, d2a, d2b, *rest
):
    if has_prev:
        prev_out, prev_in = rest[:2]
        rest = rest[2:]
    (out_ref, in_ref,
     tu0, tum, tup, tu2a, tu2b, td0, tdm, tdp, td2a, td2b,
     tokg, cotg, upw, dnw, dnr, uterm, dterm, out_acc, in_acc) = rest
    j = pl.program_id(0)

    @pl.when(j == 0)
    def _():
        out_acc[...] = jnp.zeros_like(out_acc)
        in_acc[...] = jnp.zeros_like(in_acc)

    part = u0.shape[2]

    def pieces(group):
        g0, gm, gp, g2a, g2b = group
        for g, ref in enumerate((g0, gm, gp)):
            for s in range(4):
                yield g * 4 + s, ref, s
        for s in range(4):
            yield 12 + s, (g2a if s < 2 else g2b), s % 2

    def at(which, i):
        return pl.ds(pl.multiple_of(rows_tbl[which, i], 16), part)

    for i, ref, s in pieces((u0, um, up, u2a, u2b)):
        upw[at(0, i), :] = ref[s, 0]
    for i, ref, s in pieces((d0, dm, dp, d2a, d2b)):
        dnr[at(1, i), :] = ref[s, 0]
    for k in range(KEEP):
        cols = slice(k * BLK, (k + 1) * BLK)
        tokg[:, cols] = tok[upk[j, k]]
        cotg[:, cols] = cot[dnk[j, k]]
        dnw[:, cols] = dnr[cols, :]

    pre = jnp.dot(tokg[...], upw[...], preferred_element_type=F32)
    nt = (((1,), (1,)), ((), ()))
    tn = (((0,), (0,)), ((), ()))
    grad_hidden = lax.dot_general(cotg[...], dnw[...], nt, preferred_element_type=F32)
    hid, slope = gelu_and_slope(pre)
    hidden = hid.astype(BF16)
    grad_pre = (grad_hidden * slope).astype(BF16)

    dt = lax.dot_general(hidden, cotg[...], tn, preferred_element_type=F32).astype(BF16)
    ut = lax.dot_general(tokg[...], grad_pre, tn, preferred_element_type=F32).astype(BF16)
    uterm[...] = ut
    for k in range(KEEP):
        cols = slice(k * BLK, (k + 1) * BLK)
        dterm[cols, :] = dt[:, cols]
    for k in range(KEEP):
        cols = slice(k * BLK, (k + 1) * BLK)
        out_acc[dnk[j, k]] += jnp.dot(hidden, dnw[:, cols], preferred_element_type=F32)
        in_acc[upk[j, k]] += lax.dot_general(
            grad_pre, upw[cols, :], nt, preferred_element_type=F32
        )
    for i, ref, s in pieces((tu0, tum, tup, tu2a, tu2b)):
        ref[s, 0] = uterm[at(0, i), :]
    for i, ref, s in pieces((td0, tdm, tdp, td2a, td2b)):
        ref[s, 0] = dterm[at(1, i), :]

    @pl.when(j == local - 1)
    def _():
        def put(f, carry):
            a, b = out_acc[f], in_acc[f]
            if has_prev:
                a = a + prev_out[f].astype(F32)
                b = b + prev_in[f].astype(F32)
            out_ref[f] = a.astype(BF16)
            in_ref[f] = b.astype(BF16)
            return carry

        lax.fori_loop(0, NFB, put, 0)


def layer_part(rows_tbl, upk, dnk, tok, cot, up_group, dn_group, prev):
    local, part = up_group[0].shape[1:3]
    tokens = tok.shape[1]
    whole = pl.BlockSpec((NFB, tokens, BLK), lambda j, *_: (0, 0, 0), pipeline_mode=pl.Buffered(1))

    def piece(n):
        return pl.BlockSpec((n, 1, part, BLK), lambda j, *_: (0, j, 0, 0))

    def shape(n):
        return jax.ShapeDtypeStruct((n, local, part, BLK), BF16)

    five = (4, 4, 4, 2, 2)
    sums = jax.ShapeDtypeStruct((NFB, tokens, BLK), BF16)
    outs = pl.pallas_call(
        functools.partial(layer_kernel, prev is not None, local),
        grid_spec=pltpu.PrefetchScalarGridSpec(
            num_scalar_prefetch=3,
            grid=(local,),
            in_specs=[whole, whole] + [piece(n) for n in five + five]
            + ([whole, whole] if prev is not None else []),
            out_specs=[whole, whole] + [piece(n) for n in five + five],
            scratch_shapes=[
                pltpu.VMEM((tokens, ROWS), BF16),
                pltpu.VMEM((tokens, ROWS), BF16),
                pltpu.VMEM((ROWS, BLK), BF16),
                pltpu.VMEM((BLK, ROWS), BF16),
                pltpu.VMEM((ROWS, BLK), BF16),
                pltpu.VMEM((ROWS, BLK), BF16),
                pltpu.VMEM((ROWS, BLK), BF16),
                pltpu.VMEM((NFB, tokens, BLK), F32),
                pltpu.VMEM((NFB, tokens, BLK), F32),
            ],
        ),
        out_shape=[sums, sums] + [shape(n) for n in five + five],
        compiler_params=pltpu.CompilerParams(vmem_limit_bytes=52 * 2**20),
        cost_estimate=pl.CostEstimate(
            flops=local * 12 * tokens * ROWS * BLK,
            bytes_accessed=4 * NFB * tokens * BLK * 2 + 8 * local * ROWS * BLK,
            transcendentals=local * tokens * BLK,
        ),
    )(rows_tbl, upk, dnk, tok, cot, *up_group, *dn_group, *(prev or ()))
    return outs[:2], outs[2:7], outs[7:]


def shift_perm(dx, dy):
    return [
        (y * SIDE + x, ((y + dy) % SIDE) * SIDE + (x + dx) % SIDE)
        for y in range(SIDE) for x in range(SIDE)
    ]


def shift(value, axis, by):
    return lax.ppermute(value, "dp", shift_perm(by, 0) if axis == 0 else shift_perm(0, by))


def gather_first(shard, axis):
    return jnp.stack(
        [shard, shift(shard, axis, 1), shift(shard, axis, -1), shift(shard, axis, 2)]
    )


def gather_second(group, axis):
    from_minus, from_plus = shift(group, axis, 1), shift(group, axis, -1)
    return (group, from_minus, from_plus,
            shift(from_minus[:2], axis, 1), shift(from_plus[2:], axis, -1))


def add(*terms):
    return sum(t.astype(F32) for t in terms).astype(BF16)


def reduce_first(terms, axis):
    own, to_minus, to_plus, far_a, far_b = terms
    got_a, got_b = shift(far_a, axis, 1), shift(far_b, axis, -1)
    send_plus = jnp.concatenate([add(to_plus[:2], got_a), to_plus[2:]])
    send_minus = jnp.concatenate([to_minus[:2], add(to_minus[2:], got_b)])
    return own, shift(send_plus, axis, 1), shift(send_minus, axis, -1)


def reduce_second(parts, axis):
    slot = [add(*(p[s] for p in parts)) for s in range(4)]
    return add(slot[0], shift(slot[1], axis, -1), shift(slot[2], axis, 1), shift(slot[3], axis, 2))


CHUNKS = 2


def body(tokens, cotangent, up_weight, down_weight, up_kept, down_kept):
    count, part = up_weight.shape[:2]
    per = count // CHUNKS
    rows = tokens.shape[0]

    def blocks(a):
        return a.reshape(rows, -1, BLK).transpose(1, 0, 2)

    tok = lax.all_gather(blocks(tokens), "tensor", axis=0, tiled=True)
    cot = lax.all_gather(blocks(cotangent), "tensor", axis=0, tiled=True)

    me = lax.axis_index("dp")
    y, x = me // SIDE, me % SIDE
    far = jnp.array(STEP, jnp.int32)
    ys, xs = (y + far) % SIDE, (x + far) % SIDE
    up_tbl = (ys[:, None] * SIDE + xs[None, :]).reshape(-1)
    dn_tbl = (ys[None, :] * SIDE + xs[:, None]).reshape(-1)
    rows_tbl = jnp.stack([up_tbl, dn_tbl]) * part

    groups = []
    for c in range(CHUNKS):
        own = slice(c * per, (c + 1) * per)
        u, d = gather_first(up_weight[own], 0), gather_first(down_weight[own], 1)
        groups.append((gather_second(u, 1), gather_second(d, 0)))
    sums, grads = None, []
    for c, (u, d) in enumerate(groups):
        own = slice(c * per, (c + 1) * per)
        sums, ut, dt = layer_part(rows_tbl, up_kept[own], down_kept[own], tok, cot, u, d, sums)
        grads.append((ut, dt))

    outs = [
        lax.psum_scatter(s, "tensor", scatter_dimension=0, tiled=True)
        .transpose(1, 0, 2).reshape(rows, -1)
        for s in sums
    ]
    ups, dns = [], []
    for ut, dt in grads:
        u, d = reduce_first(ut, 1), reduce_first(dt, 0)
        ups.append(reduce_second(u, 0))
        dns.append(reduce_second(d, 1))
    return outs[0], outs[1], jnp.concatenate(ups), jnp.concatenate(dns)


def solution(mesh):
    placed = (
        P("dp", "tensor"),
        P("dp", "tensor"),
        P("tensor", "dp", None),
        P("tensor", "dp", None),
        P("tensor", None),
        P("tensor", None),
    )
    return jax.shard_map(
        body,
        mesh=mesh,
        in_specs=placed,
        out_specs=placed[:4],
        check_vma=False,
    )
```

time: 621 us -> 289 us (0.47)
  waiting for transfers between devices: 303 us -> 108 us
  other arithmetic: 157 us -> 6.05 us
  starting transfers between devices: 0.32 us -> 79.1 us
  matrix products: 63.8 us -> 0 us
  local copies, waits for them, and re-layouts: 81 us -> 28 us
  Pallas kernels: 0 us -> 51.4 us
    reduce_scatter x4 -> x2, waiting for transfers between devices: 196 us -> 0.01 us  [body(): lax.psum_scatter(s, 'tensor', scatter_dimension=0, tiled=True)]
    scatter-add x2 -> x0, other arithmetic: 124 us -> none  [place_blocks(): placed = placed.at[:, kept_index.reshape(-1)].add(terms)]
    ppermute x0 -> x56, waiting for transfers between devices: none -> 107 us  [shift(): lax.ppermute(value, 'dp', shift_perm(by, 0) if axis == 0 else shift_perm(...]
    all_gather x4 -> x2, waiting for transfers between devices: 106 us -> 0.01 us  [the longest x1 0.01 us: body(): tok = lax.all_gather(blocks(tokens), 'tensor', axis=0, tiled=True)]
    ppermute x0 -> x56, starting transfers between devices: none -> 78.9 us  [shift(): lax.ppermute(value, 'dp', shift_perm(by, 0) if axis == 0 else shift_perm(...]
    dot_general x6 -> x0, matrix products: 63.8 us -> none  [the longest x1 13.5 us: body(): jnp.einsum('tfe,fked->tfkd', hidden, down_four, preferred_element_type=jn...]
    pallas_call x0 -> x2, Pallas kernels: none -> 51.4 us  [layer_part(): pl.pallas_call(functools.partial(layer_kernel, prev is not None, local),...]
    select_n x6 -> x0, other arithmetic: 22.1 us -> none  [the longest x2 11.1 us: body(): jnp.take(tok_full.reshape(token_count, block_count, BLK), up_kept.reshape...]
  transfers between devices with their start and end apart: 8 -> 60, of which waited for: 6 -> 26; matrix products, arithmetic and copies ran while one was open for 32% -> 10% of each run, Pallas kernels for 0% -> 8%
where the time goes in v1:
time: 289 us; the launch traced here: 287 us
  waiting for transfers between devices  108 us (37%)
  starting transfers between devices  79.1 us (27%)
  Pallas kernels  51.4 us (18%)
  local copies, waits for them, and re-layouts  28 us (10%)
  between operations  14.5 us (5%)
  other arithmetic  6.05 us (2%)
    ppermute x56, waiting for transfers between devices, shift(): lax.ppermute(value, 'dp', shift_perm(by, 0) if axis == 0 else shift_perm(...  107 us
    ppermute x56, starting transfers between devices, shift(): lax.ppermute(value, 'dp', shift_perm(by, 0) if axis == 0 else shift_perm(...  78.9 us
    pallas_call x2, Pallas kernels, layer_part(): pl.pallas_call(functools.partial(layer_kernel, prev is not None, local),...  51.4 us
    slice x4, local copies, waits for them, and re-layouts, gather_second(): from_plus[2:]  7.15 us
  transfers between devices with their start and end apart: 60, of which 26 were waited for; matrix products, arithmetic and copies ran while one was open for 10% of the time, Pallas kernels for 8%

profile of v1, /device:TPU:0, one launch (start us, length us, event | category | flops | bytes accessed | tf_op | source)
XLA Modules:
  0.0 287.0 jit_solution(7159934790636352573)
XLA Ops:
  13.6 1.7 collective-permute-start.15
  15.3 1.9 collective-permute-start.16
  17.3 1.6 collective-permute-start.21
  19.9 1.7 collective-permute-done.15
  21.5 3.8 %collective-permute-done.16 = bf16[7,112,128]{2,1,0:T(8,128)(2,1)S(1)} collective-permute-done((bf16[7,112,128]{2,1,0:T(8,128)(2,1)S(1)}, bf16[7,112,128]{2,1,0:T(8,128)(2,1)S(1)}, u32[]{:S(2)}, u32[]{:S(2)}) %collective-permute-start.16) | collective-permute-done | bytes 200736 | tf_op jit(solution)/shard_map/ppermute | solution.py:161
  25.5 1.6 collective-permute-start.17
  27.1 1.7 collective-permute-start.18
  28.8 1.8 collective-permute-start.22
  31.2 2.3 collective-permute-start.8
  33.5 22.6 %collective-permute-done.22 = bf16[7,112,128]{2,1,0:T(8,128)(2,1)S(1)} collective-permute-done((bf16[7,112,128]{2,1,0:T(8,128)(2,1)S(1)}, bf16[7,112,128]{2,1,0:T(8,128)(2,1)S(1)}, u32[]{:S(2)}, u32[]{:S(2)}) %collective-permute-start.22) | collective-permute-done | bytes 200736 | tf_op jit(solution)/shard_map/ppermute | solution.py:161
  56.4 4.3 %collective-permute-start.7 = (bf16[7,112,128]{2,1,0:T(8,128)(2,1)S(1)}, bf16[7,112,128]{2,1,0:T(8,128)(2,1)S(1)}, u32[]{:S(2)}, u32[]{:S(2)}) collective-permute-start(bf16[7,112,128]{2,1,0:T(8,128)(2,1)S(1)} %get-tuple-element.75), channel_id=1, source_target_pairs={{0,32},{8,40},{16,48},{24,56},{32,64},{40,72},{48,80},{56,88},{64,... | collective-permute-start | bytes 602120 | tf_op jit(solution)/shard_map/ppermute | solution.py:161
  63.4 1.9 collective-permute-start.1
  67.5 1.7 collective-permute-done
  71.2 2.0 collective-permute-start.25
  73.2 1.7 collective-permute-done.2
  76.1 2.3 collective-permute-start.11
  78.4 1.8 collective-permute-start.3
  80.2 11.6 %collective-permute-done.24.dm = bf16[4,7,112,128]{3,2,1,0:T(8,128)(2,1)S(1)} collective-permute-done((bf16[4,7,112,128]{3,2,1,0:T(8,128)(2,1)}, bf16[4,7,112,128]{3,2,1,0:T(8,128)(2,1)S(1)}, u32[]{:S(2)}, u32[]{:S(2)}) %collective-permute-start.24) | collective-permute-done | bytes 802848 | tf_op jit(solution)/shard_map/ppermute | solution.py:161
  91.8 3.9 %collective-permute-start.4 = (bf16[4,7,112,128]{3,2,1,0:T(8,128)(2,1)S(1)}, bf16[4,7,112,128]{3,2,1,0:T(8,128)(2,1)}, u32[]{:S(2)}, u32[]{:S(2)}) collective-permute-start(bf16[4,7,112,128]{3,2,1,0:T(8,128)(2,1)S(1)} %pad_maximum_fusion.u0), channel_id=1, source_target_pairs={{0,96},{8,104},{16,112},{24,120},{32,0},{40,8},{48,16},{56,24},{64... | collective-permute-start | bytes 2408456 | tf_op jit(solution)/shard_map/ppermute | solution.py:161
  95.8 1.8 slice.324
  97.5 1.8 slice.325
  100.5 1.8 slice.327
  102.2 2.0 collective-permute-done.10.dm
  104.2 4.5 %collective-permute-start.20 = (bf16[2,7,112,128]{3,2,1,0:T(8,128)(2,1)}, bf16[2,7,112,128]{3,2,1,0:T(8,128)(2,1)}, u32[]{:S(2)}, u32[]{:S(2)}) collective-permute-start(bf16[2,7,112,128]{3,2,1,0:T(8,128)(2,1)} %slice.325), channel_id=1, source_target_pairs={{0,96},{8,104},{16,112},{24,120},{32,0},{40,8},{48,16},{56,24},{64... | collective-permute-start | bytes 1204232 | tf_op jit(solution)/shard_map/ppermute | solution.py:161
  109.2 2.8 collective-permute-start.27
  113.1 1.8 slice.323
  114.9 1.8 slice.320
  116.6 1.8 slice.321
  118.4 3.2 %collective-permute-start.13 = (bf16[2,7,112,128]{3,2,1,0:T(8,128)(2,1)}, bf16[2,7,112,128]{3,2,1,0:T(8,128)(2,1)}, u32[]{:S(2)}, u32[]{:S(2)}) collective-permute-start(bf16[2,7,112,128]{3,2,1,0:T(8,128)(2,1)} %slice.323), channel_id=1, source_target_pairs={{0,24},{8,0},{16,8},{24,16},{32,56},{40,32},{48,40},{56,48},{64,88... | collective-permute-start | bytes 1204232 | tf_op jit(solution)/shard_map/ppermute | solution.py:161
  121.7 3.2 %collective-permute-start.6 = (bf16[2,7,112,128]{3,2,1,0:T(8,128)(2,1)}, bf16[2,7,112,128]{3,2,1,0:T(8,128)(2,1)}, u32[]{:S(2)}, u32[]{:S(2)}) collective-permute-start(bf16[2,7,112,128]{3,2,1,0:T(8,128)(2,1)} %slice.321), channel_id=1, source_target_pairs={{0,96},{8,104},{16,112},{24,120},{32,0},{40,8},{48,16},{56,24},{64... | collective-permute-start | bytes 1204232 | tf_op jit(solution)/shard_map/ppermute | solution.py:161
  124.9 24.4 %shard_map.102 = (bf16[56,256,128]{2,1,0:T(8,128)(2,1)}, bf16[56,256,128]{2,1,0:T(8,128)(2,1)}, bf16[4,7,112,128]{3,2,1,0:T(8,128)(2,1)}, bf16[4,7,112,128]{3,2,...) custom-call(s32[2,16]{1,0:T(2,128)S(1)} %add_multiply_fusion.rows_tb, ...), custom_call_target="tpu_custom_call" | custom-call | flops 4932501504 | bytes 27525120 | tf_op jit(solution)/shard_map/pallas_call | solution.py:122
  149.3 27.0 %shard_map.103 = (bf16[56,256,128]{2,1,0:T(8,128)(2,1)}, bf16[56,256,128]{2,1,0:T(8,128)(2,1)}, bf16[4,7,112,128]{3,2,1,0:T(8,128)(2,1)}, bf16[4,7,112,128]{3,2,...) custom-call(s32[2,16]{1,0:T(2,128)S(1)} %add_multiply_fusion.rows_tb, ...), custom_call_target="tpu_custom_call" | custom-call | flops 4932501504 | bytes 27525120 | tf_op jit(solution)/shard_map/pallas_call | solution.py:122
  177.8 3.2 %collective-permute-start.44 = (bf16[2,7,112,128]{3,2,1,0:T(8,128)(2,1)S(1)}, bf16[2,7,112,128]{3,2,1,0:T(8,128)(2,1)S(1)}, u32[]{:S(2)}, u32[]{:S(2)}) collective-permute-start(bf16[2,7,112,128]{3,2,1,0:T(8,128)(2,1)S(1)} %get-tuple-element.46), channel_id=1, source_target_pairs={{0,24},{8,0},{16,8},{24,16},{32,56},{40,32},{48,40},{56,48},{64,88... | collective-permute-start | bytes 1204232 | tf_op jit(solution)/shard_map/ppermute | solution.py:161
  184.3 3.3 %collective-permute-start.51 = (bf16[2,7,112,128]{3,2,1,0:T(8,128)(2,1)S(1)}, bf16[2,7,112,128]{3,2,1,0:T(8,128)(2,1)S(1)}, u32[]{:S(2)}, u32[]{:S(2)}) collective-permute-start(bf16[2,7,112,128]{3,2,1,0:T(8,128)(2,1)S(1)} %get-tuple-element.51), channel_id=1, source_target_pairs={{0,24},{8,0},{16,8},{24,16},{32,56},{40,32},{48,40},{56,48},{64,88... | collective-permute-start | bytes 1204232 | tf_op jit(solution)/shard_map/ppermute | solution.py:161
  190.0 3.2 %collective-permute-start.30 = (bf16[2,7,112,128]{3,2,1,0:T(8,128)(2,1)S(1)}, bf16[2,7,112,128]{3,2,1,0:T(8,128)(2,1)S(1)}, u32[]{:S(2)}, u32[]{:S(2)}) collective-permute-start(bf16[2,7,112,128]{3,2,1,0:T(8,128)(2,1)S(1)} %get-tuple-element.36), channel_id=1, source_target_pairs={{0,96},{8,104},{16,112},{24,120},{32,0},{40,8},{48,16},{56,24},{64... | collective-permute-start | bytes 1204232 | tf_op jit(solution)/shard_map/ppermute | solution.py:161
  193.8 3.1 %collective-permute-start.37 = (bf16[2,7,112,128]{3,2,1,0:T(8,128)(2,1)S(1)}, bf16[2,7,112,128]{3,2,1,0:T(8,128)(2,1)S(1)}, u32[]{:S(2)}, u32[]{:S(2)}) collective-permute-start(bf16[2,7,112,128]{3,2,1,0:T(8,128)(2,1)S(1)} %get-tuple-element.41), channel_id=1, source_target_pairs={{0,96},{8,104},{16,112},{24,120},{32,0},{40,8},{48,16},{56,24},{64... | collective-permute-start | bytes 1204232 | tf_op jit(solution)/shard_map/ppermute | solution.py:161
  198.4 2.3 collective-permute-start.45
  201.5 3.8 %collective-permute-done.35 = bf16[2,7,112,128]{3,2,1,0:T(8,128)(2,1)S(1)} collective-permute-done((bf16[2,7,112,128]{3,2,1,0:T(8,128)(2,1)S(1)}, bf16[2,7,112,128]{3,2,1,0:T(8,128)(2,1)S(1)}, u32[]{:S(2)}, u32[]{:S(2)}) %collective-permute-start.35) | collective-permute-done | bytes 401440 | tf_op jit(solution)/shard_map/ppermute | solution.py:161
  205.8 13.4 %collective-permute-done.43 = bf16[4,7,112,128]{3,2,1,0:T(8,128)(2,1)S(1)} collective-permute-done((bf16[4,7,112,128]{3,2,1,0:T(8,128)(2,1)S(1)}, bf16[4,7,112,128]{3,2,1,0:T(8,128)(2,1)S(1)}, u32[]{:S(2)}, u32[]{:S(2)}) %collective-permute-start.43) | collective-permute-done | bytes 802848 | tf_op jit(solution)/shard_map/ppermute | solution.py:161
  219.3 2.1 collective-permute-start.36
  221.4 6.5 %collective-permute-done.50 = bf16[4,7,112,128]{3,2,1,0:T(8,128)(2,1)S(1)} collective-permute-done((bf16[4,7,112,128]{3,2,1,0:T(8,128)(2,1)S(1)}, bf16[4,7,112,128]{3,2,1,0:T(8,128)(2,1)S(1)}, u32[]{:S(2)}, u32[]{:S(2)}) %collective-permute-start.50) | collective-permute-done | bytes 802848 | tf_op jit(solution)/shard_map/ppermute | solution.py:161
  229.1 2.0 collective-permute-start.46
  231.5 8.4 %collective-permute-done.31 = bf16[4,7,112,128]{3,2,1,0:T(8,128)(2,1)S(1)} collective-permute-done((bf16[4,7,112,128]{3,2,1,0:T(8,128)(2,1)S(1)}, bf16[4,7,112,128]{3,2,1,0:T(8,128)(2,1)S(1)}, u32[]{:S(2)}, u32[]{:S(2)}) %collective-permute-start.31) | collective-permute-done | bytes 802848 | tf_op jit(solution)/shard_map/ppermute | solution.py:161
  242.4 14.2 %collective-permute-done.38 = bf16[4,7,112,128]{3,2,1,0:T(8,128)(2,1)S(1)} collective-permute-done((bf16[4,7,112,128]{3,2,1,0:T(8,128)(2,1)S(1)}, bf16[4,7,112,128]{3,2,1,0:T(8,128)(2,1)S(1)}, u32[]{:S(2)}, u32[]{:S(2)}) %collective-permute-start.38) | collective-permute-done | bytes 802848 | tf_op jit(solution)/shard_map/ppermute | solution.py:161
  256.9 1.9 collective-permute-done.46
  259.7 2.0 collective-permute-start.33
  267.0 2.7 collective-permute-start.41
  270.6 4.5 %collective-permute-done.40 = bf16[7,112,128]{2,1,0:T(8,128)(2,1)S(1)} collective-permute-done((bf16[7,112,128]{2,1,0:T(8,128)(2,1)S(1)}, bf16[7,112,128]{2,1,0:T(8,128)(2,1)S(1)}, u32[]{:S(2)}, u32[]{:S(2)}) %collective-permute-start.40) | collective-permute-done | bytes 200736 | tf_op jit(solution)/shard_map/ppermute | solution.py:161
  (192 shorter events, 46.2 us)
Async XLA Ops:
  7.2 117.7 %all-gather.3.cloned.1.call-start = ((), (), s32[]{:S(2)}) async-start(), calls=%async_computation.2 | async-start | bytes 4128768 | tf_op jit(solution)/shard_map/all_gather | solution.py:204
  9.5 115.4 %all-gather.5.cloned.1.call-start = ((), (), s32[]{:S(2)}) async-start(), calls=%async_computation.3 | async-start | bytes 4128768 | tf_op jit(solution)/shard_map/all_gather | solution.py:205
  11.8 264.2 %reduce-scatter.3.cloned.1.call-start = ((), (), s32[]{:S(2)}) async-start(), calls=%async_computation.4 | async-start | bytes 4128768 | tf_op jit(solution)/shard_map/reduce_scatter | solution.py:227
  15.3 10.1 %collective-permute-start.16 = (bf16[7,112,128]{2,1,0:T(8,128)(2,1)S(1)}, bf16[7,112,128]{2,1,0:T(8,128)(2,1)S(1)}, u32[]{:S(2)}, u32[]{:S(2)}) collective-permute-start(bf16[7,112,128]{2,1,0:T(8,128)(2,1)S(1)} %get-tuple-element.78), channel_id=1, source_target_pairs={{0,16},{8,24},{16,0},{24,8},{32,48},{40,56},{48,32},{56,40},{64,80... | collective-permute-start | bytes 602120 | tf_op jit(solution)/shard_map/ppermute | solution.py:161
  17.3 13.9 %collective-permute-start.21 = (bf16[7,112,128]{2,1,0:T(8,128)(2,1)S(1)}, bf16[7,112,128]{2,1,0:T(8,128)(2,1)S(1)}, u32[]{:S(2)}, u32[]{:S(2)}) collective-permute-start(bf16[7,112,128]{2,1,0:T(8,128)(2,1)S(1)} %get-tuple-element.74), channel_id=1, source_target_pairs={{0,32},{8,40},{16,48},{24,56},{32,64},{40,72},{48,80},{56,88},{64,... | collective-permute-start | bytes 602120 | tf_op jit(solution)/shard_map/ppermute | solution.py:161
  25.5 50.6 %collective-permute-start.17 = (bf16[4,7,112,128]{3,2,1,0:T(8,128)(2,1)S(1)}, bf16[4,7,112,128]{3,2,1,0:T(8,128)(2,1)S(1)}, u32[]{:S(2)}, u32[]{:S(2)}) collective-permute-start(bf16[4,7,112,128]{3,2,1,0:T(8,128)(2,1)S(1)} %pad_maximum_fusion.2.u0), channel_id=1, source_target_pairs={{0,32},{8,40},{16,48},{24,56},{32,64},{40,72},{48,80},{56,88},{64,... | collective-permute-start | bytes 2408456 | tf_op jit(solution)/shard_map/ppermute | solution.py:161
  27.1 51.3 %collective-permute-start.18 = (bf16[4,7,112,128]{3,2,1,0:T(8,128)(2,1)S(1)}, bf16[4,7,112,128]{3,2,1,0:T(8,128)(2,1)S(1)}, u32[]{:S(2)}, u32[]{:S(2)}) collective-permute-start(bf16[4,7,112,128]{3,2,1,0:T(8,128)(2,1)S(1)} %pad_maximum_fusion.2.u0), channel_id=1, source_target_pairs={{0,96},{8,104},{16,112},{24,120},{32,0},{40,8},{48,16},{56,24},{64... | collective-permute-start | bytes 2408456 | tf_op jit(solution)/shard_map/ppermute | solution.py:161
  28.8 27.3 %collective-permute-start.22 = (bf16[7,112,128]{2,1,0:T(8,128)(2,1)S(1)}, bf16[7,112,128]{2,1,0:T(8,128)(2,1)S(1)}, u32[]{:S(2)}, u32[]{:S(2)}) collective-permute-start(bf16[7,112,128]{2,1,0:T(8,128)(2,1)S(1)} %get-tuple-element.74), channel_id=1, source_target_pairs={{0,96},{8,104},{16,112},{24,120},{32,0},{40,8},{48,16},{56,24},{64... | collective-permute-start | bytes 602120 | tf_op jit(solution)/shard_map/ppermute | solution.py:161
  30.6 25.9 %collective-permute-start.23 = (bf16[7,112,128]{2,1,0:T(8,128)(2,1)S(1)}, bf16[7,112,128]{2,1,0:T(8,128)(2,1)S(1)}, u32[]{:S(2)}, u32[]{:S(2)}) collective-permute-start(bf16[7,112,128]{2,1,0:T(8,128)(2,1)S(1)} %get-tuple-element.74), channel_id=1, source_target_pairs={{0,64},{8,72},{16,80},{24,88},{32,96},{40,104},{48,112},{56,120},{... | collective-permute-start | bytes 602120 | tf_op jit(solution)/shard_map/ppermute | solution.py:161
  31.2 29.5 %collective-permute-start.8 = (bf16[7,112,128]{2,1,0:T(8,128)(2,1)S(1)}, bf16[7,112,128]{2,1,0:T(8,128)(2,1)S(1)}, u32[]{:S(2)}, u32[]{:S(2)}) collective-permute-start(bf16[7,112,128]{2,1,0:T(8,128)(2,1)S(1)} %get-tuple-element.75), channel_id=1, source_target_pairs={{0,96},{8,104},{16,112},{24,120},{32,0},{40,8},{48,16},{56,24},{64... | collective-permute-start | bytes 602120 | tf_op jit(solution)/shard_map/ppermute | solution.py:161
  65.4 9.4 %collective-permute-start.2 = (bf16[7,112,128]{2,1,0:T(8,128)(2,1)S(1)}, bf16[7,112,128]{2,1,0:T(8,128)(2,1)S(1)}, u32[]{:S(2)}, u32[]{:S(2)}) collective-permute-start(bf16[7,112,128]{2,1,0:T(8,128)(2,1)S(1)} %get-tuple-element.79), channel_id=1, source_target_pairs={{0,16},{8,24},{16,0},{24,8},{32,48},{40,56},{48,32},{56,40},{64,80... | collective-permute-start | bytes 602120 | tf_op jit(solution)/shard_map/ppermute | solution.py:161
  69.3 22.6 %collective-permute-start.24 = (bf16[4,7,112,128]{3,2,1,0:T(8,128)(2,1)}, bf16[4,7,112,128]{3,2,1,0:T(8,128)(2,1)S(1)}, u32[]{:S(2)}, u32[]{:S(2)}) collective-permute-start(bf16[4,7,112,128]{3,2,1,0:T(8,128)(2,1)} %pad_maximum_fusion.3.d0), channel_id=1, source_target_pairs={{0,8},{8,16},{16,24},{24,0},{32,40},{40,48},{48,56},{56,32},{64,72... | collective-permute-start | bytes 2408456 | tf_op jit(solution)/shard_map/ppermute | solution.py:161
  71.2 29.2 %collective-permute-start.25 = (bf16[4,7,112,128]{3,2,1,0:T(8,128)(2,1)}, bf16[4,7,112,128]{3,2,1,0:T(8,128)(2,1)}, u32[]{:S(2)}, u32[]{:S(2)}) collective-permute-start(bf16[4,7,112,128]{3,2,1,0:T(8,128)(2,1)} %pad_maximum_fusion.3.d0), channel_id=1, source_target_pairs={{0,24},{8,0},{16,8},{24,16},{32,56},{40,32},{48,40},{56,48},{64,88... | collective-permute-start | bytes 2408456 | tf_op jit(solution)/shard_map/ppermute | solution.py:161
  74.9 29.4 %collective-permute-start.10 = (bf16[4,7,112,128]{3,2,1,0:T(8,128)(2,1)S(1)}, bf16[4,7,112,128]{3,2,1,0:T(8,128)(2,1)S(1)}, u32[]{:S(2)}, u32[]{:S(2)}) collective-permute-start(bf16[4,7,112,128]{3,2,1,0:T(8,128)(2,1)S(1)} %pad_maximum_fusion.1.d0), channel_id=1, source_target_pairs={{0,8},{8,16},{16,24},{24,0},{32,40},{40,48},{48,56},{56,32},{64,72... | collective-permute-start | bytes 2408456 | tf_op jit(solution)/shard_map/ppermute | solution.py:161
  76.1 32.7 %collective-permute-start.11 = (bf16[4,7,112,128]{3,2,1,0:T(8,128)(2,1)S(1)}, bf16[4,7,112,128]{3,2,1,0:T(8,128)(2,1)}, u32[]{:S(2)}, u32[]{:S(2)}) collective-permute-start(bf16[4,7,112,128]{3,2,1,0:T(8,128)(2,1)S(1)} %pad_maximum_fusion.1.d0), channel_id=1, source_target_pairs={{0,24},{8,0},{16,8},{24,16},{32,56},{40,32},{48,40},{56,48},{64,88... | collective-permute-start | bytes 2408456 | tf_op jit(solution)/shard_map/ppermute | solution.py:161
  78.4 30.8 %collective-permute-start.3 = (bf16[4,7,112,128]{3,2,1,0:T(8,128)(2,1)S(1)}, bf16[4,7,112,128]{3,2,1,0:T(8,128)(2,1)}, u32[]{:S(2)}, u32[]{:S(2)}) collective-permute-start(bf16[4,7,112,128]{3,2,1,0:T(8,128)(2,1)S(1)} %pad_maximum_fusion.u0), channel_id=1, source_target_pairs={{0,32},{8,40},{16,48},{24,56},{32,64},{40,72},{48,80},{56,88},{64,... | collective-permute-start | bytes 2408456 | tf_op jit(solution)/shard_map/ppermute | solution.py:161
  91.8 24.8 %collective-permute-start.4 = (bf16[4,7,112,128]{3,2,1,0:T(8,128)(2,1)S(1)}, bf16[4,7,112,128]{3,2,1,0:T(8,128)(2,1)}, u32[]{:S(2)}, u32[]{:S(2)}) collective-permute-start(bf16[4,7,112,128]{3,2,1,0:T(8,128)(2,1)S(1)} %pad_maximum_fusion.u0), channel_id=1, source_target_pairs={{0,96},{8,104},{16,112},{24,120},{32,0},{40,8},{48,16},{56,24},{64... | collective-permute-start | bytes 2408456 | tf_op jit(solution)/shard_map/ppermute | solution.py:161
  100.4 18.0 %collective-permute-start.19 = (bf16[2,7,112,128]{3,2,1,0:T(8,128)(2,1)}, bf16[2,7,112,128]{3,2,1,0:T(8,128)(2,1)S(1)}, u32[]{:S(2)}, u32[]{:S(2)}) collective-permute-start(bf16[2,7,112,128]{3,2,1,0:T(8,128)(2,1)} %slice.324), channel_id=1, source_target_pairs={{0,32},{8,40},{16,48},{24,56},{32,64},{40,72},{48,80},{56,88},{64,... | collective-permute-start | bytes 1204232 | tf_op jit(solution)/shard_map/ppermute | solution.py:161
  104.2 17.4 %collective-permute-start.20 = (bf16[2,7,112,128]{3,2,1,0:T(8,128)(2,1)}, bf16[2,7,112,128]{3,2,1,0:T(8,128)(2,1)}, u32[]{:S(2)}, u32[]{:S(2)}) collective-permute-start(bf16[2,7,112,128]{3,2,1,0:T(8,128)(2,1)} %slice.325), channel_id=1, source_target_pairs={{0,96},{8,104},{16,112},{24,120},{32,0},{40,8},{48,16},{56,24},{64... | collective-permute-start | bytes 1204232 | tf_op jit(solution)/shard_map/ppermute | solution.py:161
  108.8 12.9 %collective-permute-start.26 = (bf16[2,7,112,128]{3,2,1,0:T(8,128)(2,1)S(1)}, bf16[2,7,112,128]{3,2,1,0:T(8,128)(2,1)}, u32[]{:S(2)}, u32[]{:S(2)}) collective-permute-start(bf16[2,7,112,128]{3,2,1,0:T(8,128)(2,1)S(1)} %slice.326), channel_id=1, source_target_pairs={{0,8},{8,16},{16,24},{24,0},{32,40},{40,48},{48,56},{56,32},{64,72... | collective-permute-start | bytes 1204232 | tf_op jit(solution)/shard_map/ppermute | solution.py:161
  109.2 15.7 %collective-permute-start.27 = (bf16[2,7,112,128]{3,2,1,0:T(8,128)(2,1)}, bf16[2,7,112,128]{3,2,1,0:T(8,128)(2,1)}, u32[]{:S(2)}, u32[]{:S(2)}) collective-permute-start(bf16[2,7,112,128]{3,2,1,0:T(8,128)(2,1)} %slice.327), channel_id=1, source_target_pairs={{0,24},{8,0},{16,8},{24,16},{32,56},{40,32},{48,40},{56,48},{64,88... | collective-permute-start | bytes 1204232 | tf_op jit(solution)/shard_map/ppermute | solution.py:161
  116.6 32.6 %collective-permute-start.12 = (bf16[2,7,112,128]{3,2,1,0:T(8,128)(2,1)}, bf16[2,7,112,128]{3,2,1,0:T(8,128)(2,1)}, u32[]{:S(2)}, u32[]{:S(2)}) collective-permute-start(bf16[2,7,112,128]{3,2,1,0:T(8,128)(2,1)} %slice.322), channel_id=1, source_target_pairs={{0,8},{8,16},{16,24},{24,0},{32,40},{40,48},{48,56},{56,32},{64,72... | collective-permute-start | bytes 1204232 | tf_op jit(solution)/shard_map/ppermute | solution.py:161
  118.4 30.9 %collective-permute-start.13 = (bf16[2,7,112,128]{3,2,1,0:T(8,128)(2,1)}, bf16[2,7,112,128]{3,2,1,0:T(8,128)(2,1)}, u32[]{:S(2)}, u32[]{:S(2)}) collective-permute-start(bf16[2,7,112,128]{3,2,1,0:T(8,128)(2,1)} %slice.323), channel_id=1, source_target_pairs={{0,24},{8,0},{16,8},{24,16},{32,56},{40,32},{48,40},{56,48},{64,88... | collective-permute-start | bytes 1204232 | tf_op jit(solution)/shard_map/ppermute | solution.py:161
  121.6 27.6 %collective-permute-start.5 = (bf16[2,7,112,128]{3,2,1,0:T(8,128)(2,1)}, bf16[2,7,112,128]{3,2,1,0:T(8,128)(2,1)S(1)}, u32[]{:S(2)}, u32[]{:S(2)}) collective-permute-start(bf16[2,7,112,128]{3,2,1,0:T(8,128)(2,1)} %slice.320), channel_id=1, source_target_pairs={{0,32},{8,40},{16,48},{24,56},{32,64},{40,72},{48,80},{56,88},{64,... | collective-permute-start | bytes 1204232 | tf_op jit(solution)/shard_map/ppermute | solution.py:161
  121.7 27.6 %collective-permute-start.6 = (bf16[2,7,112,128]{3,2,1,0:T(8,128)(2,1)}, bf16[2,7,112,128]{3,2,1,0:T(8,128)(2,1)}, u32[]{:S(2)}, u32[]{:S(2)}) collective-permute-start(bf16[2,7,112,128]{3,2,1,0:T(8,128)(2,1)} %slice.321), channel_id=1, source_target_pairs={{0,96},{8,104},{16,112},{24,120},{32,0},{40,8},{48,16},{56,24},{64... | collective-permute-start | bytes 1204232 | tf_op jit(solution)/shard_map/ppermute | solution.py:161
  177.1 101.1 %reduce-scatter.5.cloned.1.call-start = ((), (), s32[]{:S(2)}) async-start(), calls=%async_computation.5 | async-start | bytes 4128768 | tf_op jit(solution)/shard_map/reduce_scatter | solution.py:227
  177.7 12.2 %collective-permute-start.42 = (bf16[2,7,112,128]{3,2,1,0:T(8,128)(2,1)S(1)}, bf16[2,7,112,128]{3,2,1,0:T(8,128)(2,1)S(1)}, u32[]{:S(2)}, u32[]{:S(2)}) collective-permute-start(bf16[2,7,112,128]{3,2,1,0:T(8,128)(2,1)S(1)} %get-tuple-element.44), channel_id=1, source_target_pairs={{0,8},{8,16},{16,24},{24,0},{32,40},{40,48},{48,56},{56,32},{64,72... | collective-permute-start | bytes 1204232 | tf_op jit(solution)/shard_map/ppermute | solution.py:161
  177.8 15.5 %collective-permute-start.44 = (bf16[2,7,112,128]{3,2,1,0:T(8,128)(2,1)S(1)}, bf16[2,7,112,128]{3,2,1,0:T(8,128)(2,1)S(1)}, u32[]{:S(2)}, u32[]{:S(2)}) collective-permute-start(bf16[2,7,112,128]{3,2,1,0:T(8,128)(2,1)S(1)} %get-tuple-element.46), channel_id=1, source_target_pairs={{0,24},{8,0},{16,8},{24,16},{32,56},{40,32},{48,40},{56,48},{64,88... | collective-permute-start | bytes 1204232 | tf_op jit(solution)/shard_map/ppermute | solution.py:161
  183.2 10.6 %collective-permute-start.49 = (bf16[2,7,112,128]{3,2,1,0:T(8,128)(2,1)S(1)}, bf16[2,7,112,128]{3,2,1,0:T(8,128)(2,1)S(1)}, u32[]{:S(2)}, u32[]{:S(2)}) collective-permute-start(bf16[2,7,112,128]{3,2,1,0:T(8,128)(2,1)S(1)} %copy-done.1), channel_id=1, source_target_pairs={{0,8},{8,16},{16,24},{24,0},{32,40},{40,48},{48,56},{56,32},{64,72... | collective-permute-start | bytes 1204232 | tf_op jit(solution)/shard_map/ppermute | solution.py:161
  184.3 12.7 %collective-permute-start.51 = (bf16[2,7,112,128]{3,2,1,0:T(8,128)(2,1)S(1)}, bf16[2,7,112,128]{3,2,1,0:T(8,128)(2,1)S(1)}, u32[]{:S(2)}, u32[]{:S(2)}) collective-permute-start(bf16[2,7,112,128]{3,2,1,0:T(8,128)(2,1)S(1)} %get-tuple-element.51), channel_id=1, source_target_pairs={{0,24},{8,0},{16,8},{24,16},{32,56},{40,32},{48,40},{56,48},{64,88... | collective-permute-start | bytes 1204232 | tf_op jit(solution)/shard_map/ppermute | solution.py:161
  188.6 9.8 %collective-permute-start.28 = (bf16[2,7,112,128]{3,2,1,0:T(8,128)(2,1)S(1)}, bf16[2,7,112,128]{3,2,1,0:T(8,128)(2,1)S(1)}, u32[]{:S(2)}, u32[]{:S(2)}) collective-permute-start(bf16[2,7,112,128]{3,2,1,0:T(8,128)(2,1)S(1)} %get-tuple-element.34), channel_id=1, source_target_pairs={{0,32},{8,40},{16,48},{24,56},{32,64},{40,72},{48,80},{56,88},{64,... | collective-permute-start | bytes 1204232 | tf_op jit(solution)/shard_map/ppermute | solution.py:161
  190.0 10.9 %collective-permute-start.30 = (bf16[2,7,112,128]{3,2,1,0:T(8,128)(2,1)S(1)}, bf16[2,7,112,128]{3,2,1,0:T(8,128)(2,1)S(1)}, u32[]{:S(2)}, u32[]{:S(2)}) collective-permute-start(bf16[2,7,112,128]{3,2,1,0:T(8,128)(2,1)S(1)} %get-tuple-element.36), channel_id=1, source_target_pairs={{0,96},{8,104},{16,112},{24,120},{32,0},{40,8},{48,16},{56,24},{64... | collective-permute-start | bytes 1204232 | tf_op jit(solution)/shard_map/ppermute | solution.py:161
  193.3 12.0 %collective-permute-start.35 = (bf16[2,7,112,128]{3,2,1,0:T(8,128)(2,1)S(1)}, bf16[2,7,112,128]{3,2,1,0:T(8,128)(2,1)S(1)}, u32[]{:S(2)}, u32[]{:S(2)}) collective-permute-start(bf16[2,7,112,128]{3,2,1,0:T(8,128)(2,1)S(1)} %get-tuple-element.39), channel_id=1, source_target_pairs={{0,32},{8,40},{16,48},{24,56},{32,64},{40,72},{48,80},{56,88},{64,... | collective-permute-start | bytes 1204232 | tf_op jit(solution)/shard_map/ppermute | solution.py:161
  193.8 11.8 %collective-permute-start.37 = (bf16[2,7,112,128]{3,2,1,0:T(8,128)(2,1)S(1)}, bf16[2,7,112,128]{3,2,1,0:T(8,128)(2,1)S(1)}, u32[]{:S(2)}, u32[]{:S(2)}) collective-permute-start(bf16[2,7,112,128]{3,2,1,0:T(8,128)(2,1)S(1)} %get-tuple-element.41), channel_id=1, source_target_pairs={{0,96},{8,104},{16,112},{24,120},{32,0},{40,8},{48,16},{56,24},{64... | collective-permute-start | bytes 1204232 | tf_op jit(solution)/shard_map/ppermute | solution.py:161
  197.1 22.1 %collective-permute-start.43 = (bf16[4,7,112,128]{3,2,1,0:T(8,128)(2,1)S(1)}, bf16[4,7,112,128]{3,2,1,0:T(8,128)(2,1)S(1)}, u32[]{:S(2)}, u32[]{:S(2)}) collective-permute-start(bf16[4,7,112,128]{3,2,1,0:T(8,128)(2,1)S(1)} %pad_maximum_fusion.8), channel_id=1, source_target_pairs={{0,8},{8,16},{16,24},{24,0},{32,40},{40,48},{48,56},{56,32},{64,72... | collective-permute-start | bytes 2408456 | tf_op jit(solution)/shard_map/ppermute | solution.py:161
  198.4 20.9 %collective-permute-start.45 = (bf16[4,7,112,128]{3,2,1,0:T(8,128)(2,1)S(1)}, bf16[4,7,112,128]{3,2,1,0:T(8,128)(2,1)S(1)}, u32[]{:S(2)}, u32[]{:S(2)}) collective-permute-start(bf16[4,7,112,128]{3,2,1,0:T(8,128)(2,1)S(1)} %pad_maximum_fusion.9), channel_id=1, source_target_pairs={{0,24},{8,0},{16,8},{24,16},{32,56},{40,32},{48,40},{56,48},{64,88... | collective-permute-start | bytes 2408456 | tf_op jit(solution)/shard_map/ppermute | solution.py:161
  200.9 27.1 %collective-permute-start.50 = (bf16[4,7,112,128]{3,2,1,0:T(8,128)(2,1)S(1)}, bf16[4,7,112,128]{3,2,1,0:T(8,128)(2,1)S(1)}, u32[]{:S(2)}, u32[]{:S(2)}) collective-permute-start(bf16[4,7,112,128]{3,2,1,0:T(8,128)(2,1)S(1)} %pad_maximum_fusion.10), channel_id=1, source_target_pairs={{0,8},{8,16},{16,24},{24,0},{32,40},{40,48},{48,56},{56,32},{64,72... | collective-permute-start | bytes 2408456 | tf_op jit(solution)/shard_map/ppermute | solution.py:161
  205.4 23.7 %collective-permute-start.52 = (bf16[4,7,112,128]{3,2,1,0:T(8,128)(2,1)S(1)}, bf16[4,7,112,128]{3,2,1,0:T(8,128)(2,1)S(1)}, u32[]{:S(2)}, u32[]{:S(2)}) collective-permute-start(bf16[4,7,112,128]{3,2,1,0:T(8,128)(2,1)S(1)} %pad_maximum_fusion.11), channel_id=1, source_target_pairs={{0,24},{8,0},{16,8},{24,16},{32,56},{40,32},{48,40},{56,48},{64,88... | collective-permute-start | bytes 2408456 | tf_op jit(solution)/shard_map/ppermute | solution.py:161
  205.6 25.7 %collective-permute-start.29 = (bf16[4,7,112,128]{3,2,1,0:T(8,128)(2,1)S(1)}, bf16[4,7,112,128]{3,2,1,0:T(8,128)(2,1)S(1)}, u32[]{:S(2)}, u32[]{:S(2)}) collective-permute-start(bf16[4,7,112,128]{3,2,1,0:T(8,128)(2,1)S(1)} %pad_maximum_fusion.4), channel_id=1, source_target_pairs={{0,32},{8,40},{16,48},{24,56},{32,64},{40,72},{48,80},{56,88},{64,... | collective-permute-start | bytes 2408456 | tf_op jit(solution)/shard_map/ppermute | solution.py:161
  219.2 20.7 %collective-permute-start.31 = (bf16[4,7,112,128]{3,2,1,0:T(8,128)(2,1)S(1)}, bf16[4,7,112,128]{3,2,1,0:T(8,128)(2,1)S(1)}, u32[]{:S(2)}, u32[]{:S(2)}) collective-permute-start(bf16[4,7,112,128]{3,2,1,0:T(8,128)(2,1)S(1)} %pad_maximum_fusion.5), channel_id=1, source_target_pairs={{0,96},{8,104},{16,112},{24,120},{32,0},{40,8},{48,16},{56,24},{64... | collective-permute-start | bytes 2408456 | tf_op jit(solution)/shard_map/ppermute | solution.py:161
  219.3 22.1 %collective-permute-start.36 = (bf16[4,7,112,128]{3,2,1,0:T(8,128)(2,1)S(1)}, bf16[4,7,112,128]{3,2,1,0:T(8,128)(2,1)S(1)}, u32[]{:S(2)}, u32[]{:S(2)}) collective-permute-start(bf16[4,7,112,128]{3,2,1,0:T(8,128)(2,1)S(1)} %pad_maximum_fusion.6), channel_id=1, source_target_pairs={{0,32},{8,40},{16,48},{24,56},{32,64},{40,72},{48,80},{56,88},{64,... | collective-permute-start | bytes 2408456 | tf_op jit(solution)/shard_map/ppermute | solution.py:161
  227.9 28.7 %collective-permute-start.38 = (bf16[4,7,112,128]{3,2,1,0:T(8,128)(2,1)S(1)}, bf16[4,7,112,128]{3,2,1,0:T(8,128)(2,1)S(1)}, u32[]{:S(2)}, u32[]{:S(2)}) collective-permute-start(bf16[4,7,112,128]{3,2,1,0:T(8,128)(2,1)S(1)} %pad_maximum_fusion.7), channel_id=1, source_target_pairs={{0,96},{8,104},{16,112},{24,120},{32,0},{40,8},{48,16},{56,24},{64... | collective-permute-start | bytes 2408456 | tf_op jit(solution)/shard_map/ppermute | solution.py:161
  229.1 29.7 %collective-permute-start.46 = (bf16[7,112,128]{2,1,0:T(8,128)(2,1)S(1)}, bf16[7,112,128]{2,1,0:T(8,128)(2,1)S(1)}, u32[]{:S(2)}, u32[]{:S(2)}) collective-permute-start(bf16[7,112,128]{2,1,0:T(8,128)(2,1)S(1)} %get-tuple-element.60), channel_id=1, source_target_pairs={{0,96},{8,104},{16,112},{24,120},{32,0},{40,8},{48,16},{56,24},{64... | collective-permute-start | bytes 602120 | tf_op jit(solution)/shard_map/ppermute | solution.py:161
  231.3 28.4 %collective-permute-start.47 = (bf16[7,112,128]{2,1,0:T(8,128)(2,1)S(1)}, bf16[7,112,128]{2,1,0:T(8,128)(2,1)S(1)}, u32[]{:S(2)}, u32[]{:S(2)}) collective-permute-start(bf16[7,112,128]{2,1,0:T(8,128)(2,1)S(1)} %get-tuple-element.62), channel_id=1, source_target_pairs={{0,32},{8,40},{16,48},{24,56},{32,64},{40,72},{48,80},{56,88},{64,... | collective-permute-start | bytes 602120 | tf_op jit(solution)/shard_map/ppermute | solution.py:161
  239.9 19.9 %collective-permute-start.48 = (bf16[7,112,128]{2,1,0:T(8,128)(2,1)S(1)}, bf16[7,112,128]{2,1,0:T(8,128)(2,1)S(1)}, u32[]{:S(2)}, u32[]{:S(2)}) collective-permute-start(bf16[7,112,128]{2,1,0:T(8,128)(2,1)S(1)} %get-tuple-element.61), channel_id=1, source_target_pairs={{0,64},{8,72},{16,80},{24,88},{32,96},{40,104},{48,112},{56,120},{... | collective-permute-start | bytes 602120 | tf_op jit(solution)/shard_map/ppermute | solution.py:161
  241.4 21.7 %collective-permute-start.53 = (bf16[7,112,128]{2,1,0:T(8,128)(2,1)S(1)}, bf16[7,112,128]{2,1,0:T(8,128)(2,1)S(1)}, u32[]{:S(2)}, u32[]{:S(2)}) collective-permute-start(bf16[7,112,128]{2,1,0:T(8,128)(2,1)S(1)} %get-tuple-element.63), channel_id=1, source_target_pairs={{0,96},{8,104},{16,112},{24,120},{32,0},{40,8},{48,16},{56,24},{64... | collective-permute-start | bytes 602120 | tf_op jit(solution)/shard_map/ppermute | solution.py:161
  259.7 9.9 %collective-permute-start.33 = (bf16[7,112,128]{2,1,0:T(8,128)(2,1)S(1)}, bf16[7,112,128]{2,1,0:T(8,128)(2,1)S(1)}, u32[]{:S(2)}, u32[]{:S(2)}) collective-permute-start(bf16[7,112,128]{2,1,0:T(8,128)(2,1)S(1)} %get-tuple-element.68), channel_id=1, source_target_pairs={{0,8},{8,16},{16,24},{24,0},{32,40},{40,48},{48,56},{56,32},{64,72... | collective-permute-start | bytes 602120 | tf_op jit(solution)/shard_map/ppermute | solution.py:161
  266.0 9.1 %collective-permute-start.40 = (bf16[7,112,128]{2,1,0:T(8,128)(2,1)S(1)}, bf16[7,112,128]{2,1,0:T(8,128)(2,1)S(1)}, u32[]{:S(2)}, u32[]{:S(2)}) collective-permute-start(bf16[7,112,128]{2,1,0:T(8,128)(2,1)S(1)} %get-tuple-element.71), channel_id=1, source_target_pairs={{0,8},{8,16},{16,24},{24,0},{32,40},{40,48},{48,56},{56,32},{64,72... | collective-permute-start | bytes 602120 | tf_op jit(solution)/shard_map/ppermute | solution.py:161
  (38 other events, 701.8 us)
Sparse Core Ops, SparseCore 0:
  10.3 32.6 all-gather.2
  45.2 29.8 all-gather.4
  177.2 35.2 reduce-scatter.2
  214.8 35.9 reduce-scatter.4

commit v2 on v0

v2 whole, which is shorter than its diff:
```python
import functools

import jax
import jax.numpy as jnp
from jax import lax
from jax.experimental import pallas as pl
from jax.experimental.pallas import tpu as pltpu
from jax.sharding import PartitionSpec as P

D = 7168
BLK = 128
KEEP = 14
NFB = D // BLK
ROWS = KEEP * BLK
F32 = jnp.float32
BF16 = jnp.bfloat16
SIDE = 4
STEP = (0, -1, 1, 2)
TENSOR = 8
VMEM_LIMIT = 56 * 2**20
MANY = 2
NT = (((1,), (1,)), ((), ()))
TN = (((0,), (0,)), ((), ()))


def gelu_and_slope(v):
    c = 0.7978845608028654
    v2 = v * v
    th = jnp.tanh(c * (v + 0.044715 * v * v2))
    half = 0.5 * (1.0 + th)
    slope = half + 0.5 * v * (1.0 - th * th) * (c * (1.0 + 3 * 0.044715 * v2))
    return v * half, slope


def cols(k):
    return slice(k * BLK, (k + 1) * BLK)


def pieces(rows_tbl, halves):
    for n, ref in enumerate(halves):
        for s in range(2):
            yield pl.ds(pl.multiple_of(rows_tbl[n * 2 + s], 16), ref.shape[3]), ref, s


def layer_kernel(base, has_prev, rows_tbl, upk, dnk, acts, *rest):
    w_in, rest = rest[:8], rest[8:]
    prev, rest = rest[:has_prev], rest[has_prev:]
    sums, w_out = rest[0], rest[1:9]
    tokg, cotg, upw, dnw, dnr, uterm, dterm, out_acc, in_acc = rest[9:]
    step = pl.program_id(0)
    per = acts.shape[2]
    many = tokg.shape[0]

    @pl.when(step == 0)
    def _():
        out_acc[...] = jnp.zeros_like(out_acc)
        in_acc[...] = jnp.zeros_like(in_acc)

    for b in range(many):
        j = base + step * many + b
        for at, ref, s in pieces(rows_tbl, w_in):
            upw[b, at, :] = ref[s, 0, b]
            dnr[b, at, :] = ref[s, 1, b]
        for k in range(KEEP):
            for which, kept, to in ((0, upk, tokg), (1, dnk, cotg)):
                f = kept[j, k]
                to[b, :, cols(k)] = acts[f // per, which, f % per]
            dnw[b, :, cols(k)] = dnr[b, cols(k), :]

    pre = [jnp.dot(tokg[b], upw[b], preferred_element_type=F32) for b in range(many)]
    grad_hidden = [
        lax.dot_general(cotg[b], dnw[b], NT, preferred_element_type=F32) for b in range(many)
    ]
    acted = [gelu_and_slope(p) for p in pre]
    hidden = [h.astype(BF16) for h, _ in acted]
    grad_pre = [(g * s).astype(BF16) for g, (_, s) in zip(grad_hidden, acted)]
    for b in range(many):
        j = base + step * many + b
        dt = lax.dot_general(hidden[b], cotg[b], TN, preferred_element_type=F32).astype(BF16)
        for k in range(KEEP):
            dterm[b, cols(k), :] = dt[:, cols(k)]
        uterm[b] = lax.dot_general(
            tokg[b], grad_pre[b], TN, preferred_element_type=F32).astype(BF16)
        for k in range(KEEP):
            out_acc[dnk[j, k]] += jnp.dot(hidden[b], dnr[b, cols(k), :], preferred_element_type=F32)
            in_acc[upk[j, k]] += lax.dot_general(
                grad_pre[b], upw[b, cols(k), :], NT, preferred_element_type=F32
            )
    for b in range(many):
        for at, ref, s in pieces(rows_tbl, w_out):
            ref[s, 0, b] = uterm[b, at, :]
            ref[s, 1, b] = dterm[b, at, :]

    @pl.when(step == pl.num_programs(0) - 1)
    def _():
        for s in range(sums.shape[0]):
            for which, acc in enumerate((out_acc, in_acc)):
                for i in range(per):
                    total = acc[s * per + i]
                    if has_prev:
                        total = total + prev[0][s, which, :, cols(i)].astype(F32)
                    sums[s, which, :, cols(i)] = total.astype(BF16)


def layer_part(base, rows_tbl, upk, dnk, acts, group, prev):
    local, part = group[0].shape[2:4]
    shards, _, per, tokens, _ = acts.shape
    many = MANY
    piece = pl.BlockSpec((2, 2, many, part, BLK), lambda j, *_: (0, 0, j, 0, 0))
    sums = jax.ShapeDtypeStruct((shards, 2, tokens, per * BLK), BF16)
    whole = pl.BlockSpec(sums.shape, lambda j, *_: (0,) * 4, pipeline_mode=pl.Buffered(1))
    term = jax.ShapeDtypeStruct(group[0].shape, BF16)
    extra = [] if prev is None else [prev]
    outs = pl.pallas_call(
        functools.partial(layer_kernel, base, len(extra)),
        grid_spec=pltpu.PrefetchScalarGridSpec(
            num_scalar_prefetch=3,
            grid=(local // many,),
            in_specs=[pl.BlockSpec(acts.shape, lambda j, *_: (0,) * 5, pipeline_mode=pl.Buffered(1))]
            + [piece] * 8 + [whole] * len(extra),
            out_specs=[whole] + [piece] * 8,
            scratch_shapes=[
                pltpu.VMEM((many, tokens, ROWS), BF16),
                pltpu.VMEM((many, tokens, ROWS), BF16),
                pltpu.VMEM((many, ROWS, BLK), BF16),
                pltpu.VMEM((many, BLK, ROWS), BF16),
                pltpu.VMEM((many, ROWS, BLK), BF16),
                pltpu.VMEM((many, ROWS, BLK), BF16),
                pltpu.VMEM((many, ROWS, BLK), BF16),
                pltpu.VMEM((NFB, tokens, BLK), F32),
                pltpu.VMEM((NFB, tokens, BLK), F32),
            ],
        ),
        out_shape=[sums] + [term] * 8,
        compiler_params=pltpu.CompilerParams(vmem_limit_bytes=VMEM_LIMIT),
        cost_estimate=pl.CostEstimate(
            flops=local * 24 * tokens * ROWS * BLK,
            bytes_accessed=4 * NFB * tokens * BLK * 2 + 8 * local * ROWS * BLK,
            transcendentals=local * tokens * BLK,
        ),
    )(rows_tbl, upk, dnk, acts, *group, *extra)
    return outs[0], outs[1:]


def shift(value, leg, by):
    pairs = []
    for y in range(SIDE):
        for x in range(SIDE):
            for t in range(TENSOR):
                along_x = t % 2 == leg
                to = (y, (x + by) % SIDE) if along_x else ((y + by) % SIDE, x)
                pairs.append(((y * SIDE + x) * TENSOR + t, (to[0] * SIDE + to[1]) * TENSOR + t))
    return lax.ppermute(value, ("dp", "tensor"), pairs)


def add(*terms):
    return sum(t.astype(F32) for t in terms).astype(BF16)


def near(shard):
    return shift(shard, 0, 1), shift(shard, 0, -1), shift(shard, 0, 2)


def cross(shard, got):
    a, b = jnp.stack([shard, got[0]]), jnp.stack([got[1], got[2]])
    return a, b, shift(a, 1, 1), shift(b, 1, 1), shift(a, 1, -1), shift(b, 1, -1)


def onward(group):
    return shift(group[2], 1, 1), shift(group[5], 1, -1)


def send_far(terms):
    _, _, to_minus_a, _, _, to_plus_b, far_a, far_b = terms
    return shift(far_a, 1, 1), shift(far_b, 1, -1), shift(to_plus_b, 1, 1), shift(to_minus_a, 1, -1)


def send_near(terms, got):
    to_minus_b, to_plus_a = terms[3], terms[4]
    return shift(add(to_plus_a, got[0]), 1, 1), shift(add(to_minus_b, got[1]), 1, -1)


def send_slots(terms, got, got_near):
    a, b = (terms[0], got_near[0], got[3]), (terms[1], got[2], got_near[1])
    slot = [add(*(p[s] for p in half)) for half in (a, b) for s in range(2)]
    return slot[0], shift(slot[1], 0, -1), shift(slot[2], 0, 1), shift(slot[3], 0, 2)


def tie(*values):
    return lax.optimization_barrier(values)


def body(tokens, cotangent, up_weight, down_weight, up_kept, down_kept):
    count, part = up_weight.shape[:2]
    rows = tokens.shape[0]
    shards = D // tokens.shape[1]

    def blocks(a):
        return a.reshape(rows, -1, BLK).transpose(1, 0, 2)

    acts = lax.all_gather(jnp.stack([blocks(tokens), blocks(cotangent)]), "tensor", axis=0)

    me = lax.axis_index("dp")
    y, x = me // SIDE, me % SIDE
    far = jnp.array(STEP, jnp.int32)
    ys, xs = (y + far) % SIDE, (x + far) % SIDE
    rows_tbl = part * jnp.where(
        lax.axis_index("tensor") % 2 == 0,
        ys[:, None] * SIDE + xs[None, :],
        ys[None, :] * SIDE + xs[:, None],
    ).reshape(-1)

    first = 6
    w = tuple(
        jnp.stack([up_weight[s], down_weight[s]]) for s in (slice(0, first), slice(first, count))
    )

    n0 = near(w[0])
    n0, w = tie(n0, w)

    c0 = cross(w[0], n0)
    c0, w = tie(c0, w)

    g0, n1 = c0 + onward(c0), near(w[1])
    g0, n1, acts = tie(g0, n1, acts)

    c1 = cross(w[1], n1)
    sums, t0 = layer_part(0, rows_tbl, up_kept, down_kept, acts, g0, None)
    c1, sums, t0, acts = tie(c1, sums, t0, acts)

    g1, f0 = c1 + onward(c1), send_far(t0)
    g1, sums, acts = tie(g1, sums, acts)

    sums, t1 = layer_part(first, rows_tbl, up_kept, down_kept, acts, g1, sums)
    sums, t0, t1, f0 = tie(sums, t0, t1, f0)

    summed = lax.psum_scatter(sums, "tensor", scatter_dimension=0)
    s0, f1 = send_near(t0, f0), send_far(t1)
    s0, f1 = tie(s0, f1)

    l0, s1 = send_slots(t0, f0, s0), send_near(t1, f1)
    l0, s1 = tie(l0, s1)

    l1 = send_slots(t1, f1, s1)
    ups, dns = zip(*(add(*part) for part in (l0, l1)))
    return summed[0], summed[1], jnp.concatenate(ups), jnp.concatenate(dns)


def solution(mesh):
    placed = (
        P("dp", "tensor"),
        P("dp", "tensor"),
        P("tensor", "dp", None),
        P("tensor", "dp", None),
        P("tensor", None),
        P("tensor", None),
    )
    return jax.shard_map(
        body,
        mesh=mesh,
        in_specs=placed,
        out_specs=placed[:4],
        check_vma=False,
    )
```

time: 621 us -> 225 us (0.36)
  waiting for transfers between devices: 303 us -> 95.3 us
  other arithmetic: 157 us -> 4.62 us
  local copies, waits for them, and re-layouts: 81 us -> 10.5 us
  matrix products: 63.8 us -> 0 us
  starting transfers between devices: 0.32 us -> 51.3 us
  Pallas kernels: 0 us -> 48.1 us
    reduce_scatter x4 -> x1, waiting for transfers between devices: 196 us -> 0.01 us  [body(): summed = lax.psum_scatter(sums, 'tensor', scatter_dimension=0)]
    scatter-add x2 -> x0, other arithmetic: 124 us -> none  [place_blocks(): placed = placed.at[:, kept_index.reshape(-1)].add(terms)]
    all_gather x4 -> x1, waiting for transfers between devices: 106 us -> 0.01 us  [body(): lax.all_gather(jnp.stack([blocks(tokens), blocks(cotangent)]), 'tensor',...]
    ppermute x0 -> x36, waiting for transfers between devices: none -> 95.2 us  [shift(): return lax.ppermute(value, ('dp', 'tensor'), pairs)]
    dot_general x6 -> x0, matrix products: 63.8 us -> none  [the longest x1 13.5 us: body(): jnp.einsum('tfe,fked->tfkd', hidden, down_four, preferred_element_type=jn...]
    ppermute x0 -> x36, starting transfers between devices: none -> 51.3 us  [shift(): return lax.ppermute(value, ('dp', 'tensor'), pairs)]
    pallas_call x0 -> x2, Pallas kernels: none -> 48.1 us  [layer_part(): pl.pallas_call(functools.partial(layer_kernel, base, len(extra)), grid_sp...]
    select_n x6 -> x0, other arithmetic: 22.1 us -> none  [the longest x2 11.1 us: body(): jnp.take(tok_full.reshape(token_count, block_count, BLK), up_kept.reshape...]
  transfers between devices with their start and end apart: 8 -> 38, of which waited for: 6 -> 17; matrix products, arithmetic and copies ran while one was open for 32% -> 2% of each run, Pallas kernels for 0% -> 21%
where the time goes in v2:
time: 225 us; the launch traced here: 224 us
  waiting for transfers between devices  95.3 us (42%)
  starting transfers between devices  51.3 us (23%)
  Pallas kernels  48.1 us (21%)
  between operations  14.5 us (6%)
  local copies, waits for them, and re-layouts  10.5 us (5%)
  other arithmetic  4.62 us (2%)
    ppermute x36, waiting for transfers between devices, shift(): return lax.ppermute(value, ('dp', 'tensor'), pairs)  95.2 us
    ppermute x36, starting transfers between devices, shift(): return lax.ppermute(value, ('dp', 'tensor'), pairs)  51.3 us
    pallas_call x2, Pallas kernels, layer_part(): pl.pallas_call(functools.partial(layer_kernel, base, len(extra)), grid_sp...  48.1 us
    unnamed x42, local copies, waits for them, and re-layouts  6.31 us
  transfers between devices with their start and end apart: 38, of which 17 were waited for; matrix products, arithmetic and copies ran while one was open for 2% of the time, Pallas kernels for 21%

profile of v2, /device:TPU:0, one launch (start us, length us, event | category | flops | bytes accessed | tf_op | source)
XLA Modules:
  0.0 224.4 jit_solution(15021859797988263005)
XLA Ops:
  7.2 1.2 copy.16
  8.4 1.2 copy.17
  9.8 1.3 copy.18
  11.3 1.7 collective-permute-start
  12.9 1.6 collective-permute-start.1
  14.6 1.9 collective-permute-start.2
  16.6 3.2 %collective-permute-done = bf16[2,6,112,128]{3,2,1,0:T(8,128)(2,1)S(1)} collective-permute-done((bf16[2,6,112,128]{3,2,1,0:T(8,128)(2,1)S(1)}, bf16[2,6,112,128]{3,2,1,0:T(8,128)(2,1)S(1)}, u32[]{:S(2)}, u32[]{:S(2)}) %collective-permute-start) | collective-permute-done | bytes 344096 | tf_op jit(solution)/shard_map/ppermute | solution.py:153
  20.2 4.4 %collective-permute-done.2 = bf16[2,6,112,128]{3,2,1,0:T(8,128)(2,1)S(1)} collective-permute-done((bf16[2,6,112,128]{3,2,1,0:T(8,128)(2,1)S(1)}, bf16[2,6,112,128]{3,2,1,0:T(8,128)(2,1)S(1)}, u32[]{:S(2)}, u32[]{:S(2)}) %collective-permute-start.2) | collective-permute-done | bytes 344096 | tf_op jit(solution)/shard_map/ppermute | solution.py:153
  24.7 1.6 collective-permute-start.3
  26.3 1.7 collective-permute-start.5
  28.5 2.9 %collective-permute-start.6 = (bf16[2,2,6,112,128]{4,3,2,1,0:T(8,128)(2,1)S(1)}, bf16[2,2,6,112,128]{4,3,2,1,0:T(8,128)(2,1)}, u32[]{:S(2)}, u32[]{:S(2)}) collective-permute-start(bf16[2,2,6,112,128]{4,3,2,1,0:T(8,128)(2,1)S(1)} %pad_maximum_fusion.4.rest_1_), channel_id=1, source_target_pairs={{0,96},{1,25},{2,98},{3,27},{4,100},{5,29},{6,102},{7,31},{8,104},... | collective-permute-start | bytes 2064392 | tf_op jit(solution)/shard_map/ppermute | solution.py:153
  31.3 5.6 %collective-permute-done.3.rest_2_ = bf16[2,2,6,112,128]{4,3,2,1,0:T(8,128)(2,1)} collective-permute-done((bf16[2,2,6,112,128]{4,3,2,1,0:T(8,128)(2,1)S(1)}, bf16[2,2,6,112,128]{4,3,2,1,0:T(8,128)(2,1)}, u32[]{:S(2)}, u32[]{:S(2)}) %collective-permute-start.3) | collective-permute-done | bytes 688160 | tf_op jit(solution)/shard_map/ppermute | solution.py:153
  37.2 7.0 %collective-permute-done.4.rest_3_ = bf16[2,2,6,112,128]{4,3,2,1,0:T(8,128)(2,1)S(1)} collective-permute-done((bf16[2,2,6,112,128]{4,3,2,1,0:T(8,128)(2,1)S(1)}, bf16[2,2,6,112,128]{4,3,2,1,0:T(8,128)(2,1)S(1)}, u32[]{:S(2)}, u32[]{:S(2)}) %collective-permute-start.4) | collective-permute-done | bytes 688160 | tf_op jit(solution)/shard_map/ppermute | solution.py:153
  44.7 1.6 collective-permute-start.7
  46.3 1.7 collective-permute-start.8
  48.0 2.3 %collective-permute-start.10 = (bf16[2,8,112,128]{3,2,1,0:T(8,128)(2,1)S(1)}, bf16[2,8,112,128]{3,2,1,0:T(8,128)(2,1)S(1)}, u32[]{:S(2)}, u32[]{:S(2)}) collective-permute-start(bf16[2,8,112,128]{3,2,1,0:T(8,128)(2,1)S(1)} %pad_maximum_fusion.5), channel_id=1, source_target_pairs={{0,24},{1,97},{2,26},{3,99},{4,28},{5,101},{6,30},{7,103},{8,0},{9... | collective-permute-start | bytes 1376264 | tf_op jit(solution)/shard_map/ppermute | solution.py:153
  50.2 1.2 collective-permute-start.11
  51.5 11.8 %collective-permute-done.10 = bf16[2,8,112,128]{3,2,1,0:T(8,128)(2,1)S(1)} collective-permute-done((bf16[2,8,112,128]{3,2,1,0:T(8,128)(2,1)S(1)}, bf16[2,8,112,128]{3,2,1,0:T(8,128)(2,1)S(1)}, u32[]{:S(2)}, u32[]{:S(2)}) %collective-permute-start.10) | collective-permute-done | bytes 458784 | tf_op jit(solution)/shard_map/ppermute | solution.py:153
  63.3 1.9 collective-permute-done.9
  65.1 1.9 collective-permute-done.7.rest_6_
  67.2 3.2 %collective-permute-start.15 = (bf16[2,2,8,112,128]{4,3,2,1,0:T(8,128)(2,1)S(1)}, bf16[2,2,8,112,128]{4,3,2,1,0:T(8,128)(2,1)}, u32[]{:S(2)}, u32[]{:S(2)}) collective-permute-start(bf16[2,2,8,112,128]{4,3,2,1,0:T(8,128)(2,1)S(1)} %pad_maximum_fusion.2.rest_1_), channel_id=1, source_target_pairs={{0,96},{1,25},{2,98},{3,27},{4,100},{5,29},{6,102},{7,31},{8,104},... | collective-permute-start | bytes 2752520 | tf_op jit(solution)/shard_map/ppermute | solution.py:153
  70.6 3.2 %collective-permute-start.14 = (bf16[2,2,8,112,128]{4,3,2,1,0:T(8,128)(2,1)S(1)}, bf16[2,2,8,112,128]{4,3,2,1,0:T(8,128)(2,1)S(1)}, u32[]{:S(2)}, u32[]{:S(2)}) collective-permute-start(bf16[2,2,8,112,128]{4,3,2,1,0:T(8,128)(2,1)S(1)} %pad_maximum_fusion.1.rest_0_), channel_id=1, source_target_pairs={{0,96},{1,25},{2,98},{3,27},{4,100},{5,29},{6,102},{7,31},{8,104},... | collective-permute-start | bytes 2752520 | tf_op jit(solution)/shard_map/ppermute | solution.py:153
  74.5 21.2 %shard_map.102 = (bf16[8,2,256,896]{3,2,1,0:T(8,128)(2,1)}, bf16[2,2,6,112,128]{4,3,2,1,0:T(8,128)(2,1)}, bf16[2,2,6,112,128]{4,3,2,1,0:T(8,128)(2,1)}, bf16[2,2...) custom-call(s32[16]{0:T(128)} %mul.13.rows_tbl, ...), custom_call_target="tpu_custom_call" | custom-call | flops 8455716864 | bytes 25690112 | tf_op jit(solution)/shard_map/pallas_call | solution.py:114
  95.8 0.8 copy-done.15
  96.7 2.4 %collective-permute-start.17 = (bf16[2,2,8,112,128]{4,3,2,1,0:T(8,128)(2,1)}, bf16[2,2,8,112,128]{4,3,2,1,0:T(8,128)(2,1)S(1)}, u32[]{:S(2)}, u32[]{:S(2)}) collective-permute-start(bf16[2,2,8,112,128]{4,3,2,1,0:T(8,128)(2,1)} %collective-permute-done.15.rest_5_), channel_id=1, source_target_pairs={{0,96},{1,25},{2,98},{3,27},{4,100},{5,29},{6,102},{7,31},{8,104},... | collective-permute-start | bytes 2752520 | tf_op jit(solution)/shard_map/ppermute | solution.py:153
  99.1 3.2 %collective-permute-start.19 = (bf16[2,2,6,112,128]{4,3,2,1,0:T(8,128)(2,1)}, bf16[2,2,6,112,128]{4,3,2,1,0:T(8,128)(2,1)S(1)}, u32[]{:S(2)}, u32[]{:S(2)}) collective-permute-start(bf16[2,2,6,112,128]{4,3,2,1,0:T(8,128)(2,1)} %get-tuple-element.160), channel_id=1, source_target_pairs={{0,96},{1,25},{2,98},{3,27},{4,100},{5,29},{6,102},{7,31},{8,104},... | collective-permute-start | bytes 2064392 | tf_op jit(solution)/shard_map/ppermute | solution.py:153
  102.3 8.3 %collective-permute-done.16.rest_6_ = bf16[2,2,8,112,128]{4,3,2,1,0:T(8,128)(2,1)S(1)} collective-permute-done((bf16[2,2,8,112,128]{4,3,2,1,0:T(8,128)(2,1)}, bf16[2,2,8,112,128]{4,3,2,1,0:T(8,128)(2,1)S(1)}, u32[]{:S(2)}, u32[]{:S(2)}) %collective-permute-start.16) | collective-permute-done | bytes 917536 | tf_op jit(solution)/shard_map/ppermute | solution.py:153
  110.7 0.9 copy-done.16
  111.6 1.0 copy-done.17
  112.5 27.0 %shard_map.103 = (bf16[8,2,256,896]{3,2,1,0:T(8,128)(2,1)}, bf16[2,2,8,112,128]{4,3,2,1,0:T(8,128)(2,1)}, bf16[2,2,8,112,128]{4,3,2,1,0:T(8,128)(2,1)}, bf16[2,2...) custom-call(s32[16]{0:T(128)} %mul.13.rows_tbl, ...), custom_call_target="tpu_custom_call" | custom-call | flops 11274289152 | bytes 29360128 | tf_op jit(solution)/shard_map/pallas_call | solution.py:114
  139.6 1.1 copy-done.11
  140.9 2.4 %collective-permute-start.23 = (bf16[2,2,6,112,128]{4,3,2,1,0:T(8,128)(2,1)S(1)}, bf16[2,2,6,112,128]{4,3,2,1,0:T(8,128)(2,1)S(1)}, u32[]{:S(2)}, u32[]{:S(2)}) collective-permute-start(bf16[2,2,6,112,128]{4,3,2,1,0:T(8,128)(2,1)S(1)} %add_convert_fusion.2), channel_id=1, source_target_pairs={{0,96},{1,25},{2,98},{3,27},{4,100},{5,29},{6,102},{7,31},{8,104},... | collective-permute-start | bytes 2064392 | tf_op jit(solution)/shard_map/ppermute | solution.py:153
  143.2 3.2 %collective-permute-start.25 = (bf16[2,2,8,112,128]{4,3,2,1,0:T(8,128)(2,1)}, bf16[2,2,8,112,128]{4,3,2,1,0:T(8,128)(2,1)S(1)}, u32[]{:S(2)}, u32[]{:S(2)}) collective-permute-start(bf16[2,2,8,112,128]{4,3,2,1,0:T(8,128)(2,1)} %get-tuple-element.176), channel_id=1, source_target_pairs={{0,96},{1,25},{2,98},{3,27},{4,100},{5,29},{6,102},{7,31},{8,104},... | collective-permute-start | bytes 2752520 | tf_op jit(solution)/shard_map/ppermute | solution.py:153
  146.5 3.2 %collective-permute-start.27 = (bf16[2,2,8,112,128]{4,3,2,1,0:T(8,128)(2,1)}, bf16[2,2,8,112,128]{4,3,2,1,0:T(8,128)(2,1)S(1)}, u32[]{:S(2)}, u32[]{:S(2)}) collective-permute-start(bf16[2,2,8,112,128]{4,3,2,1,0:T(8,128)(2,1)} %get-tuple-element.178), channel_id=1, source_target_pairs={{0,96},{1,25},{2,98},{3,27},{4,100},{5,29},{6,102},{7,31},{8,104},... | collective-permute-start | bytes 2752520 | tf_op jit(solution)/shard_map/ppermute | solution.py:153
  149.9 1.9 collective-permute-done.23
  151.9 1.1 collective-permute-start.22
  153.0 22.3 %collective-permute-done.22 = bf16[2,2,6,112,128]{4,3,2,1,0:T(8,128)(2,1)S(1)} collective-permute-done((bf16[2,2,6,112,128]{4,3,2,1,0:T(8,128)(2,1)S(1)}, bf16[2,2,6,112,128]{4,3,2,1,0:T(8,128)(2,1)S(1)}, u32[]{:S(2)}, u32[]{:S(2)}) %collective-permute-start.22) | collective-permute-done | bytes 688160 | tf_op jit(solution)/shard_map/ppermute | solution.py:153
  175.9 2.1 collective-permute-start.31
  178.3 1.5 collective-permute-start.29
  179.8 2.2 %collective-permute-start.30 = (bf16[2,6,112,128]{3,2,1,0:T(8,128)(2,1)S(1)}, bf16[2,6,112,128]{3,2,1,0:T(8,128)(2,1)S(1)}, u32[]{:S(2)}, u32[]{:S(2)}) collective-permute-start(bf16[2,6,112,128]{3,2,1,0:T(8,128)(2,1)S(1)} %get-tuple-element.200), channel_id=1, source_target_pairs={{0,16},{1,65},{2,18},{3,67},{4,20},{5,69},{6,22},{7,71},{8,24},{9,... | collective-permute-start | bytes 1032200 | tf_op jit(solution)/shard_map/ppermute | solution.py:153
  182.9 10.3 %collective-permute-done.29 = bf16[2,6,112,128]{3,2,1,0:T(8,128)(2,1)S(1)} collective-permute-done((bf16[2,6,112,128]{3,2,1,0:T(8,128)(2,1)S(1)}, bf16[2,6,112,128]{3,2,1,0:T(8,128)(2,1)S(1)}, u32[]{:S(2)}, u32[]{:S(2)}) %collective-permute-start.29) | collective-permute-done | bytes 344096 | tf_op jit(solution)/shard_map/ppermute | solution.py:153
  193.2 2.6 %collective-permute-done.32 = bf16[2,2,8,112,128]{4,3,2,1,0:T(8,128)(2,1)S(1)} collective-permute-done((bf16[2,2,8,112,128]{4,3,2,1,0:T(8,128)(2,1)S(1)}, bf16[2,2,8,112,128]{4,3,2,1,0:T(8,128)(2,1)S(1)}, u32[]{:S(2)}, u32[]{:S(2)}) %collective-permute-start.32) | collective-permute-done | bytes 917536 | tf_op jit(solution)/shard_map/ppermute | solution.py:153
  196.0 2.4 %collective-permute-start.33 = (bf16[2,8,112,128]{3,2,1,0:T(8,128)(2,1)S(1)}, bf16[2,8,112,128]{3,2,1,0:T(8,128)(2,1)S(1)}, u32[]{:S(2)}, u32[]{:S(2)}) collective-permute-start(bf16[2,8,112,128]{3,2,1,0:T(8,128)(2,1)S(1)} %fusion.4), channel_id=1, source_target_pairs={{0,24},{1,97},{2,26},{3,99},{4,28},{5,101},{6,30},{7,103},{8,0},{9... | collective-permute-start | bytes 1376264 | tf_op jit(solution)/shard_map/ppermute | solution.py:153
  198.8 1.5 collective-permute-start.35
  200.5 8.8 %collective-permute-done.33 = bf16[2,8,112,128]{3,2,1,0:T(8,128)(2,1)S(1)} collective-permute-done((bf16[2,8,112,128]{3,2,1,0:T(8,128)(2,1)S(1)}, bf16[2,8,112,128]{3,2,1,0:T(8,128)(2,1)S(1)}, u32[]{:S(2)}, u32[]{:S(2)}) %collective-permute-start.33) | collective-permute-done | bytes 458784 | tf_op jit(solution)/shard_map/ppermute | solution.py:153
  209.3 4.1 %collective-permute-done.34 = bf16[2,8,112,128]{3,2,1,0:T(8,128)(2,1)S(1)} collective-permute-done((bf16[2,8,112,128]{3,2,1,0:T(8,128)(2,1)S(1)}, bf16[2,8,112,128]{3,2,1,0:T(8,128)(2,1)S(1)}, u32[]{:S(2)}, u32[]{:S(2)}) %collective-permute-start.34) | collective-permute-done | bytes 458784 | tf_op jit(solution)/shard_map/ppermute | solution.py:153
  213.8 0.8 pad_maximum_fusion.7
  215.4 2.1 slice_bitcast_fusion
  (102 shorter events, 7.3 us)
Async XLA Ops:
  7.2 59.8 %all-gather.3.cloned.1.call-start = ((), (), s32[]{:S(2)}) async-start(), calls=%async_computation.2 | async-start | bytes 8257536 | tf_op jit(solution)/shard_map/all_gather | solution.py:201
  11.1 204.2 %reduce-scatter.2.cloned.1.call-start = ((), (), s32[]{:S(2)}) async-start(), calls=%async_computation.1 | async-start | bytes 8257536 | tf_op jit(solution)/shard_map/reduce_scatter | solution.py:237
  11.3 8.5 %collective-permute-start = (bf16[2,6,112,128]{3,2,1,0:T(8,128)(2,1)S(1)}, bf16[2,6,112,128]{3,2,1,0:T(8,128)(2,1)S(1)}, u32[]{:S(2)}, u32[]{:S(2)}) collective-permute-start(bf16[2,6,112,128]{3,2,1,0:T(8,128)(2,1)S(1)} %pad_maximum_fusion.8), channel_id=1, source_target_pairs={{0,8},{1,33},{2,10},{3,35},{4,12},{5,37},{6,14},{7,39},{8,16},{9,4... | collective-permute-start | bytes 1032200 | tf_op jit(solution)/shard_map/ppermute | solution.py:153
  12.9 7.2 %collective-permute-start.1 = (bf16[2,6,112,128]{3,2,1,0:T(8,128)(2,1)S(1)}, bf16[2,6,112,128]{3,2,1,0:T(8,128)(2,1)S(1)}, u32[]{:S(2)}, u32[]{:S(2)}) collective-permute-start(bf16[2,6,112,128]{3,2,1,0:T(8,128)(2,1)S(1)} %pad_maximum_fusion.8), channel_id=1, source_target_pairs={{0,24},{1,97},{2,26},{3,99},{4,28},{5,101},{6,30},{7,103},{8,0},{9... | collective-permute-start | bytes 1032200 | tf_op jit(solution)/shard_map/ppermute | solution.py:153
  14.6 10.0 %collective-permute-start.2 = (bf16[2,6,112,128]{3,2,1,0:T(8,128)(2,1)S(1)}, bf16[2,6,112,128]{3,2,1,0:T(8,128)(2,1)S(1)}, u32[]{:S(2)}, u32[]{:S(2)}) collective-permute-start(bf16[2,6,112,128]{3,2,1,0:T(8,128)(2,1)S(1)} %pad_maximum_fusion.8), channel_id=1, source_target_pairs={{0,16},{1,65},{2,18},{3,67},{4,20},{5,69},{6,22},{7,71},{8,24},{9,... | collective-permute-start | bytes 1032200 | tf_op jit(solution)/shard_map/ppermute | solution.py:153
  16.5 34.9 %copy-start.14 = (s32[4]{0:T(128)S(1)}, s32[4]{0:T(128)}, u32[]{:S(2)}) copy-start(s32[4]{0:T(128)} %constant.63.clone) | copy-start | bytes 52
  24.6 45.9 %copy-start.6 = (bf16[2,2,6,112,128]{4,3,2,1,0:T(8,128)(2,1)}, bf16[2,2,6,112,128]{4,3,2,1,0:T(8,128)(2,1)S(1)}, u32[]{:S(2)}) copy-start(bf16[2,2,6,112,128]{4,3,2,1,0:T(8,128)(2,1)S(1)} %pad_maximum_fusion.3.rest_0_) | copy-start | bytes 2064388
  24.7 12.3 %collective-permute-start.3 = (bf16[2,2,6,112,128]{4,3,2,1,0:T(8,128)(2,1)S(1)}, bf16[2,2,6,112,128]{4,3,2,1,0:T(8,128)(2,1)}, u32[]{:S(2)}, u32[]{:S(2)}) collective-permute-start(bf16[2,2,6,112,128]{4,3,2,1,0:T(8,128)(2,1)S(1)} %pad_maximum_fusion.3.rest_0_), channel_id=1, source_target_pairs={{0,32},{1,9},{2,34},{3,11},{4,36},{5,13},{6,38},{7,15},{8,40},{9,1... | collective-permute-start | bytes 2064392 | tf_op jit(solution)/shard_map/ppermute | solution.py:153
  26.3 10.9 %collective-permute-start.5 = (bf16[2,2,6,112,128]{4,3,2,1,0:T(8,128)(2,1)S(1)}, bf16[2,2,6,112,128]{4,3,2,1,0:T(8,128)(2,1)S(1)}, u32[]{:S(2)}, u32[]{:S(2)}) collective-permute-start(bf16[2,2,6,112,128]{4,3,2,1,0:T(8,128)(2,1)S(1)} %pad_maximum_fusion.3.rest_0_), channel_id=1, source_target_pairs={{0,96},{1,25},{2,98},{3,27},{4,100},{5,29},{6,102},{7,31},{8,104},... | collective-permute-start | bytes 2064392 | tf_op jit(solution)/shard_map/ppermute | solution.py:153
  28.0 39.0 %copy-start.7 = (bf16[2,2,6,112,128]{4,3,2,1,0:T(8,128)(2,1)}, bf16[2,2,6,112,128]{4,3,2,1,0:T(8,128)(2,1)S(1)}, u32[]{:S(2)}) copy-start(bf16[2,2,6,112,128]{4,3,2,1,0:T(8,128)(2,1)S(1)} %pad_maximum_fusion.4.rest_1_) | copy-start | bytes 2064388
  28.0 16.2 %collective-permute-start.4 = (bf16[2,2,6,112,128]{4,3,2,1,0:T(8,128)(2,1)S(1)}, bf16[2,2,6,112,128]{4,3,2,1,0:T(8,128)(2,1)S(1)}, u32[]{:S(2)}, u32[]{:S(2)}) collective-permute-start(bf16[2,2,6,112,128]{4,3,2,1,0:T(8,128)(2,1)S(1)} %pad_maximum_fusion.4.rest_1_), channel_id=1, source_target_pairs={{0,32},{1,9},{2,34},{3,11},{4,36},{5,13},{6,38},{7,15},{8,40},{9,1... | collective-permute-start | bytes 2064392 | tf_op jit(solution)/shard_map/ppermute | solution.py:153
  28.5 16.2 %collective-permute-start.6 = (bf16[2,2,6,112,128]{4,3,2,1,0:T(8,128)(2,1)S(1)}, bf16[2,2,6,112,128]{4,3,2,1,0:T(8,128)(2,1)}, u32[]{:S(2)}, u32[]{:S(2)}) collective-permute-start(bf16[2,2,6,112,128]{4,3,2,1,0:T(8,128)(2,1)S(1)} %pad_maximum_fusion.4.rest_1_), channel_id=1, source_target_pairs={{0,96},{1,25},{2,98},{3,27},{4,100},{5,29},{6,102},{7,31},{8,104},... | collective-permute-start | bytes 2064392 | tf_op jit(solution)/shard_map/ppermute | solution.py:153
  37.2 13.0 %copy-start.18 = (bf16[2,2,6,112,128]{4,3,2,1,0:T(8,128)(2,1)}, bf16[2,2,6,112,128]{4,3,2,1,0:T(8,128)(2,1)S(1)}, u32[]{:S(2)}) copy-start(bf16[2,2,6,112,128]{4,3,2,1,0:T(8,128)(2,1)S(1)} %collective-permute-done.5.rest_4_) | copy-start | bytes 2064388
  44.7 22.3 %collective-permute-start.7 = (bf16[2,2,6,112,128]{4,3,2,1,0:T(8,128)(2,1)}, bf16[2,2,6,112,128]{4,3,2,1,0:T(8,128)(2,1)}, u32[]{:S(2)}, u32[]{:S(2)}) collective-permute-start(bf16[2,2,6,112,128]{4,3,2,1,0:T(8,128)(2,1)} %collective-permute-done.3.rest_2_), channel_id=1, source_target_pairs={{0,32},{1,9},{2,34},{3,11},{4,36},{5,13},{6,38},{7,15},{8,40},{9,1... | collective-permute-start | bytes 2064392 | tf_op jit(solution)/shard_map/ppermute | solution.py:153
  46.3 20.7 %collective-permute-start.8 = (bf16[2,2,6,112,128]{4,3,2,1,0:T(8,128)(2,1)}, bf16[2,2,6,112,128]{4,3,2,1,0:T(8,128)(2,1)}, u32[]{:S(2)}, u32[]{:S(2)}) collective-permute-start(bf16[2,2,6,112,128]{4,3,2,1,0:T(8,128)(2,1)} %collective-permute-done.6.rest_5_), channel_id=1, source_target_pairs={{0,96},{1,25},{2,98},{3,27},{4,100},{5,29},{6,102},{7,31},{8,104},... | collective-permute-start | bytes 2064392 | tf_op jit(solution)/shard_map/ppermute | solution.py:153
  48.0 15.3 %collective-permute-start.10 = (bf16[2,8,112,128]{3,2,1,0:T(8,128)(2,1)S(1)}, bf16[2,8,112,128]{3,2,1,0:T(8,128)(2,1)S(1)}, u32[]{:S(2)}, u32[]{:S(2)}) collective-permute-start(bf16[2,8,112,128]{3,2,1,0:T(8,128)(2,1)S(1)} %pad_maximum_fusion.5), channel_id=1, source_target_pairs={{0,24},{1,97},{2,26},{3,99},{4,28},{5,101},{6,30},{7,103},{8,0},{9... | collective-permute-start | bytes 1376264 | tf_op jit(solution)/shard_map/ppermute | solution.py:153
  50.2 13.0 %collective-permute-start.11 = (bf16[2,8,112,128]{3,2,1,0:T(8,128)(2,1)S(1)}, bf16[2,8,112,128]{3,2,1,0:T(8,128)(2,1)S(1)}, u32[]{:S(2)}, u32[]{:S(2)}) collective-permute-start(bf16[2,8,112,128]{3,2,1,0:T(8,128)(2,1)S(1)} %pad_maximum_fusion.5), channel_id=1, source_target_pairs={{0,16},{1,65},{2,18},{3,67},{4,20},{5,69},{6,22},{7,71},{8,24},{9,... | collective-permute-start | bytes 1376264 | tf_op jit(solution)/shard_map/ppermute | solution.py:153
  51.4 13.7 %collective-permute-start.9 = (bf16[2,8,112,128]{3,2,1,0:T(8,128)(2,1)S(1)}, bf16[2,8,112,128]{3,2,1,0:T(8,128)(2,1)S(1)}, u32[]{:S(2)}, u32[]{:S(2)}) collective-permute-start(bf16[2,8,112,128]{3,2,1,0:T(8,128)(2,1)S(1)} %pad_maximum_fusion.5), channel_id=1, source_target_pairs={{0,8},{1,33},{2,10},{3,35},{4,12},{5,37},{6,14},{7,39},{8,16},{9,4... | collective-permute-start | bytes 1376264 | tf_op jit(solution)/shard_map/ppermute | solution.py:153
  67.1 28.6 %copy-start.2 = (bf16[2,2,8,112,128]{4,3,2,1,0:T(8,128)(2,1)}, bf16[2,2,8,112,128]{4,3,2,1,0:T(8,128)(2,1)S(1)}, u32[]{:S(2)}) copy-start(bf16[2,2,8,112,128]{4,3,2,1,0:T(8,128)(2,1)S(1)} %pad_maximum_fusion.2.rest_1_) | copy-start | bytes 2752516
  67.1 28.6 %collective-permute-start.13 = (bf16[2,2,8,112,128]{4,3,2,1,0:T(8,128)(2,1)S(1)}, bf16[2,2,8,112,128]{4,3,2,1,0:T(8,128)(2,1)}, u32[]{:S(2)}, u32[]{:S(2)}) collective-permute-start(bf16[2,2,8,112,128]{4,3,2,1,0:T(8,128)(2,1)S(1)} %pad_maximum_fusion.2.rest_1_), channel_id=1, source_target_pairs={{0,32},{1,9},{2,34},{3,11},{4,36},{5,13},{6,38},{7,15},{8,40},{9,1... | collective-permute-start | bytes 2752520 | tf_op jit(solution)/shard_map/ppermute | solution.py:153
  67.2 28.5 %collective-permute-start.15 = (bf16[2,2,8,112,128]{4,3,2,1,0:T(8,128)(2,1)S(1)}, bf16[2,2,8,112,128]{4,3,2,1,0:T(8,128)(2,1)}, u32[]{:S(2)}, u32[]{:S(2)}) collective-permute-start(bf16[2,2,8,112,128]{4,3,2,1,0:T(8,128)(2,1)S(1)} %pad_maximum_fusion.2.rest_1_), channel_id=1, source_target_pairs={{0,96},{1,25},{2,98},{3,27},{4,100},{5,29},{6,102},{7,31},{8,104},... | collective-permute-start | bytes 2752520 | tf_op jit(solution)/shard_map/ppermute | solution.py:153
  70.5 25.2 %copy-start.3 = (bf16[2,2,8,112,128]{4,3,2,1,0:T(8,128)(2,1)}, bf16[2,2,8,112,128]{4,3,2,1,0:T(8,128)(2,1)S(1)}, u32[]{:S(2)}) copy-start(bf16[2,2,8,112,128]{4,3,2,1,0:T(8,128)(2,1)S(1)} %pad_maximum_fusion.1.rest_0_) | copy-start | bytes 2752516
  70.5 25.2 %collective-permute-start.12 = (bf16[2,2,8,112,128]{4,3,2,1,0:T(8,128)(2,1)S(1)}, bf16[2,2,8,112,128]{4,3,2,1,0:T(8,128)(2,1)}, u32[]{:S(2)}, u32[]{:S(2)}) collective-permute-start(bf16[2,2,8,112,128]{4,3,2,1,0:T(8,128)(2,1)S(1)} %pad_maximum_fusion.1.rest_0_), channel_id=1, source_target_pairs={{0,32},{1,9},{2,34},{3,11},{4,36},{5,13},{6,38},{7,15},{8,40},{9,1... | collective-permute-start | bytes 2752520 | tf_op jit(solution)/shard_map/ppermute | solution.py:153
  70.6 25.1 %collective-permute-start.14 = (bf16[2,2,8,112,128]{4,3,2,1,0:T(8,128)(2,1)S(1)}, bf16[2,2,8,112,128]{4,3,2,1,0:T(8,128)(2,1)S(1)}, u32[]{:S(2)}, u32[]{:S(2)}) collective-permute-start(bf16[2,2,8,112,128]{4,3,2,1,0:T(8,128)(2,1)S(1)} %pad_maximum_fusion.1.rest_0_), channel_id=1, source_target_pairs={{0,96},{1,25},{2,98},{3,27},{4,100},{5,29},{6,102},{7,31},{8,104},... | collective-permute-start | bytes 2752520 | tf_op jit(solution)/shard_map/ppermute | solution.py:153
  95.8 14.9 %collective-permute-start.16 = (bf16[2,2,8,112,128]{4,3,2,1,0:T(8,128)(2,1)}, bf16[2,2,8,112,128]{4,3,2,1,0:T(8,128)(2,1)S(1)}, u32[]{:S(2)}, u32[]{:S(2)}) collective-permute-start(bf16[2,2,8,112,128]{4,3,2,1,0:T(8,128)(2,1)} %collective-permute-done.12.rest_2_), channel_id=1, source_target_pairs={{0,32},{1,9},{2,34},{3,11},{4,36},{5,13},{6,38},{7,15},{8,40},{9,1... | collective-permute-start | bytes 2752520 | tf_op jit(solution)/shard_map/ppermute | solution.py:153
  96.7 14.0 %collective-permute-start.17 = (bf16[2,2,8,112,128]{4,3,2,1,0:T(8,128)(2,1)}, bf16[2,2,8,112,128]{4,3,2,1,0:T(8,128)(2,1)S(1)}, u32[]{:S(2)}, u32[]{:S(2)}) collective-permute-start(bf16[2,2,8,112,128]{4,3,2,1,0:T(8,128)(2,1)} %collective-permute-done.15.rest_5_), channel_id=1, source_target_pairs={{0,96},{1,25},{2,98},{3,27},{4,100},{5,29},{6,102},{7,31},{8,104},... | collective-permute-start | bytes 2752520 | tf_op jit(solution)/shard_map/ppermute | solution.py:153
  99.1 40.5 %collective-permute-start.18 = (bf16[2,2,6,112,128]{4,3,2,1,0:T(8,128)(2,1)}, bf16[2,2,6,112,128]{4,3,2,1,0:T(8,128)(2,1)S(1)}, u32[]{:S(2)}, u32[]{:S(2)}) collective-permute-start(bf16[2,2,6,112,128]{4,3,2,1,0:T(8,128)(2,1)} %get-tuple-element.159), channel_id=1, source_target_pairs={{0,32},{1,9},{2,34},{3,11},{4,36},{5,13},{6,38},{7,15},{8,40},{9,1... | collective-permute-start | bytes 2064392 | tf_op jit(solution)/shard_map/ppermute | solution.py:153
  99.1 40.5 %collective-permute-start.19 = (bf16[2,2,6,112,128]{4,3,2,1,0:T(8,128)(2,1)}, bf16[2,2,6,112,128]{4,3,2,1,0:T(8,128)(2,1)S(1)}, u32[]{:S(2)}, u32[]{:S(2)}) collective-permute-start(bf16[2,2,6,112,128]{4,3,2,1,0:T(8,128)(2,1)} %get-tuple-element.160), channel_id=1, source_target_pairs={{0,96},{1,25},{2,98},{3,27},{4,100},{5,29},{6,102},{7,31},{8,104},... | collective-permute-start | bytes 2064392 | tf_op jit(solution)/shard_map/ppermute | solution.py:153
  102.3 37.2 %collective-permute-start.20 = (bf16[2,2,6,112,128]{4,3,2,1,0:T(8,128)(2,1)}, bf16[2,2,6,112,128]{4,3,2,1,0:T(8,128)(2,1)S(1)}, u32[]{:S(2)}, u32[]{:S(2)}) collective-permute-start(bf16[2,2,6,112,128]{4,3,2,1,0:T(8,128)(2,1)} %get-tuple-element.158), channel_id=1, source_target_pairs={{0,32},{1,9},{2,34},{3,11},{4,36},{5,13},{6,38},{7,15},{8,40},{9,1... | collective-permute-start | bytes 2064392 | tf_op jit(solution)/shard_map/ppermute | solution.py:153
  110.6 28.9 %collective-permute-start.21 = (bf16[2,2,6,112,128]{4,3,2,1,0:T(8,128)(2,1)}, bf16[2,2,6,112,128]{4,3,2,1,0:T(8,128)(2,1)S(1)}, u32[]{:S(2)}, u32[]{:S(2)}) collective-permute-start(bf16[2,2,6,112,128]{4,3,2,1,0:T(8,128)(2,1)} %get-tuple-element.155), channel_id=1, source_target_pairs={{0,96},{1,25},{2,98},{3,27},{4,100},{5,29},{6,102},{7,31},{8,104},... | collective-permute-start | bytes 2064392 | tf_op jit(solution)/shard_map/ppermute | solution.py:153
  140.7 34.6 %copy-start.5 = (bf16[2,2,8,112,128]{4,3,2,1,0:T(8,128)(2,1)S(1)}, bf16[2,2,8,112,128]{4,3,2,1,0:T(8,128)(2,1)}, u32[]{:S(2)}) copy-start(bf16[2,2,8,112,128]{4,3,2,1,0:T(8,128)(2,1)} %get-tuple-element.186) | copy-start | bytes 2752516
  140.9 11.0 %collective-permute-start.23 = (bf16[2,2,6,112,128]{4,3,2,1,0:T(8,128)(2,1)S(1)}, bf16[2,2,6,112,128]{4,3,2,1,0:T(8,128)(2,1)S(1)}, u32[]{:S(2)}, u32[]{:S(2)}) collective-permute-start(bf16[2,2,6,112,128]{4,3,2,1,0:T(8,128)(2,1)S(1)} %add_convert_fusion.2), channel_id=1, source_target_pairs={{0,96},{1,25},{2,98},{3,27},{4,100},{5,29},{6,102},{7,31},{8,104},... | collective-permute-start | bytes 2064392 | tf_op jit(solution)/shard_map/ppermute | solution.py:153
  143.2 32.0 %collective-permute-start.24 = (bf16[2,2,8,112,128]{4,3,2,1,0:T(8,128)(2,1)}, bf16[2,2,8,112,128]{4,3,2,1,0:T(8,128)(2,1)S(1)}, u32[]{:S(2)}, u32[]{:S(2)}) collective-permute-start(bf16[2,2,8,112,128]{4,3,2,1,0:T(8,128)(2,1)} %get-tuple-element.175), channel_id=1, source_target_pairs={{0,32},{1,9},{2,34},{3,11},{4,36},{5,13},{6,38},{7,15},{8,40},{9,1... | collective-permute-start | bytes 2752520 | tf_op jit(solution)/shard_map/ppermute | solution.py:153
  143.2 32.0 %collective-permute-start.25 = (bf16[2,2,8,112,128]{4,3,2,1,0:T(8,128)(2,1)}, bf16[2,2,8,112,128]{4,3,2,1,0:T(8,128)(2,1)S(1)}, u32[]{:S(2)}, u32[]{:S(2)}) collective-permute-start(bf16[2,2,8,112,128]{4,3,2,1,0:T(8,128)(2,1)} %get-tuple-element.176), channel_id=1, source_target_pairs={{0,96},{1,25},{2,98},{3,27},{4,100},{5,29},{6,102},{7,31},{8,104},... | collective-permute-start | bytes 2752520 | tf_op jit(solution)/shard_map/ppermute | solution.py:153
  146.5 28.8 %collective-permute-start.26 = (bf16[2,2,8,112,128]{4,3,2,1,0:T(8,128)(2,1)}, bf16[2,2,8,112,128]{4,3,2,1,0:T(8,128)(2,1)S(1)}, u32[]{:S(2)}, u32[]{:S(2)}) collective-permute-start(bf16[2,2,8,112,128]{4,3,2,1,0:T(8,128)(2,1)} %get-tuple-element.177), channel_id=1, source_target_pairs={{0,32},{1,9},{2,34},{3,11},{4,36},{5,13},{6,38},{7,15},{8,40},{9,1... | collective-permute-start | bytes 2752520 | tf_op jit(solution)/shard_map/ppermute | solution.py:153
  146.5 28.8 %collective-permute-start.27 = (bf16[2,2,8,112,128]{4,3,2,1,0:T(8,128)(2,1)}, bf16[2,2,8,112,128]{4,3,2,1,0:T(8,128)(2,1)S(1)}, u32[]{:S(2)}, u32[]{:S(2)}) collective-permute-start(bf16[2,2,8,112,128]{4,3,2,1,0:T(8,128)(2,1)} %get-tuple-element.178), channel_id=1, source_target_pairs={{0,96},{1,25},{2,98},{3,27},{4,100},{5,29},{6,102},{7,31},{8,104},... | collective-permute-start | bytes 2752520 | tf_op jit(solution)/shard_map/ppermute | solution.py:153
  149.9 25.7 %copy-start.4 = (bf16[2,2,8,112,128]{4,3,2,1,0:T(8,128)(2,1)S(1)}, bf16[2,2,8,112,128]{4,3,2,1,0:T(8,128)(2,1)}, u32[]{:S(2)}) copy-start(bf16[2,2,8,112,128]{4,3,2,1,0:T(8,128)(2,1)} %get-tuple-element.184) | copy-start | bytes 2752516
  151.9 23.4 %collective-permute-start.22 = (bf16[2,2,6,112,128]{4,3,2,1,0:T(8,128)(2,1)S(1)}, bf16[2,2,6,112,128]{4,3,2,1,0:T(8,128)(2,1)S(1)}, u32[]{:S(2)}, u32[]{:S(2)}) collective-permute-start(bf16[2,2,6,112,128]{4,3,2,1,0:T(8,128)(2,1)S(1)} %add_convert_fusion.3), channel_id=1, source_target_pairs={{0,32},{1,9},{2,34},{3,11},{4,36},{5,13},{6,38},{7,15},{8,40},{9,1... | collective-permute-start | bytes 2064392 | tf_op jit(solution)/shard_map/ppermute | solution.py:153
  175.6 20.2 %collective-permute-start.32 = (bf16[2,2,8,112,128]{4,3,2,1,0:T(8,128)(2,1)S(1)}, bf16[2,2,8,112,128]{4,3,2,1,0:T(8,128)(2,1)S(1)}, u32[]{:S(2)}, u32[]{:S(2)}) collective-permute-start(bf16[2,2,8,112,128]{4,3,2,1,0:T(8,128)(2,1)S(1)} %add_convert_fusion), channel_id=1, source_target_pairs={{0,96},{1,25},{2,98},{3,27},{4,100},{5,29},{6,102},{7,31},{8,104},... | collective-permute-start | bytes 2752520 | tf_op jit(solution)/shard_map/ppermute | solution.py:153
  175.9 19.9 %collective-permute-start.31 = (bf16[2,2,8,112,128]{4,3,2,1,0:T(8,128)(2,1)S(1)}, bf16[2,2,8,112,128]{4,3,2,1,0:T(8,128)(2,1)S(1)}, u32[]{:S(2)}, u32[]{:S(2)}) collective-permute-start(bf16[2,2,8,112,128]{4,3,2,1,0:T(8,128)(2,1)S(1)} %add_convert_fusion.1), channel_id=1, source_target_pairs={{0,32},{1,9},{2,34},{3,11},{4,36},{5,13},{6,38},{7,15},{8,40},{9,1... | collective-permute-start | bytes 2752520 | tf_op jit(solution)/shard_map/ppermute | solution.py:153
  178.3 17.5 %copy-start = (bf16[2,2,8,112,128]{4,3,2,1,0:T(8,128)(2,1)S(1)}, bf16[2,2,8,112,128]{4,3,2,1,0:T(8,128)(2,1)}, u32[]{:S(2)}) copy-start(bf16[2,2,8,112,128]{4,3,2,1,0:T(8,128)(2,1)} %get-tuple-element.192) | copy-start | bytes 2752516
  178.3 14.9 %collective-permute-start.29 = (bf16[2,6,112,128]{3,2,1,0:T(8,128)(2,1)S(1)}, bf16[2,6,112,128]{3,2,1,0:T(8,128)(2,1)S(1)}, u32[]{:S(2)}, u32[]{:S(2)}) collective-permute-start(bf16[2,6,112,128]{3,2,1,0:T(8,128)(2,1)S(1)} %get-tuple-element.201), channel_id=1, source_target_pairs={{0,8},{1,33},{2,10},{3,35},{4,12},{5,37},{6,14},{7,39},{8,16},{9,4... | collective-permute-start | bytes 1032200 | tf_op jit(solution)/shard_map/ppermute | solution.py:153
  179.8 18.6 %copy-start.1 = (bf16[2,2,8,112,128]{4,3,2,1,0:T(8,128)(2,1)S(1)}, bf16[2,2,8,112,128]{4,3,2,1,0:T(8,128)(2,1)}, u32[]{:S(2)}) copy-start(bf16[2,2,8,112,128]{4,3,2,1,0:T(8,128)(2,1)} %get-tuple-element.195) | copy-start | bytes 2752516
  179.8 13.4 %collective-permute-start.30 = (bf16[2,6,112,128]{3,2,1,0:T(8,128)(2,1)S(1)}, bf16[2,6,112,128]{3,2,1,0:T(8,128)(2,1)S(1)}, u32[]{:S(2)}, u32[]{:S(2)}) collective-permute-start(bf16[2,6,112,128]{3,2,1,0:T(8,128)(2,1)S(1)} %get-tuple-element.200), channel_id=1, source_target_pairs={{0,16},{1,65},{2,18},{3,67},{4,20},{5,69},{6,22},{7,71},{8,24},{9,... | collective-permute-start | bytes 1032200 | tf_op jit(solution)/shard_map/ppermute | solution.py:153
  182.3 10.9 %collective-permute-start.28 = (bf16[2,6,112,128]{3,2,1,0:T(8,128)(2,1)S(1)}, bf16[2,6,112,128]{3,2,1,0:T(8,128)(2,1)S(1)}, u32[]{:S(2)}, u32[]{:S(2)}) collective-permute-start(bf16[2,6,112,128]{3,2,1,0:T(8,128)(2,1)S(1)} %get-tuple-element.202), channel_id=1, source_target_pairs={{0,24},{1,97},{2,26},{3,99},{4,28},{5,101},{6,30},{7,103},{8,0},{9... | collective-permute-start | bytes 1032200 | tf_op jit(solution)/shard_map/ppermute | solution.py:153
  196.0 13.3 %collective-permute-start.33 = (bf16[2,8,112,128]{3,2,1,0:T(8,128)(2,1)S(1)}, bf16[2,8,112,128]{3,2,1,0:T(8,128)(2,1)S(1)}, u32[]{:S(2)}, u32[]{:S(2)}) collective-permute-start(bf16[2,8,112,128]{3,2,1,0:T(8,128)(2,1)S(1)} %fusion.4), channel_id=1, source_target_pairs={{0,24},{1,97},{2,26},{3,99},{4,28},{5,101},{6,30},{7,103},{8,0},{9... | collective-permute-start | bytes 1376264 | tf_op jit(solution)/shard_map/ppermute | solution.py:153
  198.7 14.7 %collective-permute-start.34 = (bf16[2,8,112,128]{3,2,1,0:T(8,128)(2,1)S(1)}, bf16[2,8,112,128]{3,2,1,0:T(8,128)(2,1)S(1)}, u32[]{:S(2)}, u32[]{:S(2)}) collective-permute-start(bf16[2,8,112,128]{3,2,1,0:T(8,128)(2,1)S(1)} %get-tuple-element.198), channel_id=1, source_target_pairs={{0,8},{1,33},{2,10},{3,35},{4,12},{5,37},{6,14},{7,39},{8,16},{9,4... | collective-permute-start | bytes 1376264 | tf_op jit(solution)/shard_map/ppermute | solution.py:153
  198.8 14.6 %collective-permute-start.35 = (bf16[2,8,112,128]{3,2,1,0:T(8,128)(2,1)S(1)}, bf16[2,8,112,128]{3,2,1,0:T(8,128)(2,1)S(1)}, u32[]{:S(2)}, u32[]{:S(2)}) collective-permute-start(bf16[2,8,112,128]{3,2,1,0:T(8,128)(2,1)S(1)} %get-tuple-element.199), channel_id=1, source_target_pairs={{0,16},{1,65},{2,18},{3,67},{4,20},{5,69},{6,22},{7,71},{8,24},{9,... | collective-permute-start | bytes 1376264 | tf_op jit(solution)/shard_map/ppermute | solution.py:153
  (10 other events, 26.5 us)
Sparse Core Ops, SparseCore 0:
  11.3 47.9 all-gather.2
  139.7 48.3 reduce-scatter.1

commit v3 on v2

--- a/solution.py
+++ b/solution.py
@@ -36,29 +36,44 @@
     return slice(k * BLK, (k + 1) * BLK)
 
 
-def pieces(rows_tbl, halves):
-    for n, ref in enumerate(halves):
-        for s in range(2):
-            yield pl.ds(pl.multiple_of(rows_tbl[n * 2 + s], 16), ref.shape[3]), ref, s
-
-
-def layer_kernel(base, has_prev, rows_tbl, upk, dnk, acts, *rest):
+WHOLE = [[(g, s) for s in range(4)] for g in range(4)]
+GATHERED = [g[n:n + 2] for g in WHOLE for n in (0, 2)]
+SENT = [WHOLE[0], WHOLE[1][2:], WHOLE[2][:2], WHOLE[3][:2] + WHOLE[2][2:], WHOLE[1][:2] + WHOLE[3][2:]]
+
+
+def pieces(rows_tbl, lists, refs):
+    for ref, entries in zip(refs, lists):
+        for n, (g, s) in enumerate(entries):
+            yield pl.ds(pl.multiple_of(rows_tbl[g * 4 + s], 16), ref.shape[3]), ref, n
+
+
+def layer_kernel(base, has_prev, rows_tbl, upk, dnk, acts_hbm, *rest):
     w_in, rest = rest[:8], rest[8:]
     prev, rest = rest[:has_prev], rest[has_prev:]
-    sums, w_out = rest[0], rest[1:9]
-    tokg, cotg, upw, dnw, dnr, uterm, dterm, out_acc, in_acc = rest[9:]
+    sums_hbm, w_out = rest[0], rest[1:6]
+    (tokg, cotg, upw, dnw, dnr, uterm, dterm, out_acc, in_acc,
+     acts, sums, acts_sem, prev_sem, sums_sem) = rest[6:]
     step = pl.program_id(0)
     per = acts.shape[2]
     many = tokg.shape[0]
+    acts_copy = pltpu.make_async_copy(acts_hbm, acts, acts_sem)
 
     @pl.when(step == 0)
     def _():
-        out_acc[...] = jnp.zeros_like(out_acc)
-        in_acc[...] = jnp.zeros_like(in_acc)
+        acts_copy.start()
+        if has_prev:
+            pltpu.make_async_copy(prev[0], sums, prev_sem).start()
+        def clear(f, carry):
+            out_acc[f] = jnp.zeros(out_acc.shape[1:], F32)
+            in_acc[f] = jnp.zeros(in_acc.shape[1:], F32)
+            return carry
+
+        lax.fori_loop(0, NFB, clear, 0)
+        acts_copy.wait()
 
     for b in range(many):
         j = base + step * many + b
-        for at, ref, s in pieces(rows_tbl, w_in):
+        for at, ref, s in pieces(rows_tbl, GATHERED, w_in):
             upw[b, at, :] = ref[s, 0, b]
             dnr[b, at, :] = ref[s, 1, b]
         for k in range(KEEP):
@@ -87,38 +102,52 @@
                 grad_pre[b], upw[b, cols(k), :], NT, preferred_element_type=F32
             )
     for b in range(many):
-        for at, ref, s in pieces(rows_tbl, w_out):
+        for at, ref, s in pieces(rows_tbl, SENT, w_out):
             ref[s, 0, b] = uterm[b, at, :]
             ref[s, 1, b] = dterm[b, at, :]
 
     @pl.when(step == pl.num_programs(0) - 1)
     def _():
-        for s in range(sums.shape[0]):
+        if has_prev:
+            pltpu.make_async_copy(prev[0], sums, prev_sem).wait()
+
+        def copy_back(s):
+            return pltpu.make_async_copy(sums.at[s], sums_hbm.at[s], sums_sem.at[s])
+
+        def finish(s, carry):
             for which, acc in enumerate((out_acc, in_acc)):
                 for i in range(per):
                     total = acc[s * per + i]
                     if has_prev:
-                        total = total + prev[0][s, which, :, cols(i)].astype(F32)
+                        total = total + sums[s, which, :, cols(i)].astype(F32)
                     sums[s, which, :, cols(i)] = total.astype(BF16)
-
-
-def layer_part(base, rows_tbl, upk, dnk, acts, group, prev):
-    local, part = group[0].shape[2:4]
+            copy_back(s).start()
+            return carry
+
+        lax.fori_loop(0, sums.shape[0], finish, 0)
+        for s in range(sums.shape[0]):
+            copy_back(s).wait()
+
+
+def layer_part(base, first, local, rows_tbl, upk, dnk, acts, group, prev):
+    part = group[0].shape[3]
     shards, _, per, tokens, _ = acts.shape
     many = MANY
-    piece = pl.BlockSpec((2, 2, many, part, BLK), lambda j, *_: (0, 0, j, 0, 0))
+    skip = first // many
+
+    def piece(entries, offset):
+        return pl.BlockSpec((len(entries), 2, many, part, BLK), lambda j, *_: (0, 0, j + offset, 0, 0))
+
+    anywhere = pl.BlockSpec(memory_space=pl.ANY)
     sums = jax.ShapeDtypeStruct((shards, 2, tokens, per * BLK), BF16)
-    whole = pl.BlockSpec(sums.shape, lambda j, *_: (0,) * 4, pipeline_mode=pl.Buffered(1))
-    term = jax.ShapeDtypeStruct(group[0].shape, BF16)
     extra = [] if prev is None else [prev]
     outs = pl.pallas_call(
-        functools.partial(layer_kernel, base, len(extra)),
+        functools.partial(layer_kernel, base + first, len(extra)),
         grid_spec=pltpu.PrefetchScalarGridSpec(
             num_scalar_prefetch=3,
             grid=(local // many,),
-            in_specs=[pl.BlockSpec(acts.shape, lambda j, *_: (0,) * 5, pipeline_mode=pl.Buffered(1))]
-            + [piece] * 8 + [whole] * len(extra),
-            out_specs=[whole] + [piece] * 8,
+            in_specs=[anywhere] + [piece(e, skip) for e in GATHERED] + [anywhere] * len(extra),
+            out_specs=[anywhere] + [piece(e, 0) for e in SENT],
             scratch_shapes=[
                 pltpu.VMEM((many, tokens, ROWS), BF16),
                 pltpu.VMEM((many, tokens, ROWS), BF16),
@@ -129,9 +158,15 @@
                 pltpu.VMEM((many, ROWS, BLK), BF16),
                 pltpu.VMEM((NFB, tokens, BLK), F32),
                 pltpu.VMEM((NFB, tokens, BLK), F32),
+                pltpu.VMEM(acts.shape, BF16),
+                pltpu.VMEM(sums.shape, BF16),
+                pltpu.SemaphoreType.DMA,
+                pltpu.SemaphoreType.DMA,
+                pltpu.SemaphoreType.DMA((shards,)),
             ],
         ),
-        out_shape=[sums] + [term] * 8,
+        out_shape=[sums] + [
+            jax.ShapeDtypeStruct((len(e), 2, local, part, BLK), BF16) for e in SENT],
         compiler_params=pltpu.CompilerParams(vmem_limit_bytes=VMEM_LIMIT),
         cost_estimate=pl.CostEstimate(
             flops=local * 24 * tokens * ROWS * BLK,
@@ -140,6 +175,20 @@
         ),
     )(rows_tbl, upk, dnk, acts, *group, *extra)
     return outs[0], outs[1:]
+
+
+def pack_kernel(tokens, cotangent, out):
+    for which, ref in enumerate((tokens, cotangent)):
+        for i in range(out.shape[1]):
+            out[which, i] = ref[:, cols(i)]
+
+
+def pack(tokens, cotangent):
+    rows, width = tokens.shape
+    return pl.pallas_call(
+        pack_kernel,
+        out_shape=jax.ShapeDtypeStruct((2, width // BLK, rows, BLK), BF16),
+    )(tokens, cotangent)
 
 
 def shift(value, leg, by):
@@ -171,18 +220,16 @@
 
 
 def send_far(terms):
-    _, _, to_minus_a, _, _, to_plus_b, far_a, far_b = terms
-    return shift(far_a, 1, 1), shift(far_b, 1, -1), shift(to_plus_b, 1, 1), shift(to_minus_a, 1, -1)
+    return shift(terms[3], 1, 1), shift(terms[4], 1, -1)
 
 
 def send_near(terms, got):
-    to_minus_b, to_plus_a = terms[3], terms[4]
-    return shift(add(to_plus_a, got[0]), 1, 1), shift(add(to_minus_b, got[1]), 1, -1)
+    return shift(add(terms[2], got[0][:2]), 1, 1), shift(add(terms[1], got[1][2:]), 1, -1)
 
 
 def send_slots(terms, got, got_near):
-    a, b = (terms[0], got_near[0], got[3]), (terms[1], got[2], got_near[1])
-    slot = [add(*(p[s] for p in half)) for half in (a, b) for s in range(2)]
+    slot = [add(terms[0][s], got_near[0][s], got[1][s]) for s in (0, 1)]
+    slot += [add(terms[0][s], got_near[1][s - 2], got[0][s]) for s in (2, 3)]
     return slot[0], shift(slot[1], 0, -1), shift(slot[2], 0, 1), shift(slot[3], 0, 2)
 
 
@@ -192,13 +239,8 @@
 
 def body(tokens, cotangent, up_weight, down_weight, up_kept, down_kept):
     count, part = up_weight.shape[:2]
-    rows = tokens.shape[0]
-    shards = D // tokens.shape[1]
-
-    def blocks(a):
-        return a.reshape(rows, -1, BLK).transpose(1, 0, 2)
-
-    acts = lax.all_gather(jnp.stack([blocks(tokens), blocks(cotangent)]), "tensor", axis=0)
+
+    acts = lax.all_gather(pack(tokens, cotangent), "tensor", axis=0)
 
     me = lax.axis_index("dp")
     y, x = me // SIDE, me % SIDE
@@ -211,6 +253,7 @@
     ).reshape(-1)
 
     first = 6
+    mid = (count - first) // 2
     w = tuple(
         jnp.stack([up_weight[s], down_weight[s]]) for s in (slice(0, first), slice(first, count))
     )
@@ -225,24 +268,29 @@
     g0, n1, acts = tie(g0, n1, acts)
 
     c1 = cross(w[1], n1)
-    sums, t0 = layer_part(0, rows_tbl, up_kept, down_kept, acts, g0, None)
+    sums, t0 = layer_part(0, 0, first, rows_tbl, up_kept, down_kept, acts, g0, None)
     c1, sums, t0, acts = tie(c1, sums, t0, acts)
 
     g1, f0 = c1 + onward(c1), send_far(t0)
     g1, sums, acts = tie(g1, sums, acts)
 
-    sums, t1 = layer_part(first, rows_tbl, up_kept, down_kept, acts, g1, sums)
-    sums, t0, t1, f0 = tie(sums, t0, t1, f0)
+    sums, t1 = layer_part(first, 0, mid, rows_tbl, up_kept, down_kept, acts, g1, sums)
+    sums, t0, t1, f0, g1, acts = tie(sums, t0, t1, f0, g1, acts)
+
+    s0, f1 = send_near(t0, f0), send_far(t1)
+    sums, t2 = layer_part(first, mid, mid, rows_tbl, up_kept, down_kept, acts, g1, sums)
+    sums, t0, t1, t2, f0, f1, s0 = tie(sums, t0, t1, t2, f0, f1, s0)
 
     summed = lax.psum_scatter(sums, "tensor", scatter_dimension=0)
-    s0, f1 = send_near(t0, f0), send_far(t1)
-    s0, f1 = tie(s0, f1)
-
-    l0, s1 = send_slots(t0, f0, s0), send_near(t1, f1)
-    l0, s1 = tie(l0, s1)
-
-    l1 = send_slots(t1, f1, s1)
-    ups, dns = zip(*(add(*part) for part in (l0, l1)))
+    s1, f2, l0 = send_near(t1, f1), send_far(t2), send_slots(t0, f0, s0)
+    s1, f2, l0 = tie(s1, f2, l0)
+
+    s2, l1 = send_near(t2, f2), send_slots(t1, f1, s1)
+    s2, l1 = tie(s2, l1)
+
+    l2 = send_slots(t2, f2, s2)
+    summed, l2 = tie((summed[0], summed[1]), l2)
+    ups, dns = zip(*(add(*part) for part in (l0, l1, l2)))
     return summed[0], summed[1], jnp.concatenate(ups), jnp.concatenate(dns)
 
 

time: 225 us -> 221 us (0.982)
  waiting for transfers between devices: 95.3 us -> 75.9 us
  Pallas kernels: 48.1 us -> 57.9 us
  other arithmetic: 4.62 us -> 10.4 us
  local copies, waits for them, and re-layouts: 10.5 us -> 5.73 us
  starting transfers between devices: 51.3 us -> 55.9 us
    ppermute x36 -> x39, waiting for transfers between devices: 95.2 us -> 75.8 us  [shift(): return lax.ppermute(value, ('dp', 'tensor'), pairs)]
    pallas_call x2 -> x4, Pallas kernels: 48.1 us -> 57.9 us  [the longest x3 55.5 us: layer_part(): pl.pallas_call(functools.partial(layer_kernel, base + first, len(extra)),...]
    convert_element_type x10 -> x12, other arithmetic: 2.49 us -> 7.34 us  [add(): return sum((t.astype(F32) for t in terms)).astype(BF16)]
    ppermute x36 -> x39, starting transfers between devices: 51.3 us -> 55.8 us  [shift(): return lax.ppermute(value, ('dp', 'tensor'), pairs)]
    unnamed x42 -> x56, local copies, waits for them, and re-layouts: 6.31 us -> 2.86 us
  transfers between devices with their start and end apart: 38 -> 41, of which waited for: 17 -> 22; matrix products, arithmetic and copies ran while one was open for 2% -> 5% of each run, Pallas kernels for 21% -> 25%
where the time goes in v3:
time: 221 us; the launch traced here: 220 us
  waiting for transfers between devices  75.9 us (34%)
  Pallas kernels  57.9 us (26%)
  starting transfers between devices  55.9 us (25%)
  between operations  14.5 us (7%)
  other arithmetic  10.4 us (5%)
  local copies, waits for them, and re-layouts  5.73 us (3%)
    ppermute x39, waiting for transfers between devices, shift(): return lax.ppermute(value, ('dp', 'tensor'), pairs)  75.8 us
    ppermute x39, starting transfers between devices, shift(): return lax.ppermute(value, ('dp', 'tensor'), pairs)  55.8 us
    pallas_call x3, Pallas kernels, layer_part(): pl.pallas_call(functools.partial(layer_kernel, base + first, len(extra)),...  55.5 us
    convert_element_type x12, other arithmetic, add(): return sum((t.astype(F32) for t in terms)).astype(BF16)  7.34 us
  transfers between devices with their start and end apart: 41, of which 22 were waited for; matrix products, arithmetic and copies ran while one was open for 5% of the time, Pallas kernels for 25%

profile of v3, /device:TPU:0, one launch (start us, length us, event | category | flops | bytes accessed | tf_op | source)
XLA Modules:
  0.0 220.4 jit_solution(4289944520822065102)
XLA Ops:
  7.2 2.4 %shard_map.102 = bf16[2,7,256,128]{3,2,1,0:T(8,128)(2,1)} custom-call(bf16[256,896]{1,0:T(8,128)(2,1)} %tokens.1, bf16[256,896]{1,0:T(8,128)(2,1)} %cotangent.1), custom_call_target="tpu_custom_call" | custom-call | tf_op jit(solution)/shard_map/pallas_call | solution.py:188
  9.8 3.2 %collective-permute-start.2 = (bf16[2,6,112,128]{3,2,1,0:T(8,128)(2,1)S(1)}, bf16[2,6,112,128]{3,2,1,0:T(8,128)(2,1)S(1)}, u32[]{:S(2)}, u32[]{:S(2)}) collective-permute-start(bf16[2,6,112,128]{3,2,1,0:T(8,128)(2,1)S(1)} %pad_maximum_fusion.7), channel_id=1, source_target_pairs={{0,16},{1,65},{2,18},{3,67},{4,20},{5,69},{6,22},{7,71},{8,24},{9,... | collective-permute-start | bytes 1032200 | tf_op jit(solution)/shard_map/ppermute | solution.py:202
  13.0 1.1 collective-permute-start.1
  15.1 3.5 %collective-permute-done.2 = bf16[2,6,112,128]{3,2,1,0:T(8,128)(2,1)S(1)} collective-permute-done((bf16[2,6,112,128]{3,2,1,0:T(8,128)(2,1)S(1)}, bf16[2,6,112,128]{3,2,1,0:T(8,128)(2,1)S(1)}, u32[]{:S(2)}, u32[]{:S(2)}) %collective-permute-start.2) | collective-permute-done | bytes 344096 | tf_op jit(solution)/shard_map/ppermute | solution.py:202
  18.6 3.9 %collective-permute-done.1 = bf16[2,6,112,128]{3,2,1,0:T(8,128)(2,1)S(1)} collective-permute-done((bf16[2,6,112,128]{3,2,1,0:T(8,128)(2,1)S(1)}, bf16[2,6,112,128]{3,2,1,0:T(8,128)(2,1)S(1)}, u32[]{:S(2)}, u32[]{:S(2)}) %collective-permute-start.1) | collective-permute-done | bytes 344096 | tf_op jit(solution)/shard_map/ppermute | solution.py:202
  22.7 3.1 %collective-permute-start.5 = (bf16[2,2,6,112,128]{4,3,2,1,0:T(8,128)(2,1)S(1)}, bf16[2,2,6,112,128]{4,3,2,1,0:T(8,128)(2,1)S(1)}, u32[]{:S(2)}, u32[]{:S(2)}) collective-permute-start(bf16[2,2,6,112,128]{4,3,2,1,0:T(8,128)(2,1)S(1)} %pad_maximum_fusion.2.rest_0_), channel_id=1, source_target_pairs={{0,96},{1,25},{2,98},{3,27},{4,100},{5,29},{6,102},{7,31},{8,104},... | collective-permute-start | bytes 2064392 | tf_op jit(solution)/shard_map/ppermute | solution.py:202
  25.8 3.3 %collective-permute-start.6 = (bf16[2,2,6,112,128]{4,3,2,1,0:T(8,128)(2,1)S(1)}, bf16[2,2,6,112,128]{4,3,2,1,0:T(8,128)(2,1)}, u32[]{:S(2)}, u32[]{:S(2)}) collective-permute-start(bf16[2,2,6,112,128]{4,3,2,1,0:T(8,128)(2,1)S(1)} %pad_maximum_fusion.3.rest_1_), channel_id=1, source_target_pairs={{0,96},{1,25},{2,98},{3,27},{4,100},{5,29},{6,102},{7,31},{8,104},... | collective-permute-start | bytes 2064392 | tf_op jit(solution)/shard_map/ppermute | solution.py:202
  29.1 5.1 %collective-permute-done.5.rest_4_ = bf16[2,2,6,112,128]{4,3,2,1,0:T(8,128)(2,1)S(1)} collective-permute-done((bf16[2,2,6,112,128]{4,3,2,1,0:T(8,128)(2,1)S(1)}, bf16[2,2,6,112,128]{4,3,2,1,0:T(8,128)(2,1)S(1)}, u32[]{:S(2)}, u32[]{:S(2)}) %collective-permute-start.5) | collective-permute-done | bytes 688160 | tf_op jit(solution)/shard_map/ppermute | solution.py:202
  34.2 3.7 %collective-permute-done.3.rest_2_ = bf16[2,2,6,112,128]{4,3,2,1,0:T(8,128)(2,1)S(1)} collective-permute-done((bf16[2,2,6,112,128]{4,3,2,1,0:T(8,128)(2,1)S(1)}, bf16[2,2,6,112,128]{4,3,2,1,0:T(8,128)(2,1)S(1)}, u32[]{:S(2)}, u32[]{:S(2)}) %collective-permute-start.3) | collective-permute-done | bytes 688160 | tf_op jit(solution)/shard_map/ppermute | solution.py:202
  37.9 3.7 %collective-permute-done.6.rest_5_ = bf16[2,2,6,112,128]{4,3,2,1,0:T(8,128)(2,1)} collective-permute-done((bf16[2,2,6,112,128]{4,3,2,1,0:T(8,128)(2,1)S(1)}, bf16[2,2,6,112,128]{4,3,2,1,0:T(8,128)(2,1)}, u32[]{:S(2)}, u32[]{:S(2)}) %collective-permute-start.6) | collective-permute-done | bytes 688160 | tf_op jit(solution)/shard_map/ppermute | solution.py:202
  41.6 3.7 %collective-permute-done.4.rest_3_ = bf16[2,2,6,112,128]{4,3,2,1,0:T(8,128)(2,1)S(1)} collective-permute-done((bf16[2,2,6,112,128]{4,3,2,1,0:T(8,128)(2,1)S(1)}, bf16[2,2,6,112,128]{4,3,2,1,0:T(8,128)(2,1)S(1)}, u32[]{:S(2)}, u32[]{:S(2)}) %collective-permute-start.4) | collective-permute-done | bytes 688160 | tf_op jit(solution)/shard_map/ppermute | solution.py:202
  45.3 3.2 %collective-permute-start.8 = (bf16[2,2,6,112,128]{4,3,2,1,0:T(8,128)(2,1)}, bf16[2,2,6,112,128]{4,3,2,1,0:T(8,128)(2,1)}, u32[]{:S(2)}, u32[]{:S(2)}) collective-permute-start(bf16[2,2,6,112,128]{4,3,2,1,0:T(8,128)(2,1)} %collective-permute-done.6.rest_5_), channel_id=1, source_target_pairs={{0,96},{1,25},{2,98},{3,27},{4,100},{5,29},{6,102},{7,31},{8,104},... | collective-permute-start | bytes 2064392 | tf_op jit(solution)/shard_map/ppermute | solution.py:202
  48.5 2.8 %collective-permute-start.11 = (bf16[2,8,112,128]{3,2,1,0:T(8,128)(2,1)S(1)}, bf16[2,8,112,128]{3,2,1,0:T(8,128)(2,1)S(1)}, u32[]{:S(2)}, u32[]{:S(2)}) collective-permute-start(bf16[2,8,112,128]{3,2,1,0:T(8,128)(2,1)S(1)} %pad_maximum_fusion.4), channel_id=1, source_target_pairs={{0,16},{1,65},{2,18},{3,67},{4,20},{5,69},{6,22},{7,71},{8,24},{9,... | collective-permute-start | bytes 1376264 | tf_op jit(solution)/shard_map/ppermute | solution.py:202
  51.4 1.2 collective-permute-start.10
  53.4 5.2 %collective-permute-done.11 = bf16[2,8,112,128]{3,2,1,0:T(8,128)(2,1)S(1)} collective-permute-done((bf16[2,8,112,128]{3,2,1,0:T(8,128)(2,1)S(1)}, bf16[2,8,112,128]{3,2,1,0:T(8,128)(2,1)S(1)}, u32[]{:S(2)}, u32[]{:S(2)}) %collective-permute-start.11) | collective-permute-done | bytes 458784 | tf_op jit(solution)/shard_map/ppermute | solution.py:202
  58.6 5.1 %collective-permute-done.10 = bf16[2,8,112,128]{3,2,1,0:T(8,128)(2,1)S(1)} collective-permute-done((bf16[2,8,112,128]{3,2,1,0:T(8,128)(2,1)S(1)}, bf16[2,8,112,128]{3,2,1,0:T(8,128)(2,1)S(1)}, u32[]{:S(2)}, u32[]{:S(2)}) %collective-permute-start.10) | collective-permute-done | bytes 458784 | tf_op jit(solution)/shard_map/ppermute | solution.py:202
  64.2 3.2 %collective-permute-done.7.rest_6_ = bf16[2,2,6,112,128]{4,3,2,1,0:T(8,128)(2,1)} collective-permute-done((bf16[2,2,6,112,128]{4,3,2,1,0:T(8,128)(2,1)S(1)}, bf16[2,2,6,112,128]{4,3,2,1,0:T(8,128)(2,1)}, u32[]{:S(2)}, u32[]{:S(2)}) %collective-permute-start.7) | collective-permute-done | bytes 688160 | tf_op jit(solution)/shard_map/ppermute | solution.py:202
  67.5 3.0 %collective-permute-start.15 = (bf16[2,2,8,112,128]{4,3,2,1,0:T(8,128)(2,1)S(1)}, bf16[2,2,8,112,128]{4,3,2,1,0:T(8,128)(2,1)S(1)}, u32[]{:S(2)}, u32[]{:S(2)}) collective-permute-start(bf16[2,2,8,112,128]{4,3,2,1,0:T(8,128)(2,1)S(1)} %pad_maximum_fusion.1.rest_1_), channel_id=1, source_target_pairs={{0,96},{1,25},{2,98},{3,27},{4,100},{5,29},{6,102},{7,31},{8,104},... | collective-permute-start | bytes 2752520 | tf_op jit(solution)/shard_map/ppermute | solution.py:202
  71.6 3.3 %collective-permute-start.14 = (bf16[2,2,8,112,128]{4,3,2,1,0:T(8,128)(2,1)S(1)}, bf16[2,2,8,112,128]{4,3,2,1,0:T(8,128)(2,1)}, u32[]{:S(2)}, u32[]{:S(2)}) collective-permute-start(bf16[2,2,8,112,128]{4,3,2,1,0:T(8,128)(2,1)S(1)} %pad_maximum_fusion.rest_0_), channel_id=1, source_target_pairs={{0,96},{1,25},{2,98},{3,27},{4,100},{5,29},{6,102},{7,31},{8,104},... | collective-permute-start | bytes 2752520 | tf_op jit(solution)/shard_map/ppermute | solution.py:202
  75.6 20.9 %shard_map.103 = (bf16[8,2,256,896]{3,2,1,0:T(8,128)(2,1)}, bf16[4,2,6,112,128]{4,3,2,1,0:T(8,128)(2,1)}, bf16[2,2,6,112,128]{4,3,2,1,0:T(8,128)(2,1)}, bf16[2,2...) custom-call(s32[16]{0:T(128)} %mul.13.rows_tbl, ...), custom_call_target="tpu_custom_call" | custom-call | flops 8455716864 | bytes 25690112 | tf_op jit(solution)/shard_map/pallas_call | solution.py:144
  96.7 3.3 %collective-permute-start.17 = (bf16[2,2,8,112,128]{4,3,2,1,0:T(8,128)(2,1)S(1)}, bf16[2,2,8,112,128]{4,3,2,1,0:T(8,128)(2,1)S(1)}, u32[]{:S(2)}, u32[]{:S(2)}) collective-permute-start(bf16[2,2,8,112,128]{4,3,2,1,0:T(8,128)(2,1)S(1)} %collective-permute-done.15.rest_5_), channel_id=1, source_target_pairs={{0,96},{1,25},{2,98},{3,27},{4,100},{5,29},{6,102},{7,31},{8,104},... | collective-permute-start | bytes 2752520 | tf_op jit(solution)/shard_map/ppermute | solution.py:202
  100.0 3.2 %collective-permute-start.19 = (bf16[4,2,6,112,128]{4,3,2,1,0:T(8,128)(2,1)}, bf16[4,2,6,112,128]{4,3,2,1,0:T(8,128)(2,1)S(1)}, u32[]{:S(2)}, u32[]{:S(2)}) collective-permute-start(bf16[4,2,6,112,128]{4,3,2,1,0:T(8,128)(2,1)} %get-tuple-element.178), channel_id=1, source_target_pairs={{0,96},{1,25},{2,98},{3,27},{4,100},{5,29},{6,102},{7,31},{8,104},... | collective-permute-start | bytes 4128776 | tf_op jit(solution)/shard_map/ppermute | solution.py:202
  103.2 8.3 %collective-permute-done.16.rest_6_ = bf16[2,2,8,112,128]{4,3,2,1,0:T(8,128)(2,1)S(1)} collective-permute-done((bf16[2,2,8,112,128]{4,3,2,1,0:T(8,128)(2,1)}, bf16[2,2,8,112,128]{4,3,2,1,0:T(8,128)(2,1)S(1)}, u32[]{:S(2)}, u32[]{:S(2)}) %collective-permute-start.16) | collective-permute-done | bytes 917536 | tf_op jit(solution)/shard_map/ppermute | solution.py:202
  113.4 17.3 %shard_map.104 = (bf16[8,2,256,896]{3,2,1,0:T(8,128)(2,1)}, bf16[4,2,4,112,128]{4,3,2,1,0:T(8,128)(2,1)}, bf16[2,2,4,112,128]{4,3,2,1,0:T(8,128)(2,1)}, bf16[2,2...) custom-call(s32[16]{0:T(128)} %mul.13.rows_tbl, ...), custom_call_target="tpu_custom_call" | custom-call | flops 5637144576 | bytes 22020096 | tf_op jit(solution)/shard_map/pallas_call | solution.py:144
  131.2 2.0 collective-permute-start.20
  133.3 1.3 collective-permute-start.21
  134.8 1.8 collective-permute-start.23
  136.5 17.3 %shard_map.105 = (bf16[8,2,256,896]{3,2,1,0:T(8,128)(2,1)}, bf16[4,2,4,112,128]{4,3,2,1,0:T(8,128)(2,1)}, bf16[2,2,4,112,128]{4,3,2,1,0:T(8,128)(2,1)}, bf16[2,2...) custom-call(s32[16]{0:T(128)} %mul.13.rows_tbl, ...), custom_call_target="tpu_custom_call" | custom-call | flops 5637144576 | bytes 22020096 | tf_op jit(solution)/shard_map/pallas_call | solution.py:144
  155.0 1.4 collective-permute-start.26
  156.3 1.9 collective-permute-start.27
  158.3 1.8 fusion.3
  160.2 1.2 add_convert_fusion.4
  161.5 1.4 collective-permute-start.25
  163.5 1.2 add_convert_fusion.5
  164.6 4.6 %collective-permute-done.30 = bf16[2,6,112,128]{3,2,1,0:T(8,128)(2,1)S(1)} collective-permute-done((bf16[2,6,112,128]{3,2,1,0:T(8,128)(2,1)S(1)}, bf16[2,6,112,128]{3,2,1,0:T(8,128)(2,1)S(1)}, u32[]{:S(2)}, u32[]{:S(2)}) %collective-permute-start.30) | collective-permute-done | bytes 344096 | tf_op jit(solution)/shard_map/ppermute | solution.py:202
  169.7 6.6 %collective-permute-done.29 = bf16[2,6,112,128]{3,2,1,0:T(8,128)(2,1)S(1)} collective-permute-done((bf16[2,6,112,128]{3,2,1,0:T(8,128)(2,1)S(1)}, bf16[2,6,112,128]{3,2,1,0:T(8,128)(2,1)S(1)}, u32[]{:S(2)}, u32[]{:S(2)}) %collective-permute-start.29) | collective-permute-done | bytes 344096 | tf_op jit(solution)/shard_map/ppermute | solution.py:202
  177.2 6.4 %collective-permute-done.28 = bf16[2,6,112,128]{3,2,1,0:T(8,128)(2,1)S(1)} collective-permute-done((bf16[2,6,112,128]{3,2,1,0:T(8,128)(2,1)S(1)}, bf16[2,6,112,128]{3,2,1,0:T(8,128)(2,1)S(1)}, u32[]{:S(2)}, u32[]{:S(2)}) %collective-permute-start.28) | collective-permute-done | bytes 344096 | tf_op jit(solution)/shard_map/ppermute | solution.py:202
  183.6 1.7 fusion.7
  186.3 2.0 collective-permute-start.34
  188.3 1.2 collective-permute-start.33
  189.7 1.8 collective-permute-start.32
  192.2 3.2 %collective-permute-done.35 = bf16[2,4,112,128]{3,2,1,0:T(8,128)(2,1)S(1)} collective-permute-done((bf16[2,4,112,128]{3,2,1,0:T(8,128)(2,1)S(1)}, bf16[2,4,112,128]{3,2,1,0:T(8,128)(2,1)S(1)}, u32[]{:S(2)}, u32[]{:S(2)}) %collective-permute-start.35) | collective-permute-done | bytes 229408 | tf_op jit(solution)/shard_map/ppermute | solution.py:202
  195.4 2.5 %collective-permute-done.34 = bf16[2,4,112,128]{3,2,1,0:T(8,128)(2,1)S(1)} collective-permute-done((bf16[2,4,112,128]{3,2,1,0:T(8,128)(2,1)S(1)}, bf16[2,4,112,128]{3,2,1,0:T(8,128)(2,1)S(1)}, u32[]{:S(2)}, u32[]{:S(2)}) %collective-permute-start.34) | collective-permute-done | bytes 229408 | tf_op jit(solution)/shard_map/ppermute | solution.py:202
  198.8 2.6 %collective-permute-done.31 = bf16[2,2,4,112,128]{4,3,2,1,0:T(8,128)(2,1)S(1)} collective-permute-done((bf16[2,2,4,112,128]{4,3,2,1,0:T(8,128)(2,1)S(1)}, bf16[2,2,4,112,128]{4,3,2,1,0:T(8,128)(2,1)S(1)}, u32[]{:S(2)}, u32[]{:S(2)}) %collective-permute-start.31) | collective-permute-done | bytes 458784 | tf_op jit(solution)/shard_map/ppermute | solution.py:202
  201.7 1.5 collective-permute-start.38
  203.2 3.2 %collective-permute-start.36 = (bf16[2,4,112,128]{3,2,1,0:T(8,128)(2,1)S(1)}, bf16[2,4,112,128]{3,2,1,0:T(8,128)(2,1)S(1)}, u32[]{:S(2)}, u32[]{:S(2)}) collective-permute-start(bf16[2,4,112,128]{3,2,1,0:T(8,128)(2,1)S(1)} %get-tuple-element.261), channel_id=1, source_target_pairs={{0,24},{1,97},{2,26},{3,99},{4,28},{5,101},{6,30},{7,103},{8,0},{9... | collective-permute-start | bytes 688136 | tf_op jit(solution)/shard_map/ppermute | solution.py:202
  206.6 2.2 slice_bitcast_fusion
  209.5 2.4 %collective-permute-done.37 = bf16[2,4,112,128]{3,2,1,0:T(8,128)(2,1)S(1)} collective-permute-done((bf16[2,4,112,128]{3,2,1,0:T(8,128)(2,1)S(1)}, bf16[2,4,112,128]{3,2,1,0:T(8,128)(2,1)S(1)}, u32[]{:S(2)}, u32[]{:S(2)}) %collective-permute-start.37) | collective-permute-done | bytes 229408 | tf_op jit(solution)/shard_map/ppermute | solution.py:202
  (125 shorter events, 16.1 us)
Async XLA Ops:
  7.2 60.2 %all-gather.3.cloned.1.call-start = ((), (), s32[]{:S(2)}) async-start(), calls=%async_computation.2 | async-start | bytes 8257536 | tf_op jit(solution)/shard_map/all_gather | solution.py:243
  9.7 197.0 %reduce-scatter.2.cloned.1.call-start = ((), (), s32[]{:S(2)}) async-start(), calls=%async_computation.1 | async-start | bytes 8257536 | tf_op jit(solution)/shard_map/reduce_scatter | solution.py:284
  9.8 8.8 %collective-permute-start.2 = (bf16[2,6,112,128]{3,2,1,0:T(8,128)(2,1)S(1)}, bf16[2,6,112,128]{3,2,1,0:T(8,128)(2,1)S(1)}, u32[]{:S(2)}, u32[]{:S(2)}) collective-permute-start(bf16[2,6,112,128]{3,2,1,0:T(8,128)(2,1)S(1)} %pad_maximum_fusion.7), channel_id=1, source_target_pairs={{0,16},{1,65},{2,18},{3,67},{4,20},{5,69},{6,22},{7,71},{8,24},{9,... | collective-permute-start | bytes 1032200 | tf_op jit(solution)/shard_map/ppermute | solution.py:202
  13.0 9.5 %collective-permute-start.1 = (bf16[2,6,112,128]{3,2,1,0:T(8,128)(2,1)S(1)}, bf16[2,6,112,128]{3,2,1,0:T(8,128)(2,1)S(1)}, u32[]{:S(2)}, u32[]{:S(2)}) collective-permute-start(bf16[2,6,112,128]{3,2,1,0:T(8,128)(2,1)S(1)} %pad_maximum_fusion.7), channel_id=1, source_target_pairs={{0,24},{1,97},{2,26},{3,99},{4,28},{5,101},{6,30},{7,103},{8,0},{9... | collective-permute-start | bytes 1032200 | tf_op jit(solution)/shard_map/ppermute | solution.py:202
  14.1 8.5 %collective-permute-start = (bf16[2,6,112,128]{3,2,1,0:T(8,128)(2,1)S(1)}, bf16[2,6,112,128]{3,2,1,0:T(8,128)(2,1)S(1)}, u32[]{:S(2)}, u32[]{:S(2)}) collective-permute-start(bf16[2,6,112,128]{3,2,1,0:T(8,128)(2,1)S(1)} %pad_maximum_fusion.7), channel_id=1, source_target_pairs={{0,8},{1,33},{2,10},{3,35},{4,12},{5,37},{6,14},{7,39},{8,16},{9,4... | collective-permute-start | bytes 1032200 | tf_op jit(solution)/shard_map/ppermute | solution.py:202
  22.6 30.8 %copy-start.23 = (s32[4]{0:T(128)S(1)}, s32[4]{0:T(128)}, u32[]{:S(2)}) copy-start(s32[4]{0:T(128)} %constant.63.clone) | copy-start | bytes 52
  22.7 28.7 %copy-start.11 = (bf16[2,2,6,112,128]{4,3,2,1,0:T(8,128)(2,1)}, bf16[2,2,6,112,128]{4,3,2,1,0:T(8,128)(2,1)S(1)}, u32[]{:S(2)}) copy-start(bf16[2,2,6,112,128]{4,3,2,1,0:T(8,128)(2,1)S(1)} %pad_maximum_fusion.2.rest_0_) | copy-start | bytes 2064388
  22.7 11.5 %collective-permute-start.5 = (bf16[2,2,6,112,128]{4,3,2,1,0:T(8,128)(2,1)S(1)}, bf16[2,2,6,112,128]{4,3,2,1,0:T(8,128)(2,1)S(1)}, u32[]{:S(2)}, u32[]{:S(2)}) collective-permute-start(bf16[2,2,6,112,128]{4,3,2,1,0:T(8,128)(2,1)S(1)} %pad_maximum_fusion.2.rest_0_), channel_id=1, source_target_pairs={{0,96},{1,25},{2,98},{3,27},{4,100},{5,29},{6,102},{7,31},{8,104},... | collective-permute-start | bytes 2064392 | tf_op jit(solution)/shard_map/ppermute | solution.py:202
  25.8 12.1 %collective-permute-start.3 = (bf16[2,2,6,112,128]{4,3,2,1,0:T(8,128)(2,1)S(1)}, bf16[2,2,6,112,128]{4,3,2,1,0:T(8,128)(2,1)S(1)}, u32[]{:S(2)}, u32[]{:S(2)}) collective-permute-start(bf16[2,2,6,112,128]{4,3,2,1,0:T(8,128)(2,1)S(1)} %pad_maximum_fusion.2.rest_0_), channel_id=1, source_target_pairs={{0,32},{1,9},{2,34},{3,11},{4,36},{5,13},{6,38},{7,15},{8,40},{9,1... | collective-permute-start | bytes 2064392 | tf_op jit(solution)/shard_map/ppermute | solution.py:202
  25.8 26.8 %copy-start.12 = (bf16[2,2,6,112,128]{4,3,2,1,0:T(8,128)(2,1)}, bf16[2,2,6,112,128]{4,3,2,1,0:T(8,128)(2,1)S(1)}, u32[]{:S(2)}) copy-start(bf16[2,2,6,112,128]{4,3,2,1,0:T(8,128)(2,1)S(1)} %pad_maximum_fusion.3.rest_1_) | copy-start | bytes 2064388
  25.8 15.7 %collective-permute-start.6 = (bf16[2,2,6,112,128]{4,3,2,1,0:T(8,128)(2,1)S(1)}, bf16[2,2,6,112,128]{4,3,2,1,0:T(8,128)(2,1)}, u32[]{:S(2)}, u32[]{:S(2)}) collective-permute-start(bf16[2,2,6,112,128]{4,3,2,1,0:T(8,128)(2,1)S(1)} %pad_maximum_fusion.3.rest_1_), channel_id=1, source_target_pairs={{0,96},{1,25},{2,98},{3,27},{4,100},{5,29},{6,102},{7,31},{8,104},... | collective-permute-start | bytes 2064392 | tf_op jit(solution)/shard_map/ppermute | solution.py:202
  29.1 16.1 %collective-permute-start.4 = (bf16[2,2,6,112,128]{4,3,2,1,0:T(8,128)(2,1)S(1)}, bf16[2,2,6,112,128]{4,3,2,1,0:T(8,128)(2,1)S(1)}, u32[]{:S(2)}, u32[]{:S(2)}) collective-permute-start(bf16[2,2,6,112,128]{4,3,2,1,0:T(8,128)(2,1)S(1)} %pad_maximum_fusion.3.rest_1_), channel_id=1, source_target_pairs={{0,32},{1,9},{2,34},{3,11},{4,36},{5,13},{6,38},{7,15},{8,40},{9,1... | collective-permute-start | bytes 2064392 | tf_op jit(solution)/shard_map/ppermute | solution.py:202
  37.9 29.4 %copy-start.26 = (bf16[2,2,6,112,128]{4,3,2,1,0:T(8,128)(2,1)}, bf16[2,2,6,112,128]{4,3,2,1,0:T(8,128)(2,1)S(1)}, u32[]{:S(2)}) copy-start(bf16[2,2,6,112,128]{4,3,2,1,0:T(8,128)(2,1)S(1)} %collective-permute-done.3.rest_2_) | copy-start | bytes 2064388
  45.3 22.1 %collective-permute-start.7 = (bf16[2,2,6,112,128]{4,3,2,1,0:T(8,128)(2,1)S(1)}, bf16[2,2,6,112,128]{4,3,2,1,0:T(8,128)(2,1)}, u32[]{:S(2)}, u32[]{:S(2)}) collective-permute-start(bf16[2,2,6,112,128]{4,3,2,1,0:T(8,128)(2,1)S(1)} %collective-permute-done.3.rest_2_), channel_id=1, source_target_pairs={{0,32},{1,9},{2,34},{3,11},{4,36},{5,13},{6,38},{7,15},{8,40},{9,1... | collective-permute-start | bytes 2064392 | tf_op jit(solution)/shard_map/ppermute | solution.py:202
  45.3 22.1 %collective-permute-start.8 = (bf16[2,2,6,112,128]{4,3,2,1,0:T(8,128)(2,1)}, bf16[2,2,6,112,128]{4,3,2,1,0:T(8,128)(2,1)}, u32[]{:S(2)}, u32[]{:S(2)}) collective-permute-start(bf16[2,2,6,112,128]{4,3,2,1,0:T(8,128)(2,1)} %collective-permute-done.6.rest_5_), channel_id=1, source_target_pairs={{0,96},{1,25},{2,98},{3,27},{4,100},{5,29},{6,102},{7,31},{8,104},... | collective-permute-start | bytes 2064392 | tf_op jit(solution)/shard_map/ppermute | solution.py:202
  48.5 10.1 %collective-permute-start.11 = (bf16[2,8,112,128]{3,2,1,0:T(8,128)(2,1)S(1)}, bf16[2,8,112,128]{3,2,1,0:T(8,128)(2,1)S(1)}, u32[]{:S(2)}, u32[]{:S(2)}) collective-permute-start(bf16[2,8,112,128]{3,2,1,0:T(8,128)(2,1)S(1)} %pad_maximum_fusion.4), channel_id=1, source_target_pairs={{0,16},{1,65},{2,18},{3,67},{4,20},{5,69},{6,22},{7,71},{8,24},{9,... | collective-permute-start | bytes 1376264 | tf_op jit(solution)/shard_map/ppermute | solution.py:202
  51.4 12.3 %collective-permute-start.10 = (bf16[2,8,112,128]{3,2,1,0:T(8,128)(2,1)S(1)}, bf16[2,8,112,128]{3,2,1,0:T(8,128)(2,1)S(1)}, u32[]{:S(2)}, u32[]{:S(2)}) collective-permute-start(bf16[2,8,112,128]{3,2,1,0:T(8,128)(2,1)S(1)} %pad_maximum_fusion.4), channel_id=1, source_target_pairs={{0,24},{1,97},{2,26},{3,99},{4,28},{5,101},{6,30},{7,103},{8,0},{9... | collective-permute-start | bytes 1376264 | tf_op jit(solution)/shard_map/ppermute | solution.py:202
  52.6 11.6 %collective-permute-start.9 = (bf16[2,8,112,128]{3,2,1,0:T(8,128)(2,1)S(1)}, bf16[2,8,112,128]{3,2,1,0:T(8,128)(2,1)S(1)}, u32[]{:S(2)}, u32[]{:S(2)}) collective-permute-start(bf16[2,8,112,128]{3,2,1,0:T(8,128)(2,1)S(1)} %pad_maximum_fusion.4), channel_id=1, source_target_pairs={{0,8},{1,33},{2,10},{3,35},{4,12},{5,37},{6,14},{7,39},{8,16},{9,4... | collective-permute-start | bytes 1376264 | tf_op jit(solution)/shard_map/ppermute | solution.py:202
  67.5 29.1 %copy-start = (bf16[2,2,8,112,128]{4,3,2,1,0:T(8,128)(2,1)}, bf16[2,2,8,112,128]{4,3,2,1,0:T(8,128)(2,1)S(1)}, u32[]{:S(2)}) copy-start(bf16[2,2,8,112,128]{4,3,2,1,0:T(8,128)(2,1)S(1)} %pad_maximum_fusion.1.rest_1_) | copy-start | bytes 2752516
  67.5 29.1 %collective-permute-start.15 = (bf16[2,2,8,112,128]{4,3,2,1,0:T(8,128)(2,1)S(1)}, bf16[2,2,8,112,128]{4,3,2,1,0:T(8,128)(2,1)S(1)}, u32[]{:S(2)}, u32[]{:S(2)}) collective-permute-start(bf16[2,2,8,112,128]{4,3,2,1,0:T(8,128)(2,1)S(1)} %pad_maximum_fusion.1.rest_1_), channel_id=1, source_target_pairs={{0,96},{1,25},{2,98},{3,27},{4,100},{5,29},{6,102},{7,31},{8,104},... | collective-permute-start | bytes 2752520 | tf_op jit(solution)/shard_map/ppermute | solution.py:202
  70.5 26.1 %collective-permute-start.13 = (bf16[2,2,8,112,128]{4,3,2,1,0:T(8,128)(2,1)S(1)}, bf16[2,2,8,112,128]{4,3,2,1,0:T(8,128)(2,1)}, u32[]{:S(2)}, u32[]{:S(2)}) collective-permute-start(bf16[2,2,8,112,128]{4,3,2,1,0:T(8,128)(2,1)S(1)} %pad_maximum_fusion.1.rest_1_), channel_id=1, source_target_pairs={{0,32},{1,9},{2,34},{3,11},{4,36},{5,13},{6,38},{7,15},{8,40},{9,1... | collective-permute-start | bytes 2752520 | tf_op jit(solution)/shard_map/ppermute | solution.py:202
  71.6 24.9 %copy-start.1 = (bf16[2,2,8,112,128]{4,3,2,1,0:T(8,128)(2,1)}, bf16[2,2,8,112,128]{4,3,2,1,0:T(8,128)(2,1)S(1)}, u32[]{:S(2)}) copy-start(bf16[2,2,8,112,128]{4,3,2,1,0:T(8,128)(2,1)S(1)} %pad_maximum_fusion.rest_0_) | copy-start | bytes 2752516
  71.6 25.0 %collective-permute-start.14 = (bf16[2,2,8,112,128]{4,3,2,1,0:T(8,128)(2,1)S(1)}, bf16[2,2,8,112,128]{4,3,2,1,0:T(8,128)(2,1)}, u32[]{:S(2)}, u32[]{:S(2)}) collective-permute-start(bf16[2,2,8,112,128]{4,3,2,1,0:T(8,128)(2,1)S(1)} %pad_maximum_fusion.rest_0_), channel_id=1, source_target_pairs={{0,96},{1,25},{2,98},{3,27},{4,100},{5,29},{6,102},{7,31},{8,104},... | collective-permute-start | bytes 2752520 | tf_op jit(solution)/shard_map/ppermute | solution.py:202
  74.9 21.7 %collective-permute-start.12 = (bf16[2,2,8,112,128]{4,3,2,1,0:T(8,128)(2,1)S(1)}, bf16[2,2,8,112,128]{4,3,2,1,0:T(8,128)(2,1)}, u32[]{:S(2)}, u32[]{:S(2)}) collective-permute-start(bf16[2,2,8,112,128]{4,3,2,1,0:T(8,128)(2,1)S(1)} %pad_maximum_fusion.rest_0_), channel_id=1, source_target_pairs={{0,32},{1,9},{2,34},{3,11},{4,36},{5,13},{6,38},{7,15},{8,40},{9,1... | collective-permute-start | bytes 2752520 | tf_op jit(solution)/shard_map/ppermute | solution.py:202
  96.6 34.1 %copy-start.14 = (bf16[2,2,6,112,128]{4,3,2,1,0:T(8,128)(2,1)S(1)}, bf16[2,2,6,112,128]{4,3,2,1,0:T(8,128)(2,1)}, u32[]{:S(2)}) copy-start(bf16[2,2,6,112,128]{4,3,2,1,0:T(8,128)(2,1)} %get-tuple-element.197) | copy-start | bytes 2064388
  96.6 14.9 %collective-permute-start.16 = (bf16[2,2,8,112,128]{4,3,2,1,0:T(8,128)(2,1)}, bf16[2,2,8,112,128]{4,3,2,1,0:T(8,128)(2,1)S(1)}, u32[]{:S(2)}, u32[]{:S(2)}) collective-permute-start(bf16[2,2,8,112,128]{4,3,2,1,0:T(8,128)(2,1)} %collective-permute-done.12.rest_2_), channel_id=1, source_target_pairs={{0,32},{1,9},{2,34},{3,11},{4,36},{5,13},{6,38},{7,15},{8,40},{9,1... | collective-permute-start | bytes 2752520 | tf_op jit(solution)/shard_map/ppermute | solution.py:202
  96.7 14.8 %collective-permute-start.17 = (bf16[2,2,8,112,128]{4,3,2,1,0:T(8,128)(2,1)S(1)}, bf16[2,2,8,112,128]{4,3,2,1,0:T(8,128)(2,1)S(1)}, u32[]{:S(2)}, u32[]{:S(2)}) collective-permute-start(bf16[2,2,8,112,128]{4,3,2,1,0:T(8,128)(2,1)S(1)} %collective-permute-done.15.rest_5_), channel_id=1, source_target_pairs={{0,96},{1,25},{2,98},{3,27},{4,100},{5,29},{6,102},{7,31},{8,104},... | collective-permute-start | bytes 2752520 | tf_op jit(solution)/shard_map/ppermute | solution.py:202
  100.0 30.7 %collective-permute-start.18 = (bf16[4,2,6,112,128]{4,3,2,1,0:T(8,128)(2,1)}, bf16[4,2,6,112,128]{4,3,2,1,0:T(8,128)(2,1)S(1)}, u32[]{:S(2)}, u32[]{:S(2)}) collective-permute-start(bf16[4,2,6,112,128]{4,3,2,1,0:T(8,128)(2,1)} %get-tuple-element.177), channel_id=1, source_target_pairs={{0,32},{1,9},{2,34},{3,11},{4,36},{5,13},{6,38},{7,15},{8,40},{9,1... | collective-permute-start | bytes 4128776 | tf_op jit(solution)/shard_map/ppermute | solution.py:202
  100.0 30.7 %collective-permute-start.19 = (bf16[4,2,6,112,128]{4,3,2,1,0:T(8,128)(2,1)}, bf16[4,2,6,112,128]{4,3,2,1,0:T(8,128)(2,1)S(1)}, u32[]{:S(2)}, u32[]{:S(2)}) collective-permute-start(bf16[4,2,6,112,128]{4,3,2,1,0:T(8,128)(2,1)} %get-tuple-element.178), channel_id=1, source_target_pairs={{0,96},{1,25},{2,98},{3,27},{4,100},{5,29},{6,102},{7,31},{8,104},... | collective-permute-start | bytes 4128776 | tf_op jit(solution)/shard_map/ppermute | solution.py:202
  130.9 22.9 %collective-permute-start.22 = (bf16[2,2,6,112,128]{4,3,2,1,0:T(8,128)(2,1)S(1)}, bf16[2,2,6,112,128]{4,3,2,1,0:T(8,128)(2,1)S(1)}, u32[]{:S(2)}, u32[]{:S(2)}) collective-permute-start(bf16[2,2,6,112,128]{4,3,2,1,0:T(8,128)(2,1)S(1)} %add_convert_fusion.1), channel_id=1, source_target_pairs={{0,32},{1,9},{2,34},{3,11},{4,36},{5,13},{6,38},{7,15},{8,40},{9,1... | collective-permute-start | bytes 2064392 | tf_op jit(solution)/shard_map/ppermute | solution.py:202
  131.2 23.7 %collective-permute-start.20 = (bf16[4,2,4,112,128]{4,3,2,1,0:T(8,128)(2,1)}, bf16[4,2,4,112,128]{4,3,2,1,0:T(8,128)(2,1)}, u32[]{:S(2)}, u32[]{:S(2)}) collective-permute-start(bf16[4,2,4,112,128]{4,3,2,1,0:T(8,128)(2,1)} %get-tuple-element.201), channel_id=1, source_target_pairs={{0,32},{1,9},{2,34},{3,11},{4,36},{5,13},{6,38},{7,15},{8,40},{9,1... | collective-permute-start | bytes 2752520 | tf_op jit(solution)/shard_map/ppermute | solution.py:202
  133.3 21.6 %collective-permute-start.21 = (bf16[4,2,4,112,128]{4,3,2,1,0:T(8,128)(2,1)S(1)}, bf16[4,2,4,112,128]{4,3,2,1,0:T(8,128)(2,1)}, u32[]{:S(2)}, u32[]{:S(2)}) collective-permute-start(bf16[4,2,4,112,128]{4,3,2,1,0:T(8,128)(2,1)S(1)} %copy-done.24), channel_id=1, source_target_pairs={{0,96},{1,25},{2,98},{3,27},{4,100},{5,29},{6,102},{7,31},{8,104},... | collective-permute-start | bytes 2752520 | tf_op jit(solution)/shard_map/ppermute | solution.py:202
  134.8 19.3 %collective-permute-start.23 = (bf16[2,2,6,112,128]{4,3,2,1,0:T(8,128)(2,1)S(1)}, bf16[2,2,6,112,128]{4,3,2,1,0:T(8,128)(2,1)S(1)}, u32[]{:S(2)}, u32[]{:S(2)}) collective-permute-start(bf16[2,2,6,112,128]{4,3,2,1,0:T(8,128)(2,1)S(1)} %add_convert_fusion), channel_id=1, source_target_pairs={{0,96},{1,25},{2,98},{3,27},{4,100},{5,29},{6,102},{7,31},{8,104},... | collective-permute-start | bytes 2064392 | tf_op jit(solution)/shard_map/ppermute | solution.py:202
  155.0 28.6 %collective-permute-start.26 = (bf16[4,2,4,112,128]{4,3,2,1,0:T(8,128)(2,1)}, bf16[4,2,4,112,128]{4,3,2,1,0:T(8,128)(2,1)S(1)}, u32[]{:S(2)}, u32[]{:S(2)}) collective-permute-start(bf16[4,2,4,112,128]{4,3,2,1,0:T(8,128)(2,1)} %get-tuple-element.217), channel_id=1, source_target_pairs={{0,32},{1,9},{2,34},{3,11},{4,36},{5,13},{6,38},{7,15},{8,40},{9,1... | collective-permute-start | bytes 2752520 | tf_op jit(solution)/shard_map/ppermute | solution.py:202
  156.3 27.3 %collective-permute-start.27 = (bf16[4,2,4,112,128]{4,3,2,1,0:T(8,128)(2,1)}, bf16[4,2,4,112,128]{4,3,2,1,0:T(8,128)(2,1)S(1)}, u32[]{:S(2)}, u32[]{:S(2)}) collective-permute-start(bf16[4,2,4,112,128]{4,3,2,1,0:T(8,128)(2,1)} %get-tuple-element.218), channel_id=1, source_target_pairs={{0,96},{1,25},{2,98},{3,27},{4,100},{5,29},{6,102},{7,31},{8,104},... | collective-permute-start | bytes 2752520 | tf_op jit(solution)/shard_map/ppermute | solution.py:202
  160.1 9.1 %collective-permute-start.30 = (bf16[2,6,112,128]{3,2,1,0:T(8,128)(2,1)S(1)}, bf16[2,6,112,128]{3,2,1,0:T(8,128)(2,1)S(1)}, u32[]{:S(2)}, u32[]{:S(2)}) collective-permute-start(bf16[2,6,112,128]{3,2,1,0:T(8,128)(2,1)S(1)} %get-tuple-element.246), channel_id=1, source_target_pairs={{0,16},{1,65},{2,18},{3,67},{4,20},{5,69},{6,22},{7,71},{8,24},{9,... | collective-permute-start | bytes 1032200 | tf_op jit(solution)/shard_map/ppermute | solution.py:202
  161.5 22.1 %collective-permute-start.25 = (bf16[2,2,4,112,128]{4,3,2,1,0:T(8,128)(2,1)S(1)}, bf16[2,2,4,112,128]{4,3,2,1,0:T(8,128)(2,1)S(1)}, u32[]{:S(2)}, u32[]{:S(2)}) collective-permute-start(bf16[2,2,4,112,128]{4,3,2,1,0:T(8,128)(2,1)S(1)} %add_convert_fusion.4), channel_id=1, source_target_pairs={{0,96},{1,25},{2,98},{3,27},{4,100},{5,29},{6,102},{7,31},{8,104},... | collective-permute-start | bytes 1376264 | tf_op jit(solution)/shard_map/ppermute | solution.py:202
  162.8 13.5 %collective-permute-start.29 = (bf16[2,6,112,128]{3,2,1,0:T(8,128)(2,1)S(1)}, bf16[2,6,112,128]{3,2,1,0:T(8,128)(2,1)S(1)}, u32[]{:S(2)}, u32[]{:S(2)}) collective-permute-start(bf16[2,6,112,128]{3,2,1,0:T(8,128)(2,1)S(1)} %get-tuple-element.247), channel_id=1, source_target_pairs={{0,8},{1,33},{2,10},{3,35},{4,12},{5,37},{6,14},{7,39},{8,16},{9,4... | collective-permute-start | bytes 1032200 | tf_op jit(solution)/shard_map/ppermute | solution.py:202
  169.2 14.4 %collective-permute-start.24 = (bf16[2,2,4,112,128]{4,3,2,1,0:T(8,128)(2,1)S(1)}, bf16[2,2,4,112,128]{4,3,2,1,0:T(8,128)(2,1)S(1)}, u32[]{:S(2)}, u32[]{:S(2)}) collective-permute-start(bf16[2,2,4,112,128]{4,3,2,1,0:T(8,128)(2,1)S(1)} %add_convert_fusion.5), channel_id=1, source_target_pairs={{0,32},{1,9},{2,34},{3,11},{4,36},{5,13},{6,38},{7,15},{8,40},{9,1... | collective-permute-start | bytes 1376264 | tf_op jit(solution)/shard_map/ppermute | solution.py:202
  176.3 7.2 %collective-permute-start.28 = (bf16[2,6,112,128]{3,2,1,0:T(8,128)(2,1)S(1)}, bf16[2,6,112,128]{3,2,1,0:T(8,128)(2,1)S(1)}, u32[]{:S(2)}, u32[]{:S(2)}) collective-permute-start(bf16[2,6,112,128]{3,2,1,0:T(8,128)(2,1)S(1)} %get-tuple-element.259), channel_id=1, source_target_pairs={{0,24},{1,97},{2,26},{3,99},{4,28},{5,101},{6,30},{7,103},{8,0},{9... | collective-permute-start | bytes 1032200 | tf_op jit(solution)/shard_map/ppermute | solution.py:202
  185.3 10.1 %collective-permute-start.35 = (bf16[2,4,112,128]{3,2,1,0:T(8,128)(2,1)S(1)}, bf16[2,4,112,128]{3,2,1,0:T(8,128)(2,1)S(1)}, u32[]{:S(2)}, u32[]{:S(2)}) collective-permute-start(bf16[2,4,112,128]{3,2,1,0:T(8,128)(2,1)S(1)} %get-tuple-element.254), channel_id=1, source_target_pairs={{0,16},{1,65},{2,18},{3,67},{4,20},{5,69},{6,22},{7,71},{8,24},{9,... | collective-permute-start | bytes 688136 | tf_op jit(solution)/shard_map/ppermute | solution.py:202
  186.3 11.6 %collective-permute-start.34 = (bf16[2,4,112,128]{3,2,1,0:T(8,128)(2,1)S(1)}, bf16[2,4,112,128]{3,2,1,0:T(8,128)(2,1)S(1)}, u32[]{:S(2)}, u32[]{:S(2)}) collective-permute-start(bf16[2,4,112,128]{3,2,1,0:T(8,128)(2,1)S(1)} %get-tuple-element.255), channel_id=1, source_target_pairs={{0,8},{1,33},{2,10},{3,35},{4,12},{5,37},{6,14},{7,39},{8,16},{9,4... | collective-permute-start | bytes 688136 | tf_op jit(solution)/shard_map/ppermute | solution.py:202
  188.3 10.4 %collective-permute-start.33 = (bf16[2,4,112,128]{3,2,1,0:T(8,128)(2,1)S(1)}, bf16[2,4,112,128]{3,2,1,0:T(8,128)(2,1)S(1)}, u32[]{:S(2)}, u32[]{:S(2)}) collective-permute-start(bf16[2,4,112,128]{3,2,1,0:T(8,128)(2,1)S(1)} %get-tuple-element.263), channel_id=1, source_target_pairs={{0,24},{1,97},{2,26},{3,99},{4,28},{5,101},{6,30},{7,103},{8,0},{9... | collective-permute-start | bytes 688136 | tf_op jit(solution)/shard_map/ppermute | solution.py:202
  189.7 9.1 %collective-permute-start.32 = (bf16[2,2,4,112,128]{4,3,2,1,0:T(8,128)(2,1)S(1)}, bf16[2,2,4,112,128]{4,3,2,1,0:T(8,128)(2,1)S(1)}, u32[]{:S(2)}, u32[]{:S(2)}) collective-permute-start(bf16[2,2,4,112,128]{4,3,2,1,0:T(8,128)(2,1)S(1)} %add_convert_fusion.2), channel_id=1, source_target_pairs={{0,96},{1,25},{2,98},{3,27},{4,100},{5,29},{6,102},{7,31},{8,104},... | collective-permute-start | bytes 1376264 | tf_op jit(solution)/shard_map/ppermute | solution.py:202
  191.6 9.8 %collective-permute-start.31 = (bf16[2,2,4,112,128]{4,3,2,1,0:T(8,128)(2,1)S(1)}, bf16[2,2,4,112,128]{4,3,2,1,0:T(8,128)(2,1)S(1)}, u32[]{:S(2)}, u32[]{:S(2)}) collective-permute-start(bf16[2,2,4,112,128]{4,3,2,1,0:T(8,128)(2,1)S(1)} %add_convert_fusion.3), channel_id=1, source_target_pairs={{0,32},{1,9},{2,34},{3,11},{4,36},{5,13},{6,38},{7,15},{8,40},{9,1... | collective-permute-start | bytes 1376264 | tf_op jit(solution)/shard_map/ppermute | solution.py:202
  201.7 7.7 %collective-permute-start.38 = (bf16[2,4,112,128]{3,2,1,0:T(8,128)(2,1)S(1)}, bf16[2,4,112,128]{3,2,1,0:T(8,128)(2,1)S(1)}, u32[]{:S(2)}, u32[]{:S(2)}) collective-permute-start(bf16[2,4,112,128]{3,2,1,0:T(8,128)(2,1)S(1)} %get-tuple-element.250), channel_id=1, source_target_pairs={{0,16},{1,65},{2,18},{3,67},{4,20},{5,69},{6,22},{7,71},{8,24},{9,... | collective-permute-start | bytes 688136 | tf_op jit(solution)/shard_map/ppermute | solution.py:202
  203.2 8.6 %collective-permute-start.37 = (bf16[2,4,112,128]{3,2,1,0:T(8,128)(2,1)S(1)}, bf16[2,4,112,128]{3,2,1,0:T(8,128)(2,1)S(1)}, u32[]{:S(2)}, u32[]{:S(2)}) collective-permute-start(bf16[2,4,112,128]{3,2,1,0:T(8,128)(2,1)S(1)} %get-tuple-element.251), channel_id=1, source_target_pairs={{0,8},{1,33},{2,10},{3,35},{4,12},{5,37},{6,14},{7,39},{8,16},{9,4... | collective-permute-start | bytes 688136 | tf_op jit(solution)/shard_map/ppermute | solution.py:202
  203.2 8.6 %collective-permute-start.36 = (bf16[2,4,112,128]{3,2,1,0:T(8,128)(2,1)S(1)}, bf16[2,4,112,128]{3,2,1,0:T(8,128)(2,1)S(1)}, u32[]{:S(2)}, u32[]{:S(2)}) collective-permute-start(bf16[2,4,112,128]{3,2,1,0:T(8,128)(2,1)S(1)} %get-tuple-element.261), channel_id=1, source_target_pairs={{0,24},{1,97},{2,26},{3,99},{4,28},{5,101},{6,30},{7,103},{8,0},{9... | collective-permute-start | bytes 688136 | tf_op jit(solution)/shard_map/ppermute | solution.py:202
  (21 other events, 121.5 us)
Sparse Core Ops, SparseCore 0:
  9.8 47.9 all-gather.2
  155.1 46.8 reduce-scatter.1

commit v4 on v3

--- a/solution.py
+++ b/solution.py
@@ -259,8 +259,6 @@
     )
 
     n0 = near(w[0])
-    n0, w = tie(n0, w)
-
     c0 = cross(w[0], n0)
     c0, w = tie(c0, w)
 

time: 221 us -> 217 us (0.982)
  waiting for transfers between devices: 75.9 us -> 68.4 us
  starting transfers between devices: 55.9 us -> 59.6 us
    ppermute x39, waiting for transfers between devices: 75.8 us -> 68.3 us  [shift(): return lax.ppermute(value, ('dp', 'tensor'), pairs)]
    ppermute x39, starting transfers between devices: 55.8 us -> 59.6 us  [shift(): return lax.ppermute(value, ('dp', 'tensor'), pairs)]
  transfers between devices with their start and end apart: 41 -> 41, of which waited for: 22 -> 21; matrix products, arithmetic and copies ran while one was open for 5% -> 5% of each run, Pallas kernels for 25% -> 26%
where the time goes in v4:
time: 217 us
  waiting for transfers between devices  68.4 us (32%)
  starting transfers between devices  59.6 us (27%)
  Pallas kernels  57.9 us (27%)
  between operations  14.6 us (7%)
  other arithmetic  10.3 us (5%)
  local copies, waits for them, and re-layouts  5.77 us (3%)
    ppermute x39, waiting for transfers between devices, shift(): return lax.ppermute(value, ('dp', 'tensor'), pairs)  68.3 us
    ppermute x39, starting transfers between devices, shift(): return lax.ppermute(value, ('dp', 'tensor'), pairs)  59.6 us
    pallas_call x3, Pallas kernels, layer_part(): pl.pallas_call(functools.partial(layer_kernel, base + first, len(extra)),...  55.5 us
    convert_element_type x12, other arithmetic, add(): return sum((t.astype(F32) for t in terms)).astype(BF16)  7.23 us
  transfers between devices with their start and end apart: 41, of which 21 were waited for; matrix products, arithmetic and copies ran while one was open for 5% of the time, Pallas kernels for 26%

profile of v4, /device:TPU:0, one launch (start us, length us, event | category | flops | bytes accessed | tf_op | source)
XLA Modules:
  0.0 216.6 jit_solution(1405271089961493708)
XLA Ops:
  7.2 2.4 %shard_map.102 = bf16[2,7,256,128]{3,2,1,0:T(8,128)(2,1)} custom-call(bf16[256,896]{1,0:T(8,128)(2,1)} %tokens.1, bf16[256,896]{1,0:T(8,128)(2,1)} %cotangent.1), custom_call_target="tpu_custom_call" | custom-call | tf_op jit(solution)/shard_map/pallas_call | solution.py:188
  9.8 1.6 collective-permute-start
  11.5 2.7 %collective-permute-start.2 = (bf16[2,6,112,128]{3,2,1,0:T(8,128)(2,1)S(1)}, bf16[2,6,112,128]{3,2,1,0:T(8,128)(2,1)S(1)}, u32[]{:S(2)}, u32[]{:S(2)}) collective-permute-start(bf16[2,6,112,128]{3,2,1,0:T(8,128)(2,1)S(1)} %get-tuple-element.259), channel_id=1, source_target_pairs={{0,16},{1,65},{2,18},{3,67},{4,20},{5,69},{6,22},{7,71},{8,24},{9,... | collective-permute-start | bytes 1032200 | tf_op jit(solution)/shard_map/ppermute | solution.py:202
  14.2 1.4 collective-permute-start.1
  15.6 2.7 %collective-permute-done = bf16[2,6,112,128]{3,2,1,0:T(8,128)(2,1)S(1)} collective-permute-done((bf16[2,6,112,128]{3,2,1,0:T(8,128)(2,1)S(1)}, bf16[2,6,112,128]{3,2,1,0:T(8,128)(2,1)S(1)}, u32[]{:S(2)}, u32[]{:S(2)}) %collective-permute-start) | collective-permute-done | bytes 344096 | tf_op jit(solution)/shard_map/ppermute | solution.py:202
  18.4 3.2 %collective-permute-start.5 = (bf16[2,2,6,112,128]{4,3,2,1,0:T(8,128)(2,1)S(1)}, bf16[2,2,6,112,128]{4,3,2,1,0:T(8,128)(2,1)S(1)}, u32[]{:S(2)}, u32[]{:S(2)}) collective-permute-start(bf16[2,2,6,112,128]{4,3,2,1,0:T(8,128)(2,1)S(1)} %pad_maximum_fusion.2.rest_0_), channel_id=1, source_target_pairs={{0,96},{1,25},{2,98},{3,27},{4,100},{5,29},{6,102},{7,31},{8,104},... | collective-permute-start | bytes 2064392 | tf_op jit(solution)/shard_map/ppermute | solution.py:202
  21.6 1.7 collective-permute-done.2
  23.3 2.2 collective-permute-done.1
  25.6 4.5 %collective-permute-start.6 = (bf16[2,2,6,112,128]{4,3,2,1,0:T(8,128)(2,1)S(1)}, bf16[2,2,6,112,128]{4,3,2,1,0:T(8,128)(2,1)}, u32[]{:S(2)}, u32[]{:S(2)}) collective-permute-start(bf16[2,2,6,112,128]{4,3,2,1,0:T(8,128)(2,1)S(1)} %pad_maximum_fusion.3.rest_1_), channel_id=1, source_target_pairs={{0,96},{1,25},{2,98},{3,27},{4,100},{5,29},{6,102},{7,31},{8,104},... | collective-permute-start | bytes 2064392 | tf_op jit(solution)/shard_map/ppermute | solution.py:202
  30.2 3.5 %collective-permute-done.3.rest_2_ = bf16[2,2,6,112,128]{4,3,2,1,0:T(8,128)(2,1)S(1)} collective-permute-done((bf16[2,2,6,112,128]{4,3,2,1,0:T(8,128)(2,1)S(1)}, bf16[2,2,6,112,128]{4,3,2,1,0:T(8,128)(2,1)S(1)}, u32[]{:S(2)}, u32[]{:S(2)}) %collective-permute-start.3) | collective-permute-done | bytes 688160 | tf_op jit(solution)/shard_map/ppermute | solution.py:202
  33.7 4.8 %collective-permute-done.6.rest_5_ = bf16[2,2,6,112,128]{4,3,2,1,0:T(8,128)(2,1)} collective-permute-done((bf16[2,2,6,112,128]{4,3,2,1,0:T(8,128)(2,1)S(1)}, bf16[2,2,6,112,128]{4,3,2,1,0:T(8,128)(2,1)}, u32[]{:S(2)}, u32[]{:S(2)}) %collective-permute-start.6) | collective-permute-done | bytes 688160 | tf_op jit(solution)/shard_map/ppermute | solution.py:202
  38.6 3.7 %collective-permute-done.4.rest_3_ = bf16[2,2,6,112,128]{4,3,2,1,0:T(8,128)(2,1)S(1)} collective-permute-done((bf16[2,2,6,112,128]{4,3,2,1,0:T(8,128)(2,1)S(1)}, bf16[2,2,6,112,128]{4,3,2,1,0:T(8,128)(2,1)S(1)}, u32[]{:S(2)}, u32[]{:S(2)}) %collective-permute-start.4) | collective-permute-done | bytes 688160 | tf_op jit(solution)/shard_map/ppermute | solution.py:202
  42.3 3.2 %collective-permute-start.8 = (bf16[2,2,6,112,128]{4,3,2,1,0:T(8,128)(2,1)}, bf16[2,2,6,112,128]{4,3,2,1,0:T(8,128)(2,1)}, u32[]{:S(2)}, u32[]{:S(2)}) collective-permute-start(bf16[2,2,6,112,128]{4,3,2,1,0:T(8,128)(2,1)} %collective-permute-done.6.rest_5_), channel_id=1, source_target_pairs={{0,96},{1,25},{2,98},{3,27},{4,100},{5,29},{6,102},{7,31},{8,104},... | collective-permute-start | bytes 2064392 | tf_op jit(solution)/shard_map/ppermute | solution.py:202
  45.5 3.1 %collective-permute-start.11 = (bf16[2,8,112,128]{3,2,1,0:T(8,128)(2,1)S(1)}, bf16[2,8,112,128]{3,2,1,0:T(8,128)(2,1)S(1)}, u32[]{:S(2)}, u32[]{:S(2)}) collective-permute-start(bf16[2,8,112,128]{3,2,1,0:T(8,128)(2,1)S(1)} %pad_maximum_fusion.4), channel_id=1, source_target_pairs={{0,16},{1,65},{2,18},{3,67},{4,20},{5,69},{6,22},{7,71},{8,24},{9,... | collective-permute-start | bytes 1376264 | tf_op jit(solution)/shard_map/ppermute | solution.py:202
  49.4 1.3 collective-permute-start.9
  50.7 4.9 %collective-permute-done.11 = bf16[2,8,112,128]{3,2,1,0:T(8,128)(2,1)S(1)} collective-permute-done((bf16[2,8,112,128]{3,2,1,0:T(8,128)(2,1)S(1)}, bf16[2,8,112,128]{3,2,1,0:T(8,128)(2,1)S(1)}, u32[]{:S(2)}, u32[]{:S(2)}) %collective-permute-start.11) | collective-permute-done | bytes 458784 | tf_op jit(solution)/shard_map/ppermute | solution.py:202
  55.6 4.1 %collective-permute-done.10 = bf16[2,8,112,128]{3,2,1,0:T(8,128)(2,1)S(1)} collective-permute-done((bf16[2,8,112,128]{3,2,1,0:T(8,128)(2,1)S(1)}, bf16[2,8,112,128]{3,2,1,0:T(8,128)(2,1)S(1)}, u32[]{:S(2)}, u32[]{:S(2)}) %collective-permute-start.10) | collective-permute-done | bytes 458784 | tf_op jit(solution)/shard_map/ppermute | solution.py:202
  60.4 3.9 %collective-permute-done.7.rest_6_ = bf16[2,2,6,112,128]{4,3,2,1,0:T(8,128)(2,1)} collective-permute-done((bf16[2,2,6,112,128]{4,3,2,1,0:T(8,128)(2,1)S(1)}, bf16[2,2,6,112,128]{4,3,2,1,0:T(8,128)(2,1)}, u32[]{:S(2)}, u32[]{:S(2)}) %collective-permute-start.7) | collective-permute-done | bytes 688160 | tf_op jit(solution)/shard_map/ppermute | solution.py:202
  64.5 2.2 %collective-permute-start.15 = (bf16[2,2,8,112,128]{4,3,2,1,0:T(8,128)(2,1)S(1)}, bf16[2,2,8,112,128]{4,3,2,1,0:T(8,128)(2,1)S(1)}, u32[]{:S(2)}, u32[]{:S(2)}) collective-permute-start(bf16[2,2,8,112,128]{4,3,2,1,0:T(8,128)(2,1)S(1)} %pad_maximum_fusion.1.rest_1_), channel_id=1, source_target_pairs={{0,96},{1,25},{2,98},{3,27},{4,100},{5,29},{6,102},{7,31},{8,104},... | collective-permute-start | bytes 2752520 | tf_op jit(solution)/shard_map/ppermute | solution.py:202
  67.8 3.3 %collective-permute-start.14 = (bf16[2,2,8,112,128]{4,3,2,1,0:T(8,128)(2,1)S(1)}, bf16[2,2,8,112,128]{4,3,2,1,0:T(8,128)(2,1)}, u32[]{:S(2)}, u32[]{:S(2)}) collective-permute-start(bf16[2,2,8,112,128]{4,3,2,1,0:T(8,128)(2,1)S(1)} %pad_maximum_fusion.rest_0_), channel_id=1, source_target_pairs={{0,96},{1,25},{2,98},{3,27},{4,100},{5,29},{6,102},{7,31},{8,104},... | collective-permute-start | bytes 2752520 | tf_op jit(solution)/shard_map/ppermute | solution.py:202
  71.8 21.0 %shard_map.103 = (bf16[8,2,256,896]{3,2,1,0:T(8,128)(2,1)}, bf16[4,2,6,112,128]{4,3,2,1,0:T(8,128)(2,1)}, bf16[2,2,6,112,128]{4,3,2,1,0:T(8,128)(2,1)}, bf16[2,2...) custom-call(s32[16]{0:T(128)} %mul.13.rows_tbl, ...), custom_call_target="tpu_custom_call" | custom-call | flops 8455716864 | bytes 25690112 | tf_op jit(solution)/shard_map/pallas_call | solution.py:144
  92.9 3.3 %collective-permute-start.17 = (bf16[2,2,8,112,128]{4,3,2,1,0:T(8,128)(2,1)S(1)}, bf16[2,2,8,112,128]{4,3,2,1,0:T(8,128)(2,1)S(1)}, u32[]{:S(2)}, u32[]{:S(2)}) collective-permute-start(bf16[2,2,8,112,128]{4,3,2,1,0:T(8,128)(2,1)S(1)} %collective-permute-done.15.rest_5_), channel_id=1, source_target_pairs={{0,96},{1,25},{2,98},{3,27},{4,100},{5,29},{6,102},{7,31},{8,104},... | collective-permute-start | bytes 2752520 | tf_op jit(solution)/shard_map/ppermute | solution.py:202
  96.2 3.2 %collective-permute-start.19 = (bf16[4,2,6,112,128]{4,3,2,1,0:T(8,128)(2,1)}, bf16[4,2,6,112,128]{4,3,2,1,0:T(8,128)(2,1)S(1)}, u32[]{:S(2)}, u32[]{:S(2)}) collective-permute-start(bf16[4,2,6,112,128]{4,3,2,1,0:T(8,128)(2,1)} %get-tuple-element.168), channel_id=1, source_target_pairs={{0,96},{1,25},{2,98},{3,27},{4,100},{5,29},{6,102},{7,31},{8,104},... | collective-permute-start | bytes 4128776 | tf_op jit(solution)/shard_map/ppermute | solution.py:202
  99.4 8.3 %collective-permute-done.16.rest_6_ = bf16[2,2,8,112,128]{4,3,2,1,0:T(8,128)(2,1)S(1)} collective-permute-done((bf16[2,2,8,112,128]{4,3,2,1,0:T(8,128)(2,1)}, bf16[2,2,8,112,128]{4,3,2,1,0:T(8,128)(2,1)S(1)}, u32[]{:S(2)}, u32[]{:S(2)}) %collective-permute-start.16) | collective-permute-done | bytes 917536 | tf_op jit(solution)/shard_map/ppermute | solution.py:202
  109.6 17.3 %shard_map.104 = (bf16[8,2,256,896]{3,2,1,0:T(8,128)(2,1)}, bf16[4,2,4,112,128]{4,3,2,1,0:T(8,128)(2,1)}, bf16[2,2,4,112,128]{4,3,2,1,0:T(8,128)(2,1)}, bf16[2,2...) custom-call(s32[16]{0:T(128)} %mul.13.rows_tbl, ...), custom_call_target="tpu_custom_call" | custom-call | flops 5637144576 | bytes 22020096 | tf_op jit(solution)/shard_map/pallas_call | solution.py:144
  127.5 2.0 collective-permute-start.20
  129.5 1.3 collective-permute-start.21
  131.0 1.8 collective-permute-start.23
  132.8 17.3 %shard_map.105 = (bf16[8,2,256,896]{3,2,1,0:T(8,128)(2,1)}, bf16[4,2,4,112,128]{4,3,2,1,0:T(8,128)(2,1)}, bf16[2,2,4,112,128]{4,3,2,1,0:T(8,128)(2,1)}, bf16[2,2...) custom-call(s32[16]{0:T(128)} %mul.13.rows_tbl, ...), custom_call_target="tpu_custom_call" | custom-call | flops 5637144576 | bytes 22020096 | tf_op jit(solution)/shard_map/pallas_call | solution.py:144
  151.2 1.4 collective-permute-start.26
  152.6 1.9 collective-permute-start.27
  154.5 1.8 fusion.3
  158.0 1.4 collective-permute-start.25
  161.5 3.8 %collective-permute-done.30 = bf16[2,6,112,128]{3,2,1,0:T(8,128)(2,1)S(1)} collective-permute-done((bf16[2,6,112,128]{3,2,1,0:T(8,128)(2,1)S(1)}, bf16[2,6,112,128]{3,2,1,0:T(8,128)(2,1)S(1)}, u32[]{:S(2)}, u32[]{:S(2)}) %collective-permute-start.30) | collective-permute-done | bytes 344096 | tf_op jit(solution)/shard_map/ppermute | solution.py:202
  165.4 2.8 %collective-permute-start.24 = (bf16[2,2,4,112,128]{4,3,2,1,0:T(8,128)(2,1)S(1)}, bf16[2,2,4,112,128]{4,3,2,1,0:T(8,128)(2,1)S(1)}, u32[]{:S(2)}, u32[]{:S(2)}) collective-permute-start(bf16[2,2,4,112,128]{4,3,2,1,0:T(8,128)(2,1)S(1)} %add_convert_fusion.5), channel_id=1, source_target_pairs={{0,32},{1,9},{2,34},{3,11},{4,36},{5,13},{6,38},{7,15},{8,40},{9,1... | collective-permute-start | bytes 1376264 | tf_op jit(solution)/shard_map/ppermute | solution.py:202
  168.2 4.3 %collective-permute-done.29 = bf16[2,6,112,128]{3,2,1,0:T(8,128)(2,1)S(1)} collective-permute-done((bf16[2,6,112,128]{3,2,1,0:T(8,128)(2,1)S(1)}, bf16[2,6,112,128]{3,2,1,0:T(8,128)(2,1)S(1)}, u32[]{:S(2)}, u32[]{:S(2)}) %collective-permute-start.29) | collective-permute-done | bytes 344096 | tf_op jit(solution)/shard_map/ppermute | solution.py:202
  172.5 7.2 %collective-permute-done.28 = bf16[2,6,112,128]{3,2,1,0:T(8,128)(2,1)S(1)} collective-permute-done((bf16[2,6,112,128]{3,2,1,0:T(8,128)(2,1)S(1)}, bf16[2,6,112,128]{3,2,1,0:T(8,128)(2,1)S(1)}, u32[]{:S(2)}, u32[]{:S(2)}) %collective-permute-start.28) | collective-permute-done | bytes 344096 | tf_op jit(solution)/shard_map/ppermute | solution.py:202
  179.8 1.7 fusion.7
  182.3 1.4 collective-permute-start.34
  183.6 1.9 collective-permute-start.33
  185.7 2.0 collective-permute-start.32
  188.2 3.3 %collective-permute-done.35 = bf16[2,4,112,128]{3,2,1,0:T(8,128)(2,1)S(1)} collective-permute-done((bf16[2,4,112,128]{3,2,1,0:T(8,128)(2,1)S(1)}, bf16[2,4,112,128]{3,2,1,0:T(8,128)(2,1)S(1)}, u32[]{:S(2)}, u32[]{:S(2)}) %collective-permute-start.35) | collective-permute-done | bytes 229408 | tf_op jit(solution)/shard_map/ppermute | solution.py:202
  191.5 2.4 %collective-permute-done.34 = bf16[2,4,112,128]{3,2,1,0:T(8,128)(2,1)S(1)} collective-permute-done((bf16[2,4,112,128]{3,2,1,0:T(8,128)(2,1)S(1)}, bf16[2,4,112,128]{3,2,1,0:T(8,128)(2,1)S(1)}, u32[]{:S(2)}, u32[]{:S(2)}) %collective-permute-start.34) | collective-permute-done | bytes 229408 | tf_op jit(solution)/shard_map/ppermute | solution.py:202
  194.7 2.9 %collective-permute-done.31 = bf16[2,2,4,112,128]{4,3,2,1,0:T(8,128)(2,1)S(1)} collective-permute-done((bf16[2,2,4,112,128]{4,3,2,1,0:T(8,128)(2,1)S(1)}, bf16[2,2,4,112,128]{4,3,2,1,0:T(8,128)(2,1)S(1)}, u32[]{:S(2)}, u32[]{:S(2)}) %collective-permute-start.31) | collective-permute-done | bytes 458784 | tf_op jit(solution)/shard_map/ppermute | solution.py:202
  197.9 1.7 collective-permute-start.38
  199.6 3.2 %collective-permute-start.36 = (bf16[2,4,112,128]{3,2,1,0:T(8,128)(2,1)S(1)}, bf16[2,4,112,128]{3,2,1,0:T(8,128)(2,1)S(1)}, u32[]{:S(2)}, u32[]{:S(2)}) collective-permute-start(bf16[2,4,112,128]{3,2,1,0:T(8,128)(2,1)S(1)} %get-tuple-element.251), channel_id=1, source_target_pairs={{0,24},{1,97},{2,26},{3,99},{4,28},{5,101},{6,30},{7,103},{8,0},{9... | collective-permute-start | bytes 688136 | tf_op jit(solution)/shard_map/ppermute | solution.py:202
  203.0 2.2 slice_bitcast_fusion
  205.6 2.4 %collective-permute-done.37 = bf16[2,4,112,128]{3,2,1,0:T(8,128)(2,1)S(1)} collective-permute-done((bf16[2,4,112,128]{3,2,1,0:T(8,128)(2,1)S(1)}, bf16[2,4,112,128]{3,2,1,0:T(8,128)(2,1)S(1)}, u32[]{:S(2)}, u32[]{:S(2)}) %collective-permute-start.37) | collective-permute-done | bytes 229408 | tf_op jit(solution)/shard_map/ppermute | solution.py:202
  (125 shorter events, 16.3 us)
Async XLA Ops:
  7.2 57.2 %all-gather.3.cloned.1.call-start = ((), (), s32[]{:S(2)}) async-start(), calls=%async_computation.2 | async-start | bytes 8257536 | tf_op jit(solution)/shard_map/all_gather | solution.py:243
  9.7 193.4 %reduce-scatter.2.cloned.1.call-start = ((), (), s32[]{:S(2)}) async-start(), calls=%async_computation.1 | async-start | bytes 8257536 | tf_op jit(solution)/shard_map/reduce_scatter | solution.py:282
  9.8 8.5 %collective-permute-start = (bf16[2,6,112,128]{3,2,1,0:T(8,128)(2,1)S(1)}, bf16[2,6,112,128]{3,2,1,0:T(8,128)(2,1)S(1)}, u32[]{:S(2)}, u32[]{:S(2)}) collective-permute-start(bf16[2,6,112,128]{3,2,1,0:T(8,128)(2,1)S(1)} %get-tuple-element.259), channel_id=1, source_target_pairs={{0,8},{1,33},{2,10},{3,35},{4,12},{5,37},{6,14},{7,39},{8,16},{9,4... | collective-permute-start | bytes 1032200 | tf_op jit(solution)/shard_map/ppermute | solution.py:202
  11.5 11.9 %collective-permute-start.2 = (bf16[2,6,112,128]{3,2,1,0:T(8,128)(2,1)S(1)}, bf16[2,6,112,128]{3,2,1,0:T(8,128)(2,1)S(1)}, u32[]{:S(2)}, u32[]{:S(2)}) collective-permute-start(bf16[2,6,112,128]{3,2,1,0:T(8,128)(2,1)S(1)} %get-tuple-element.259), channel_id=1, source_target_pairs={{0,16},{1,65},{2,18},{3,67},{4,20},{5,69},{6,22},{7,71},{8,24},{9,... | collective-permute-start | bytes 1032200 | tf_op jit(solution)/shard_map/ppermute | solution.py:202
  14.2 11.3 %collective-permute-start.1 = (bf16[2,6,112,128]{3,2,1,0:T(8,128)(2,1)S(1)}, bf16[2,6,112,128]{3,2,1,0:T(8,128)(2,1)S(1)}, u32[]{:S(2)}, u32[]{:S(2)}) collective-permute-start(bf16[2,6,112,128]{3,2,1,0:T(8,128)(2,1)S(1)} %get-tuple-element.259), channel_id=1, source_target_pairs={{0,24},{1,97},{2,26},{3,99},{4,28},{5,101},{6,30},{7,103},{8,0},{9... | collective-permute-start | bytes 1032200 | tf_op jit(solution)/shard_map/ppermute | solution.py:202
  18.4 11.8 %collective-permute-start.5 = (bf16[2,2,6,112,128]{4,3,2,1,0:T(8,128)(2,1)S(1)}, bf16[2,2,6,112,128]{4,3,2,1,0:T(8,128)(2,1)S(1)}, u32[]{:S(2)}, u32[]{:S(2)}) collective-permute-start(bf16[2,2,6,112,128]{4,3,2,1,0:T(8,128)(2,1)S(1)} %pad_maximum_fusion.2.rest_0_), channel_id=1, source_target_pairs={{0,96},{1,25},{2,98},{3,27},{4,100},{5,29},{6,102},{7,31},{8,104},... | collective-permute-start | bytes 2064392 | tf_op jit(solution)/shard_map/ppermute | solution.py:202
  21.6 12.1 %collective-permute-start.3 = (bf16[2,2,6,112,128]{4,3,2,1,0:T(8,128)(2,1)S(1)}, bf16[2,2,6,112,128]{4,3,2,1,0:T(8,128)(2,1)S(1)}, u32[]{:S(2)}, u32[]{:S(2)}) collective-permute-start(bf16[2,2,6,112,128]{4,3,2,1,0:T(8,128)(2,1)S(1)} %pad_maximum_fusion.2.rest_0_), channel_id=1, source_target_pairs={{0,32},{1,9},{2,34},{3,11},{4,36},{5,13},{6,38},{7,15},{8,40},{9,1... | collective-permute-start | bytes 2064392 | tf_op jit(solution)/shard_map/ppermute | solution.py:202
  25.5 25.1 %copy-start.23 = (s32[4]{0:T(128)S(1)}, s32[4]{0:T(128)}, u32[]{:S(2)}) copy-start(s32[4]{0:T(128)} %constant.63.clone) | copy-start | bytes 52
  25.6 23.0 %copy-start.12 = (bf16[2,2,6,112,128]{4,3,2,1,0:T(8,128)(2,1)}, bf16[2,2,6,112,128]{4,3,2,1,0:T(8,128)(2,1)S(1)}, u32[]{:S(2)}) copy-start(bf16[2,2,6,112,128]{4,3,2,1,0:T(8,128)(2,1)S(1)} %pad_maximum_fusion.3.rest_1_) | copy-start | bytes 2064388
  25.6 13.0 %collective-permute-start.6 = (bf16[2,2,6,112,128]{4,3,2,1,0:T(8,128)(2,1)S(1)}, bf16[2,2,6,112,128]{4,3,2,1,0:T(8,128)(2,1)}, u32[]{:S(2)}, u32[]{:S(2)}) collective-permute-start(bf16[2,2,6,112,128]{4,3,2,1,0:T(8,128)(2,1)S(1)} %pad_maximum_fusion.3.rest_1_), channel_id=1, source_target_pairs={{0,96},{1,25},{2,98},{3,27},{4,100},{5,29},{6,102},{7,31},{8,104},... | collective-permute-start | bytes 2064392 | tf_op jit(solution)/shard_map/ppermute | solution.py:202
  30.1 12.1 %collective-permute-start.4 = (bf16[2,2,6,112,128]{4,3,2,1,0:T(8,128)(2,1)S(1)}, bf16[2,2,6,112,128]{4,3,2,1,0:T(8,128)(2,1)S(1)}, u32[]{:S(2)}, u32[]{:S(2)}) collective-permute-start(bf16[2,2,6,112,128]{4,3,2,1,0:T(8,128)(2,1)S(1)} %pad_maximum_fusion.3.rest_1_), channel_id=1, source_target_pairs={{0,32},{1,9},{2,34},{3,11},{4,36},{5,13},{6,38},{7,15},{8,40},{9,1... | collective-permute-start | bytes 2064392 | tf_op jit(solution)/shard_map/ppermute | solution.py:202
  33.7 30.6 %copy-start.26 = (bf16[2,2,6,112,128]{4,3,2,1,0:T(8,128)(2,1)}, bf16[2,2,6,112,128]{4,3,2,1,0:T(8,128)(2,1)S(1)}, u32[]{:S(2)}) copy-start(bf16[2,2,6,112,128]{4,3,2,1,0:T(8,128)(2,1)S(1)} %collective-permute-done.3.rest_2_) | copy-start | bytes 2064388
  42.3 22.1 %collective-permute-start.7 = (bf16[2,2,6,112,128]{4,3,2,1,0:T(8,128)(2,1)S(1)}, bf16[2,2,6,112,128]{4,3,2,1,0:T(8,128)(2,1)}, u32[]{:S(2)}, u32[]{:S(2)}) collective-permute-start(bf16[2,2,6,112,128]{4,3,2,1,0:T(8,128)(2,1)S(1)} %collective-permute-done.3.rest_2_), channel_id=1, source_target_pairs={{0,32},{1,9},{2,34},{3,11},{4,36},{5,13},{6,38},{7,15},{8,40},{9,1... | collective-permute-start | bytes 2064392 | tf_op jit(solution)/shard_map/ppermute | solution.py:202
  42.3 22.1 %collective-permute-start.8 = (bf16[2,2,6,112,128]{4,3,2,1,0:T(8,128)(2,1)}, bf16[2,2,6,112,128]{4,3,2,1,0:T(8,128)(2,1)}, u32[]{:S(2)}, u32[]{:S(2)}) collective-permute-start(bf16[2,2,6,112,128]{4,3,2,1,0:T(8,128)(2,1)} %collective-permute-done.6.rest_5_), channel_id=1, source_target_pairs={{0,96},{1,25},{2,98},{3,27},{4,100},{5,29},{6,102},{7,31},{8,104},... | collective-permute-start | bytes 2064392 | tf_op jit(solution)/shard_map/ppermute | solution.py:202
  45.5 10.1 %collective-permute-start.11 = (bf16[2,8,112,128]{3,2,1,0:T(8,128)(2,1)S(1)}, bf16[2,8,112,128]{3,2,1,0:T(8,128)(2,1)S(1)}, u32[]{:S(2)}, u32[]{:S(2)}) collective-permute-start(bf16[2,8,112,128]{3,2,1,0:T(8,128)(2,1)S(1)} %pad_maximum_fusion.4), channel_id=1, source_target_pairs={{0,16},{1,65},{2,18},{3,67},{4,20},{5,69},{6,22},{7,71},{8,24},{9,... | collective-permute-start | bytes 1376264 | tf_op jit(solution)/shard_map/ppermute | solution.py:202
  48.6 11.1 %collective-permute-start.10 = (bf16[2,8,112,128]{3,2,1,0:T(8,128)(2,1)S(1)}, bf16[2,8,112,128]{3,2,1,0:T(8,128)(2,1)S(1)}, u32[]{:S(2)}, u32[]{:S(2)}) collective-permute-start(bf16[2,8,112,128]{3,2,1,0:T(8,128)(2,1)S(1)} %pad_maximum_fusion.4), channel_id=1, source_target_pairs={{0,24},{1,97},{2,26},{3,99},{4,28},{5,101},{6,30},{7,103},{8,0},{9... | collective-permute-start | bytes 1376264 | tf_op jit(solution)/shard_map/ppermute | solution.py:202
  49.4 11.0 %collective-permute-start.9 = (bf16[2,8,112,128]{3,2,1,0:T(8,128)(2,1)S(1)}, bf16[2,8,112,128]{3,2,1,0:T(8,128)(2,1)S(1)}, u32[]{:S(2)}, u32[]{:S(2)}) collective-permute-start(bf16[2,8,112,128]{3,2,1,0:T(8,128)(2,1)S(1)} %pad_maximum_fusion.4), channel_id=1, source_target_pairs={{0,8},{1,33},{2,10},{3,35},{4,12},{5,37},{6,14},{7,39},{8,16},{9,4... | collective-permute-start | bytes 1376264 | tf_op jit(solution)/shard_map/ppermute | solution.py:202
  64.4 28.3 %copy-start = (bf16[2,2,8,112,128]{4,3,2,1,0:T(8,128)(2,1)}, bf16[2,2,8,112,128]{4,3,2,1,0:T(8,128)(2,1)S(1)}, u32[]{:S(2)}) copy-start(bf16[2,2,8,112,128]{4,3,2,1,0:T(8,128)(2,1)S(1)} %pad_maximum_fusion.1.rest_1_) | copy-start | bytes 2752516
  64.5 28.3 %collective-permute-start.15 = (bf16[2,2,8,112,128]{4,3,2,1,0:T(8,128)(2,1)S(1)}, bf16[2,2,8,112,128]{4,3,2,1,0:T(8,128)(2,1)S(1)}, u32[]{:S(2)}, u32[]{:S(2)}) collective-permute-start(bf16[2,2,8,112,128]{4,3,2,1,0:T(8,128)(2,1)S(1)} %pad_maximum_fusion.1.rest_1_), channel_id=1, source_target_pairs={{0,96},{1,25},{2,98},{3,27},{4,100},{5,29},{6,102},{7,31},{8,104},... | collective-permute-start | bytes 2752520 | tf_op jit(solution)/shard_map/ppermute | solution.py:202
  66.7 26.1 %collective-permute-start.13 = (bf16[2,2,8,112,128]{4,3,2,1,0:T(8,128)(2,1)S(1)}, bf16[2,2,8,112,128]{4,3,2,1,0:T(8,128)(2,1)}, u32[]{:S(2)}, u32[]{:S(2)}) collective-permute-start(bf16[2,2,8,112,128]{4,3,2,1,0:T(8,128)(2,1)S(1)} %pad_maximum_fusion.1.rest_1_), channel_id=1, source_target_pairs={{0,32},{1,9},{2,34},{3,11},{4,36},{5,13},{6,38},{7,15},{8,40},{9,1... | collective-permute-start | bytes 2752520 | tf_op jit(solution)/shard_map/ppermute | solution.py:202
  67.8 25.0 %copy-start.1 = (bf16[2,2,8,112,128]{4,3,2,1,0:T(8,128)(2,1)}, bf16[2,2,8,112,128]{4,3,2,1,0:T(8,128)(2,1)S(1)}, u32[]{:S(2)}) copy-start(bf16[2,2,8,112,128]{4,3,2,1,0:T(8,128)(2,1)S(1)} %pad_maximum_fusion.rest_0_) | copy-start | bytes 2752516
  67.8 25.0 %collective-permute-start.14 = (bf16[2,2,8,112,128]{4,3,2,1,0:T(8,128)(2,1)S(1)}, bf16[2,2,8,112,128]{4,3,2,1,0:T(8,128)(2,1)}, u32[]{:S(2)}, u32[]{:S(2)}) collective-permute-start(bf16[2,2,8,112,128]{4,3,2,1,0:T(8,128)(2,1)S(1)} %pad_maximum_fusion.rest_0_), channel_id=1, source_target_pairs={{0,96},{1,25},{2,98},{3,27},{4,100},{5,29},{6,102},{7,31},{8,104},... | collective-permute-start | bytes 2752520 | tf_op jit(solution)/shard_map/ppermute | solution.py:202
  71.1 21.7 %collective-permute-start.12 = (bf16[2,2,8,112,128]{4,3,2,1,0:T(8,128)(2,1)S(1)}, bf16[2,2,8,112,128]{4,3,2,1,0:T(8,128)(2,1)}, u32[]{:S(2)}, u32[]{:S(2)}) collective-permute-start(bf16[2,2,8,112,128]{4,3,2,1,0:T(8,128)(2,1)S(1)} %pad_maximum_fusion.rest_0_), channel_id=1, source_target_pairs={{0,32},{1,9},{2,34},{3,11},{4,36},{5,13},{6,38},{7,15},{8,40},{9,1... | collective-permute-start | bytes 2752520 | tf_op jit(solution)/shard_map/ppermute | solution.py:202
  92.8 34.2 %copy-start.14 = (bf16[2,2,6,112,128]{4,3,2,1,0:T(8,128)(2,1)S(1)}, bf16[2,2,6,112,128]{4,3,2,1,0:T(8,128)(2,1)}, u32[]{:S(2)}) copy-start(bf16[2,2,6,112,128]{4,3,2,1,0:T(8,128)(2,1)} %get-tuple-element.187) | copy-start | bytes 2064388
  92.8 14.9 %collective-permute-start.16 = (bf16[2,2,8,112,128]{4,3,2,1,0:T(8,128)(2,1)}, bf16[2,2,8,112,128]{4,3,2,1,0:T(8,128)(2,1)S(1)}, u32[]{:S(2)}, u32[]{:S(2)}) collective-permute-start(bf16[2,2,8,112,128]{4,3,2,1,0:T(8,128)(2,1)} %collective-permute-done.12.rest_2_), channel_id=1, source_target_pairs={{0,32},{1,9},{2,34},{3,11},{4,36},{5,13},{6,38},{7,15},{8,40},{9,1... | collective-permute-start | bytes 2752520 | tf_op jit(solution)/shard_map/ppermute | solution.py:202
  92.9 14.8 %collective-permute-start.17 = (bf16[2,2,8,112,128]{4,3,2,1,0:T(8,128)(2,1)S(1)}, bf16[2,2,8,112,128]{4,3,2,1,0:T(8,128)(2,1)S(1)}, u32[]{:S(2)}, u32[]{:S(2)}) collective-permute-start(bf16[2,2,8,112,128]{4,3,2,1,0:T(8,128)(2,1)S(1)} %collective-permute-done.15.rest_5_), channel_id=1, source_target_pairs={{0,96},{1,25},{2,98},{3,27},{4,100},{5,29},{6,102},{7,31},{8,104},... | collective-permute-start | bytes 2752520 | tf_op jit(solution)/shard_map/ppermute | solution.py:202
  96.2 30.7 %collective-permute-start.18 = (bf16[4,2,6,112,128]{4,3,2,1,0:T(8,128)(2,1)}, bf16[4,2,6,112,128]{4,3,2,1,0:T(8,128)(2,1)S(1)}, u32[]{:S(2)}, u32[]{:S(2)}) collective-permute-start(bf16[4,2,6,112,128]{4,3,2,1,0:T(8,128)(2,1)} %get-tuple-element.167), channel_id=1, source_target_pairs={{0,32},{1,9},{2,34},{3,11},{4,36},{5,13},{6,38},{7,15},{8,40},{9,1... | collective-permute-start | bytes 4128776 | tf_op jit(solution)/shard_map/ppermute | solution.py:202
  96.2 30.7 %collective-permute-start.19 = (bf16[4,2,6,112,128]{4,3,2,1,0:T(8,128)(2,1)}, bf16[4,2,6,112,128]{4,3,2,1,0:T(8,128)(2,1)S(1)}, u32[]{:S(2)}, u32[]{:S(2)}) collective-permute-start(bf16[4,2,6,112,128]{4,3,2,1,0:T(8,128)(2,1)} %get-tuple-element.168), channel_id=1, source_target_pairs={{0,96},{1,25},{2,98},{3,27},{4,100},{5,29},{6,102},{7,31},{8,104},... | collective-permute-start | bytes 4128776 | tf_op jit(solution)/shard_map/ppermute | solution.py:202
  127.2 22.9 %collective-permute-start.22 = (bf16[2,2,6,112,128]{4,3,2,1,0:T(8,128)(2,1)S(1)}, bf16[2,2,6,112,128]{4,3,2,1,0:T(8,128)(2,1)S(1)}, u32[]{:S(2)}, u32[]{:S(2)}) collective-permute-start(bf16[2,2,6,112,128]{4,3,2,1,0:T(8,128)(2,1)S(1)} %add_convert_fusion.1), channel_id=1, source_target_pairs={{0,32},{1,9},{2,34},{3,11},{4,36},{5,13},{6,38},{7,15},{8,40},{9,1... | collective-permute-start | bytes 2064392 | tf_op jit(solution)/shard_map/ppermute | solution.py:202
  127.5 23.7 %collective-permute-start.20 = (bf16[4,2,4,112,128]{4,3,2,1,0:T(8,128)(2,1)}, bf16[4,2,4,112,128]{4,3,2,1,0:T(8,128)(2,1)}, u32[]{:S(2)}, u32[]{:S(2)}) collective-permute-start(bf16[4,2,4,112,128]{4,3,2,1,0:T(8,128)(2,1)} %get-tuple-element.191), channel_id=1, source_target_pairs={{0,32},{1,9},{2,34},{3,11},{4,36},{5,13},{6,38},{7,15},{8,40},{9,1... | collective-permute-start | bytes 2752520 | tf_op jit(solution)/shard_map/ppermute | solution.py:202
  129.5 21.7 %collective-permute-start.21 = (bf16[4,2,4,112,128]{4,3,2,1,0:T(8,128)(2,1)S(1)}, bf16[4,2,4,112,128]{4,3,2,1,0:T(8,128)(2,1)}, u32[]{:S(2)}, u32[]{:S(2)}) collective-permute-start(bf16[4,2,4,112,128]{4,3,2,1,0:T(8,128)(2,1)S(1)} %copy-done.24), channel_id=1, source_target_pairs={{0,96},{1,25},{2,98},{3,27},{4,100},{5,29},{6,102},{7,31},{8,104},... | collective-permute-start | bytes 2752520 | tf_op jit(solution)/shard_map/ppermute | solution.py:202
  131.0 19.3 %collective-permute-start.23 = (bf16[2,2,6,112,128]{4,3,2,1,0:T(8,128)(2,1)S(1)}, bf16[2,2,6,112,128]{4,3,2,1,0:T(8,128)(2,1)S(1)}, u32[]{:S(2)}, u32[]{:S(2)}) collective-permute-start(bf16[2,2,6,112,128]{4,3,2,1,0:T(8,128)(2,1)S(1)} %add_convert_fusion), channel_id=1, source_target_pairs={{0,96},{1,25},{2,98},{3,27},{4,100},{5,29},{6,102},{7,31},{8,104},... | collective-permute-start | bytes 2064392 | tf_op jit(solution)/shard_map/ppermute | solution.py:202
  151.2 28.5 %collective-permute-start.26 = (bf16[4,2,4,112,128]{4,3,2,1,0:T(8,128)(2,1)}, bf16[4,2,4,112,128]{4,3,2,1,0:T(8,128)(2,1)S(1)}, u32[]{:S(2)}, u32[]{:S(2)}) collective-permute-start(bf16[4,2,4,112,128]{4,3,2,1,0:T(8,128)(2,1)} %get-tuple-element.207), channel_id=1, source_target_pairs={{0,32},{1,9},{2,34},{3,11},{4,36},{5,13},{6,38},{7,15},{8,40},{9,1... | collective-permute-start | bytes 2752520 | tf_op jit(solution)/shard_map/ppermute | solution.py:202
  152.6 27.2 %collective-permute-start.27 = (bf16[4,2,4,112,128]{4,3,2,1,0:T(8,128)(2,1)}, bf16[4,2,4,112,128]{4,3,2,1,0:T(8,128)(2,1)S(1)}, u32[]{:S(2)}, u32[]{:S(2)}) collective-permute-start(bf16[4,2,4,112,128]{4,3,2,1,0:T(8,128)(2,1)} %get-tuple-element.208), channel_id=1, source_target_pairs={{0,96},{1,25},{2,98},{3,27},{4,100},{5,29},{6,102},{7,31},{8,104},... | collective-permute-start | bytes 2752520 | tf_op jit(solution)/shard_map/ppermute | solution.py:202
  156.3 23.4 %copy-start.10 = (bf16[4,2,4,112,128]{4,3,2,1,0:T(8,128)(2,1)S(1)}, bf16[4,2,4,112,128]{4,3,2,1,0:T(8,128)(2,1)}, u32[]{:S(2)}) copy-start(bf16[4,2,4,112,128]{4,3,2,1,0:T(8,128)(2,1)} %get-tuple-element.217) | copy-start | bytes 2752516
  156.4 9.0 %collective-permute-start.30 = (bf16[2,6,112,128]{3,2,1,0:T(8,128)(2,1)S(1)}, bf16[2,6,112,128]{3,2,1,0:T(8,128)(2,1)S(1)}, u32[]{:S(2)}, u32[]{:S(2)}) collective-permute-start(bf16[2,6,112,128]{3,2,1,0:T(8,128)(2,1)S(1)} %get-tuple-element.236), channel_id=1, source_target_pairs={{0,16},{1,65},{2,18},{3,67},{4,20},{5,69},{6,22},{7,71},{8,24},{9,... | collective-permute-start | bytes 1032200 | tf_op jit(solution)/shard_map/ppermute | solution.py:202
  158.0 21.7 %collective-permute-start.25 = (bf16[2,2,4,112,128]{4,3,2,1,0:T(8,128)(2,1)S(1)}, bf16[2,2,4,112,128]{4,3,2,1,0:T(8,128)(2,1)S(1)}, u32[]{:S(2)}, u32[]{:S(2)}) collective-permute-start(bf16[2,2,4,112,128]{4,3,2,1,0:T(8,128)(2,1)S(1)} %add_convert_fusion.4), channel_id=1, source_target_pairs={{0,96},{1,25},{2,98},{3,27},{4,100},{5,29},{6,102},{7,31},{8,104},... | collective-permute-start | bytes 1376264 | tf_op jit(solution)/shard_map/ppermute | solution.py:202
  159.4 13.1 %collective-permute-start.29 = (bf16[2,6,112,128]{3,2,1,0:T(8,128)(2,1)S(1)}, bf16[2,6,112,128]{3,2,1,0:T(8,128)(2,1)S(1)}, u32[]{:S(2)}, u32[]{:S(2)}) collective-permute-start(bf16[2,6,112,128]{3,2,1,0:T(8,128)(2,1)S(1)} %get-tuple-element.237), channel_id=1, source_target_pairs={{0,8},{1,33},{2,10},{3,35},{4,12},{5,37},{6,14},{7,39},{8,16},{9,4... | collective-permute-start | bytes 1032200 | tf_op jit(solution)/shard_map/ppermute | solution.py:202
  165.4 14.4 %collective-permute-start.24 = (bf16[2,2,4,112,128]{4,3,2,1,0:T(8,128)(2,1)S(1)}, bf16[2,2,4,112,128]{4,3,2,1,0:T(8,128)(2,1)S(1)}, u32[]{:S(2)}, u32[]{:S(2)}) collective-permute-start(bf16[2,2,4,112,128]{4,3,2,1,0:T(8,128)(2,1)S(1)} %add_convert_fusion.5), channel_id=1, source_target_pairs={{0,32},{1,9},{2,34},{3,11},{4,36},{5,13},{6,38},{7,15},{8,40},{9,1... | collective-permute-start | bytes 1376264 | tf_op jit(solution)/shard_map/ppermute | solution.py:202
  172.5 7.2 %collective-permute-start.28 = (bf16[2,6,112,128]{3,2,1,0:T(8,128)(2,1)S(1)}, bf16[2,6,112,128]{3,2,1,0:T(8,128)(2,1)S(1)}, u32[]{:S(2)}, u32[]{:S(2)}) collective-permute-start(bf16[2,6,112,128]{3,2,1,0:T(8,128)(2,1)S(1)} %get-tuple-element.249), channel_id=1, source_target_pairs={{0,24},{1,97},{2,26},{3,99},{4,28},{5,101},{6,30},{7,103},{8,0},{9... | collective-permute-start | bytes 1032200 | tf_op jit(solution)/shard_map/ppermute | solution.py:202
  181.5 10.1 %collective-permute-start.35 = (bf16[2,4,112,128]{3,2,1,0:T(8,128)(2,1)S(1)}, bf16[2,4,112,128]{3,2,1,0:T(8,128)(2,1)S(1)}, u32[]{:S(2)}, u32[]{:S(2)}) collective-permute-start(bf16[2,4,112,128]{3,2,1,0:T(8,128)(2,1)S(1)} %get-tuple-element.244), channel_id=1, source_target_pairs={{0,16},{1,65},{2,18},{3,67},{4,20},{5,69},{6,22},{7,71},{8,24},{9,... | collective-permute-start | bytes 688136 | tf_op jit(solution)/shard_map/ppermute | solution.py:202
  182.3 11.6 %collective-permute-start.34 = (bf16[2,4,112,128]{3,2,1,0:T(8,128)(2,1)S(1)}, bf16[2,4,112,128]{3,2,1,0:T(8,128)(2,1)S(1)}, u32[]{:S(2)}, u32[]{:S(2)}) collective-permute-start(bf16[2,4,112,128]{3,2,1,0:T(8,128)(2,1)S(1)} %get-tuple-element.245), channel_id=1, source_target_pairs={{0,8},{1,33},{2,10},{3,35},{4,12},{5,37},{6,14},{7,39},{8,16},{9,4... | collective-permute-start | bytes 688136 | tf_op jit(solution)/shard_map/ppermute | solution.py:202
  183.6 11.0 %collective-permute-start.33 = (bf16[2,4,112,128]{3,2,1,0:T(8,128)(2,1)S(1)}, bf16[2,4,112,128]{3,2,1,0:T(8,128)(2,1)S(1)}, u32[]{:S(2)}, u32[]{:S(2)}) collective-permute-start(bf16[2,4,112,128]{3,2,1,0:T(8,128)(2,1)S(1)} %get-tuple-element.253), channel_id=1, source_target_pairs={{0,24},{1,97},{2,26},{3,99},{4,28},{5,101},{6,30},{7,103},{8,0},{9... | collective-permute-start | bytes 688136 | tf_op jit(solution)/shard_map/ppermute | solution.py:202
  185.7 9.0 %collective-permute-start.32 = (bf16[2,2,4,112,128]{4,3,2,1,0:T(8,128)(2,1)S(1)}, bf16[2,2,4,112,128]{4,3,2,1,0:T(8,128)(2,1)S(1)}, u32[]{:S(2)}, u32[]{:S(2)}) collective-permute-start(bf16[2,2,4,112,128]{4,3,2,1,0:T(8,128)(2,1)S(1)} %add_convert_fusion.2), channel_id=1, source_target_pairs={{0,96},{1,25},{2,98},{3,27},{4,100},{5,29},{6,102},{7,31},{8,104},... | collective-permute-start | bytes 1376264 | tf_op jit(solution)/shard_map/ppermute | solution.py:202
  187.8 9.8 %collective-permute-start.31 = (bf16[2,2,4,112,128]{4,3,2,1,0:T(8,128)(2,1)S(1)}, bf16[2,2,4,112,128]{4,3,2,1,0:T(8,128)(2,1)S(1)}, u32[]{:S(2)}, u32[]{:S(2)}) collective-permute-start(bf16[2,2,4,112,128]{4,3,2,1,0:T(8,128)(2,1)S(1)} %add_convert_fusion.3), channel_id=1, source_target_pairs={{0,32},{1,9},{2,34},{3,11},{4,36},{5,13},{6,38},{7,15},{8,40},{9,1... | collective-permute-start | bytes 1376264 | tf_op jit(solution)/shard_map/ppermute | solution.py:202
  197.9 7.7 %collective-permute-start.38 = (bf16[2,4,112,128]{3,2,1,0:T(8,128)(2,1)S(1)}, bf16[2,4,112,128]{3,2,1,0:T(8,128)(2,1)S(1)}, u32[]{:S(2)}, u32[]{:S(2)}) collective-permute-start(bf16[2,4,112,128]{3,2,1,0:T(8,128)(2,1)S(1)} %get-tuple-element.240), channel_id=1, source_target_pairs={{0,16},{1,65},{2,18},{3,67},{4,20},{5,69},{6,22},{7,71},{8,24},{9,... | collective-permute-start | bytes 688136 | tf_op jit(solution)/shard_map/ppermute | solution.py:202
  199.6 8.4 %collective-permute-start.37 = (bf16[2,4,112,128]{3,2,1,0:T(8,128)(2,1)S(1)}, bf16[2,4,112,128]{3,2,1,0:T(8,128)(2,1)S(1)}, u32[]{:S(2)}, u32[]{:S(2)}) collective-permute-start(bf16[2,4,112,128]{3,2,1,0:T(8,128)(2,1)S(1)} %get-tuple-element.241), channel_id=1, source_target_pairs={{0,8},{1,33},{2,10},{3,35},{4,12},{5,37},{6,14},{7,39},{8,16},{9,4... | collective-permute-start | bytes 688136 | tf_op jit(solution)/shard_map/ppermute | solution.py:202
  199.6 8.4 %collective-permute-start.36 = (bf16[2,4,112,128]{3,2,1,0:T(8,128)(2,1)S(1)}, bf16[2,4,112,128]{3,2,1,0:T(8,128)(2,1)S(1)}, u32[]{:S(2)}, u32[]{:S(2)}) collective-permute-start(bf16[2,4,112,128]{3,2,1,0:T(8,128)(2,1)S(1)} %get-tuple-element.251), channel_id=1, source_target_pairs={{0,24},{1,97},{2,26},{3,99},{4,28},{5,101},{6,30},{7,103},{8,0},{9... | collective-permute-start | bytes 688136 | tf_op jit(solution)/shard_map/ppermute | solution.py:202
  (21 other events, 112.7 us)
Sparse Core Ops, SparseCore 0:
  9.8 47.9 all-gather.2
  151.3 46.8 reduce-scatter.1
